TPU v7x, 32 devices: a whole 2x2x4 slice. The times are simulated.
32 devices in a mesh: ty: 4 (over x, core), tx: 8 (over z, y).
Axes of the slice: x: 2, y: 2, z: 4, core: 2. Of those that a mesh axis runs over, the one named last changes fastest.
Arguments:
- roi_feat: bfloat16 [384, 14, 14, 256], P(('ty', 'tx')), may hold values from -6 to 6
- pre_one: bfloat16 [384, 14, 14, 256], P(('ty', 'tx')), may hold values from -6 to 6
- grad_two: bfloat16 [384, 14, 14, 256], P(('ty', 'tx')), may hold values from -6 to 6
- w_one: bfloat16 [3, 3, 256, 256], replicated, may hold values from -0.125 to 0.125
- w_two: bfloat16 [3, 3, 256, 256], replicated, may hold values from -0.125 to 0.125
- roi_rows: bfloat16 [384, 16, 14], P(('ty', 'tx')), may hold values from -1.5 to 1.5
- roi_cols: bfloat16 [384, 16, 14], P(('ty', 'tx')), may hold values from -1.5 to 1.5
- target_col: int32 [384, 1], P(('ty', 'tx')), may hold values from 0 to 7; in each aligned block of 12 rows (0 to 11, 12 to 23, ...) at most 3 rows name the same one
- off_row: int32 [384], P(('ty', 'tx')), may hold values from 0 to 15
- off_col: int32 [384], P(('ty', 'tx')), may hold values from 0 to 63
- fpn_input: bfloat16 [64, 512, 256], P('ty', 'tx'), may hold values from -6 to 6
- fpn_grad: bfloat16 [64, 512, 256], P('ty', 'tx'), may hold values from -6 to 6
- w_fpn: bfloat16 [3, 3, 256, 256], replicated, may hold values from -0.125 to 0.125
Outputs:
- grad_fpn_input: bfloat16 [64, 512, 256], P('ty', 'tx')
- grad_w_one: float32 [589824], P(('ty', 'tx'))
- grad_w_two: float32 [589824], P(('ty', 'tx'))
- grad_w_fpn: float32 [589824], P(('ty', 'tx'))
Inputs may be any that keep to these rules, and one draw needn't show every extreme that they name: `target_col`: at most 3 regions of one device name the same column, and in every draw some device names some column exactly 3 times.
All inputs are finite; a program needn't handle non-finite values.
Results may differ from a plain program's by a relative error of at most 0.0075.
Values may be sent and summed in bfloat16 or wider, within the bound.
No kernel may reach another device: no remote copies, remote signals or barrier semaphores. Data moves between devices by JAX's collectives and lax.ppermute only.
A program may use at most 128 MiB of HBM per device.

v0:
```python
import jax
import jax.numpy as jnp
from jax import lax
from jax.sharding import PartitionSpec as P


def shifted(shard, axis, by):
    devices = lax.axis_size(axis)
    pairs = [(i, i + by) for i in range(devices) if 0 <= i + by < devices]
    return lax.ppermute(shard, axis, pairs)


def extended(block, sides, width):
    for axis, dim in sides:
        count = lax.axis_size(axis)
        forward = [(i, i + 1) for i in range(count - 1)]
        backward = [(target, source) for source, target in forward]
        low = lax.ppermute(
            lax.slice_in_dim(block, block.shape[dim] - width, None, axis=dim), axis, forward
        )
        high = lax.ppermute(lax.slice_in_dim(block, 0, width, axis=dim), axis, backward)
        block = jnp.concatenate([low, block, high], axis=dim)
    return block


def window_patches(padded, row_count, col_count, flipped):
    pieces = []
    for row_step in range(3):
        for col_step in range(3):
            row_start = 2 - row_step if flipped else row_step
            col_start = 2 - col_step if flipped else col_step
            pieces.append(
                padded[..., row_start : row_start + row_count, col_start : col_start + col_count, :]
            )
    return jnp.concatenate(pieces, axis=-1)


def flipped_weight(weight):
    channels = weight.shape[2]
    return jnp.transpose(weight, (0, 1, 3, 2)).reshape(9 * channels, channels)


def weight_term(gradient, inputs_patch):
    return lax.dot_general(
        gradient, inputs_patch, (((0,), (0,)), ((), ())), preferred_element_type=jnp.float32
    )


def region_windows(region_grad, row_weights, col_weights):
    highest = lax.Precision.HIGHEST
    partial_sum = jnp.einsum(
        "nxj,nijc->nixc",
        col_weights.astype(jnp.float32),
        region_grad.astype(jnp.float32),
        precision=highest,
    )
    return jnp.einsum(
        "nyi,nixc->nyxc", row_weights.astype(jnp.float32), partial_sum, precision=highest
    ).astype(jnp.bfloat16)


def place_windows(windows, offsets, row_count, col_count):
    extent = windows.shape[1]
    inside = jnp.arange(extent, dtype=jnp.int32)[None, None, :]
    row_hit = (
        jnp.arange(row_count + extent, dtype=jnp.int32)[None, :, None]
        == offsets[:, 0][:, None, None] + inside
    ).astype(jnp.bfloat16)
    col_hit = (
        jnp.arange(col_count + extent, dtype=jnp.int32)[None, :, None]
        == offsets[:, 1][:, None, None] + inside
    ).astype(jnp.bfloat16)
    spread = jnp.einsum(
        "sXx,syxc->syXc", col_hit, windows, preferred_element_type=jnp.float32
    ).astype(jnp.bfloat16)
    return jnp.einsum("sYy,syXc->YXc", row_hit, spread, preferred_element_type=jnp.float32)


def local(
    roi_feat,
    pre_one,
    grad_two,
    w_one,
    w_two,
    roi_rows,
    roi_cols,
    target_col,
    off_row,
    off_col,
    fpn_input,
    fpn_grad,
    w_fpn,
):
    region_count, pool_size, channels = (roi_feat.shape[0], roi_feat.shape[1], roi_feat.shape[3])
    tile_rows, tile_cols = (fpn_input.shape[0], fpn_input.shape[1])
    extent = roi_rows.shape[1]
    columns = lax.axis_size("tx")
    capacity = max(2, (2 * region_count + columns - 1) // columns)
    positions = region_count * pool_size * pool_size
    region_pad = ((0, 0), (1, 1), (1, 1), (0, 0))
    active = jnp.maximum(pre_one, 0)
    back_two = jnp.dot(
        window_patches(jnp.pad(grad_two, region_pad), pool_size, pool_size, True).reshape(
            positions, 9 * channels
        ),
        flipped_weight(w_two),
        preferred_element_type=jnp.float32,
    )
    grad_one = jnp.where(pre_one.reshape(positions, channels) > 0, back_two, 0.0).astype(
        jnp.bfloat16
    )
    term_two = weight_term(
        grad_two.reshape(positions, channels),
        window_patches(jnp.pad(active, region_pad), pool_size, pool_size, False).reshape(
            positions, 9 * channels
        ),
    )
    term_one = weight_term(
        grad_one,
        window_patches(jnp.pad(roi_feat, region_pad), pool_size, pool_size, False).reshape(
            positions, 9 * channels
        ),
    )
    region_grad = (
        jnp.dot(
            window_patches(
                jnp.pad(grad_one.reshape(region_count, pool_size, pool_size, channels), region_pad),
                pool_size,
                pool_size,
                True,
            ).reshape(positions, 9 * channels),
            flipped_weight(w_one),
            preferred_element_type=jnp.float32,
        )
        .astype(jnp.bfloat16)
        .reshape(region_count, pool_size, pool_size, channels)
    )
    targets = target_col[:, 0]
    order_ids = jnp.arange(region_count, dtype=jnp.int32)
    earlier = order_ids[None, :] < order_ids[:, None]
    slot_rank = jnp.sum(
        ((targets[None, :] == targets[:, None]) & earlier).astype(jnp.int32), axis=1
    )
    slot_index = targets * capacity + slot_rank
    selector = (
        jnp.arange(columns * capacity, dtype=jnp.int32)[:, None] == slot_index[None, :]
    ).astype(jnp.bfloat16)
    offsets = jnp.stack([off_row, off_col], axis=1).astype(jnp.bfloat16)

    def pack_slots(values):
        flattened = values.reshape(region_count, -1)
        packed = jnp.dot(selector, flattened, preferred_element_type=jnp.float32).astype(
            jnp.bfloat16
        )
        return packed.reshape((columns, capacity) + values.shape[1:])

    windows = region_windows(region_grad, roi_rows, roi_cols)
    received, got_offsets = (
        lax.all_to_all(pack_slots(windows), "tx", split_axis=0, concat_axis=0, tiled=True),
        lax.all_to_all(pack_slots(offsets), "tx", split_axis=0, concat_axis=0, tiled=True),
    )
    slot_total = columns * capacity
    windows_in = received.reshape((slot_total,) + received.shape[2:])
    place_at = got_offsets.reshape(slot_total, 2).astype(jnp.int32)
    canvas = place_windows(windows_in, place_at, tile_rows, tile_cols)
    spill_right = shifted(canvas[:, tile_cols:, :].astype(jnp.bfloat16), "tx", 1).astype(
        jnp.float32
    )
    canvas = canvas[:, :tile_cols, :].at[:, :extent, :].add(spill_right)
    spill_low = shifted(canvas[tile_rows:, :, :].astype(jnp.bfloat16), "ty", 1).astype(jnp.float32)
    canvas = canvas[:tile_rows].at[:extent].add(spill_low)
    feature_grad = (fpn_grad.astype(jnp.float32) + canvas).astype(jnp.bfloat16)
    grad_padded, input_padded = (
        extended(feature_grad, (("ty", 0), ("tx", 1)), 1),
        extended(fpn_input, (("ty", 0), ("tx", 1)), 1),
    )
    tile_positions = tile_rows * tile_cols
    input_grad = (
        jnp.dot(
            window_patches(grad_padded, tile_rows, tile_cols, True).reshape(
                tile_positions, 9 * channels
            ),
            flipped_weight(w_fpn),
            preferred_element_type=jnp.float32,
        )
        .astype(jnp.bfloat16)
        .reshape(tile_rows, tile_cols, channels)
    )
    term_fpn = weight_term(
        feature_grad.reshape(tile_positions, channels),
        window_patches(input_padded, tile_rows, tile_cols, False).reshape(
            tile_positions, 9 * channels
        ),
    )
    head_one, head_two, fpn_total = (
        lax.psum_scatter(term_one.reshape(-1), ("ty", "tx"), scatter_dimension=0, tiled=True),
        lax.psum_scatter(term_two.reshape(-1), ("ty", "tx"), scatter_dimension=0, tiled=True),
        lax.psum_scatter(term_fpn.reshape(-1), ("ty", "tx"), scatter_dimension=0, tiled=True),
    )
    return (input_grad, head_one, head_two, fpn_total)


def solution(mesh):
    placed = (
        P(("ty", "tx"), None, None, None),
        P(("ty", "tx"), None, None, None),
        P(("ty", "tx"), None, None, None),
        P(),
        P(),
        P(("ty", "tx"), None, None),
        P(("ty", "tx"), None, None),
        P(("ty", "tx"), None),
        P(("ty", "tx")),
        P(("ty", "tx")),
        P("ty", "tx", None),
        P("ty", "tx", None),
        P(),
    )
    return jax.shard_map(
        local,
        mesh=mesh,
        in_specs=placed,
        out_specs=(P("ty", "tx", None), P(("ty", "tx")), P(("ty", "tx")), P(("ty", "tx"))),
        check_vma=False,
    )
```

profile of v0, /device:TPU:1, one launch (start us, length us, event | category | flops | bytes accessed | tf_op | source)
XLA Modules:
  0.0 480.4 jit_solution(14640340188337101602)
XLA Ops:
  10.3 6.4 %all-to-all-start = ((bf16[8,3,2]{1,2,0:T(2,128)(2,1)}), bf16[8,3,2]{1,2,0:T(2,128)(2,1)S(1)}, u32[]{:S(2)}, u32[]{:S(2)}) async-start(bf16[8,3,2]{1,2,0:T(2,128)(2,1)} %copy.62), calls=%async_computation | async-start | bytes 8192 | tf_op jit(solution)/shard_map/all_to_all | solution.py:160
  18.8 3.9 collective-permute-start.6
  22.8 2.1 collective-permute-start.7
  24.9 2.6 broadcast_compare_fusion
  27.5 1.5 slice_dynamic-update-slice_fusion.23
  30.4 1.8 slice_dynamic-update-slice_fusion.21
  32.1 1.6 slice_dynamic-update-slice_fusion.20
  35.0 1.7 slice_dynamic-update-slice_fusion.19
  36.8 1.6 slice_dynamic-update-slice_fusion.18
  39.8 1.8 slice_dynamic-update-slice_fusion.16
  41.6 16.8 %reshape.197 = bf16[2352,2304]{1,0:T(8,128)(2,1)} reshape(bf16[12,14,14,2304]{3,2,1,0:T(8,128)(2,1)} %slice_dynamic-update-slice_fusion.16) | data formatting | bytes 21676032 | tf_op jit(solution)/shard_map/reshape | solution.py:103
  58.4 2.8 gt.11
  61.2 2.4 copy.65
  63.6 8.5 %fusion.2 = bf16[2352,256]{1,0:T(8,128)(2,1)} fusion(pred[2352,256]{1,0:T(8,128)(4,1)} %gt.11, bf16[2352,2304]{1,0:T(8,128)(2,1)} %reshape.197, bf16[2304,256]{1,0:T(8,128)(2,1)} %bitcast.91), kind=kOutput, calls=%fused_computation.8 | convolution fusion | flops 2775736320 | bytes 13824000 | tf_op jit(solution)/shard_map/dot_general | solution.py:102
  72.1 3.0 reshape.199
  75.1 8.5 %pad_slice_fusion = (bf16[12,14,14,256]{3,2,1,0:T(8,128)(2,1)}, bf16[12,14,14,256]{3,2,1,0:T(8,128)(2,1)}, bf16[12,14,14,256]{3,2,1,0:T(8,128)(2,1)}, bf16[12,14...) fusion(bf16[12,14,14,256]{3,2,1,0:T(8,128)(2,1)} %reshape.199), kind=kLoop, calls=%fused_computation.45 | loop fusion | bytes 10838016 | tf_op jit(solution)/shard_map/slice | solution.py:33
  83.6 3.0 concatenate.80
  86.7 2.4 constant_dynamic-update-slice_fusion.9
  89.1 3.0 concatenate.81
  92.1 3.0 concatenate.82
  95.1 3.0 concatenate.83
  98.2 2.6 constant_dynamic-update-slice_fusion.8
  104.4 3.0 concatenate.84
  107.4 3.0 concatenate.85
  110.5 3.0 concatenate.86
  113.5 3.0 concatenate.87
  116.5 2.4 copy.66
  118.9 2.6 constant_dynamic-update-slice_fusion.4
  125.2 8.1 %convolution_convert_fusion.1 = bf16[2352,256]{1,0:T(8,128)(2,1)} fusion(bf16[2352,2304]{1,0:T(8,128)(2,1)} %constant_dynamic-update-slice_fusion.1, bf16[2304,256]{1,0:T(8,128)(2,1)S(1)} %bitcast.90), kind=kOutput, calls=%fused_computation.6 | convolution fusion | flops 2775134208 | bytes 13221888 | tf_op jit(solution)/shard_map/dot_general | solution.py:125
  133.3 3.4 reshape.201
  136.7 1.8 convolution_bitcast_fusion.2
  138.6 3.6 fusion.11
  148.8 4.5 copy-done.17
  153.3 2.5 copy.85
  155.8 5.7 %all-to-all-start.1 = ((bf16[8,3,16,16,256]{4,3,2,1,0:T(8,128)(2,1)}), bf16[8,3,16,16,256]{4,3,2,1,0:T(8,128)(2,1)}, u32[]{:S(2)}, u32[]{:S(2)}) async-start(bf16[8,3,16,16,256]{4,3,2,1,0:T(8,128)(2,1)} %bitcast.83), calls=%async_computation.1 | async-start | bytes 6291456 | tf_op jit(solution)/shard_map/all_to_all | solution.py:159
  161.7 9.6 %convolution_bitcast_fusion.1 = f32[256,2304]{0,1:T(8,128)} fusion(bf16[12,14,14,2304]{3,2,1,0:T(8,128)(2,1)} %copy-done.17, bf16[12,14,14,256]{3,2,1,0:T(8,128)(2,1)S(1)} %copy-done.2), kind=kOutput, calls=%fused_computation.5 | convolution fusion | flops 2774532096 | bytes 14401536 | tf_op jit(solution)/shard_map/dot_general | solution.py:44
  171.3 3.0 copy.72
  174.4 3.2 reshape.210
  177.6 1.6 slice_dynamic-update-slice_fusion.15
  180.4 1.7 slice_dynamic-update-slice_fusion.13
  182.1 1.7 slice_dynamic-update-slice_fusion.12
  185.1 1.7 slice_dynamic-update-slice_fusion.11
  186.7 1.8 slice_dynamic-update-slice_fusion.10
  189.9 1.6 slice_dynamic-update-slice_fusion.8
  191.5 16.7 %reshape.208 = bf16[2352,2304]{1,0:T(8,128)(2,1)} reshape(bf16[12,14,14,2304]{3,2,1,0:T(8,128)(2,1)} %slice_dynamic-update-slice_fusion.8) | data formatting | bytes 21676032 | tf_op jit(solution)/shard_map/reshape | solution.py:120
  208.2 8.8 %fusion.36 = f32[256,2304]{1,0:T(8,128)} fusion(bf16[2352,256]{1,0:T(8,128)(2,1)S(1)} %copy-done.5, bf16[2352,2304]{1,0:T(8,128)(2,1)} %reshape.208), kind=kOutput, calls=%fused_computation.128 | convolution fusion | flops 2774532096 | bytes 14401536 | tf_op jit(solution)/shard_map/dot_general | solution.py:44
  217.0 3.1 reshape.209
  220.5 3.3 collective-permute-start.8
  225.1 3.5 collective-permute-done.9
  233.2 11.7 %convert_bitcast_fusion = bf16[24,16,80,256]{3,2,1,0:T(8,128)(2,1)} fusion(bf16[24,16,16,256]{3,2,1,0:T(8,128)(2,1)} %bitcast.15, s32[24,16]{1,0:T(8,128)S(1)} %iota_add_fusion), kind=kOutput, calls=%fused_computation.3 | convolution fusion | flops 259553280 | bytes 18875904 | tf_op jit(solution)/shard_map/sXx,syxc->syXc/dot_general | solution.py:73
  244.8 29.1 %fusion.5 = f32[32,80,256]{2,0,1:T(8,128)S(1)} fusion(bf16[24,16,80,256]{3,2,1,0:T(8,128)(2,1)} %convert_bitcast_fusion, s32[24,16]{0,1:T(8,128)S(1)} %iota_add_fusion.1), kind=kOutput, calls=%fused_computation.12 | convolution fusion | flops 503328768 | bytes 18351616 | tf_op jit(solution)/shard_map/sYy,syXc->YXc/dot_general | solution.py:76
  274.0 6.2 %collective-permute-start = (bf16[32,16,256]{2,0,1:T(8,128)(2,1)S(1)}, bf16[32,16,256]{2,0,1:T(8,128)(2,1)S(1)}, u32[]{:S(2)}, u32[]{:S(2)}) collective-permute-start(bf16[32,16,256]{2,0,1:T(8,128)(2,1)S(1)} %slice.393), channel_id=1, source_target_pairs={{0,1},{1,2},{2,3},{3,4},{4,5},{5,6},{6,7},{8,9},{9,10},{10,11},{11... | collective-permute-start | bytes 786440 | tf_op jit(solution)/shard_map/ppermute | solution.py:10
  282.7 2.8 collective-permute-done
  285.6 2.6 collective-permute-start.1
  291.5 2.8 collective-permute-done.1
  294.8 3.7 convolution_bitcast_fusion
  298.6 1.6 reshape.211
  300.3 4.5 collective-permute-start.2
  304.8 1.9 collective-permute-start.3
  306.7 3.6 collective-permute-done.3
  311.7 5.3 %collective-permute-start.5 = (bf16[18,1,256]{2,0,1:T(8,128)(2,1)S(1)}, bf16[18,1,256]{2,0,1:T(8,128)(2,1)S(1)}, u32[]{:S(2)}, u32[]{:S(2)}) collective-permute-start(bf16[18,1,256]{2,0,1:T(8,128)(2,1)S(1)} %get-tuple-element.53), channel_id=1, source_target_pairs={{0,1},{1,2},{2,3},{3,4},{4,5},{5,6},{6,7},{8,9},{9,10},{10,11},{11... | collective-permute-start | bytes 27656 | tf_op jit(solution)/shard_map/ppermute | solution.py:18
  321.4 2.2 convolution_convert_fusion.2
  323.6 145.3 %all-reduce.10.cloned.1.call-done = (f32[589824]{0:T(1024)}, f32[589824]{0:T(1024)}, f32[589824]{0:T(1024)}) async-done(((f32[589824]{0:T(1024)}, f32[589824]{0:T(1024)}, f32[589824]{0:T(1024)}), (f32[589824]{0:T(1024)}, f32[589824]{0:T(1024)}, f32[589824]{0:T(1024)})) %all-reduce.10.cloned.1.call-update) | async-done | bytes 7077904
  470.3 1.5 dynamic-slice.14
  (120 shorter events, 48.8 us)
Async XLA Ops:
  7.2 131.4 %copy-start = (bf16[12,16,14]{2,1,0:T(8,128)(2,1)S(1)}, bf16[12,16,14]{2,1,0:T(8,128)(2,1)}, u32[]{:S(2)}) copy-start(bf16[12,16,14]{2,1,0:T(8,128)(2,1)} %param.24) | copy-start | bytes 16132
  10.3 145.5 %all-to-all-start = ((bf16[8,3,2]{1,2,0:T(2,128)(2,1)}), bf16[8,3,2]{1,2,0:T(2,128)(2,1)S(1)}, u32[]{:S(2)}, u32[]{:S(2)}) async-start(bf16[8,3,2]{1,2,0:T(2,128)(2,1)} %copy.62), calls=%async_computation | async-start | bytes 8192 | tf_op jit(solution)/shard_map/all_to_all | solution.py:160
  16.6 10.8 %copy-start.6 = (bf16[12,14,14,256]{3,2,1,0:T(8,128)(2,1)S(1)}, bf16[12,14,14,256]{3,2,1,0:T(8,128)(2,1)}, u32[]{:S(2)}) copy-start(bf16[12,14,14,256]{3,2,1,0:T(8,128)(2,1)} %param.20) | copy-start | bytes 3612676
  18.8 201.6 %collective-permute-start.6 = (bf16[1,64,256]{2,0,1:T(2,128)(2,1)}, bf16[1,64,256]{2,0,1:T(2,128)(2,1)S(1)}, u32[]{:S(2)}, u32[]{:S(2)}) collective-permute-start(bf16[1,64,256]{2,0,1:T(2,128)(2,1)} %get-tuple-element.55), channel_id=1, source_target_pairs={{0,8},{8,16},{16,24},{1,9},{9,17},{17,25},{2,10},{10,18},{18,26},{... | collective-permute-start | bytes 98312 | tf_op jit(solution)/shard_map/ppermute | solution.py:18
  22.8 4.7 copy-start.2
  22.8 197.7 %collective-permute-start.7 = (bf16[1,64,256]{2,0,1:T(2,128)(2,1)S(1)}, bf16[1,64,256]{2,0,1:T(2,128)(2,1)S(1)}, u32[]{:S(2)}, u32[]{:S(2)}) collective-permute-start(bf16[1,64,256]{2,0,1:T(2,128)(2,1)S(1)} %get-tuple-element.56), channel_id=1, source_target_pairs={{8,0},{16,8},{24,16},{9,1},{17,9},{25,17},{10,2},{18,10},{26,18},{... | collective-permute-start | bytes 98312 | tf_op jit(solution)/shard_map/ppermute | solution.py:21
  98.2 2.6 copy-start.12
  98.2 3.8 copy-start.11
  100.8 2.4 copy-start.4
  118.9 2.6 copy-start.10
  118.9 3.9 copy-start.8
  121.5 2.4 copy-start.9
  122.8 2.4 copy-start.15
  145.8 1.3 copy-start.7
  148.8 4.5 copy-start.17
  155.8 77.4 %all-to-all-start.1 = ((bf16[8,3,16,16,256]{4,3,2,1,0:T(8,128)(2,1)}), bf16[8,3,16,16,256]{4,3,2,1,0:T(8,128)(2,1)}, u32[]{:S(2)}, u32[]{:S(2)}) async-start(bf16[8,3,16,16,256]{4,3,2,1,0:T(8,128)(2,1)} %bitcast.83), calls=%async_computation.1 | async-start | bytes 6291456 | tf_op jit(solution)/shard_map/all_to_all | solution.py:159
  161.5 307.4 %all-reduce.10.cloned.1.call-start = ((), (), s32[]{:S(2)}) async-start(), calls=%async_computation.2 | async-start | bytes 14155776
  174.4 3.2 copy-start.3
  191.5 16.7 %copy-start.5 = (bf16[2352,256]{1,0:T(8,128)(2,1)S(1)}, bf16[2352,256]{1,0:T(8,128)(2,1)}, u32[]{:S(2)}) copy-start(bf16[2352,256]{1,0:T(8,128)(2,1)} %fusion.2) | copy-start | bytes 3612676
  220.5 4.6 collective-permute-start.8
  223.8 4.8 %collective-permute-start.9 = (bf16[18,1,256]{2,0,1:T(8,128)(2,1)S(1)}, bf16[18,1,256]{2,0,1:T(8,128)(2,1)S(1)}, u32[]{:S(2)}, u32[]{:S(2)}) collective-permute-start(bf16[18,1,256]{2,0,1:T(8,128)(2,1)S(1)} %get-tuple-element.49), channel_id=1, source_target_pairs={{1,0},{2,1},{3,2},{4,3},{5,4},{6,5},{7,6},{9,8},{10,9},{11,10},{12... | collective-permute-start | bytes 27656 | tf_op jit(solution)/shard_map/ppermute | solution.py:21
  244.8 35.3 %copy-start.13 = (bf16[16,64,256]{2,1,0:T(8,128)(2,1)S(1)}, bf16[16,64,256]{2,1,0:T(8,128)(2,1)}, u32[]{:S(2)}) copy-start(bf16[16,64,256]{2,1,0:T(8,128)(2,1)} %param.29) | copy-start | bytes 1572868
  274.0 11.4 %collective-permute-start = (bf16[32,16,256]{2,0,1:T(8,128)(2,1)S(1)}, bf16[32,16,256]{2,0,1:T(8,128)(2,1)S(1)}, u32[]{:S(2)}, u32[]{:S(2)}) collective-permute-start(bf16[32,16,256]{2,0,1:T(8,128)(2,1)S(1)} %slice.393), channel_id=1, source_target_pairs={{0,1},{1,2},{2,3},{3,4},{4,5},{5,6},{6,7},{8,9},{9,10},{10,11},{11... | collective-permute-start | bytes 786440 | tf_op jit(solution)/shard_map/ppermute | solution.py:10
  285.5 8.8 %copy-start.16 = (bf16[16,64,256]{2,1,0:T(8,128)(2,1)S(1)}, bf16[16,64,256]{2,1,0:T(8,128)(2,1)}, u32[]{:S(2)}) copy-start(bf16[16,64,256]{2,1,0:T(8,128)(2,1)} %param.30) | copy-start | bytes 1572868
  285.6 8.7 %collective-permute-start.1 = (bf16[16,64,256]{2,0,1:T(8,128)(2,1)S(1)}, bf16[16,64,256]{2,0,1:T(8,128)(2,1)S(1)}, u32[]{:S(2)}, u32[]{:S(2)}) collective-permute-start(bf16[16,64,256]{2,0,1:T(8,128)(2,1)S(1)} %slice.392), channel_id=1, source_target_pairs={{0,8},{8,16},{16,24},{1,9},{9,17},{17,25},{2,10},{10,18},{18,26},{... | collective-permute-start | bytes 1572872 | tf_op jit(solution)/shard_map/ppermute | solution.py:10
  300.1 16.8 %copy-start.14 = (bf16[3,3,256,256]{3,2,1,0:T(8,128)(2,1)S(1)}, bf16[3,3,256,256]{3,2,1,0:T(8,128)(2,1)}, u32[]{:S(2)}) copy-start(bf16[3,3,256,256]{3,2,1,0:T(8,128)(2,1)} %param.31) | copy-start | bytes 3538948
  300.3 6.5 %collective-permute-start.2 = (bf16[1,64,256]{2,0,1:T(2,128)(2,1)S(1)}, bf16[1,64,256]{2,0,1:T(2,128)(2,1)S(1)}, u32[]{:S(2)}, u32[]{:S(2)}) collective-permute-start(bf16[1,64,256]{2,0,1:T(2,128)(2,1)S(1)} %get-tuple-element.57), channel_id=1, source_target_pairs={{0,8},{8,16},{16,24},{1,9},{9,17},{17,25},{2,10},{10,18},{18,26},{... | collective-permute-start | bytes 98312 | tf_op jit(solution)/shard_map/ppermute | solution.py:18
  304.8 5.6 %collective-permute-start.3 = (bf16[1,64,256]{2,0,1:T(2,128)(2,1)S(1)}, bf16[1,64,256]{2,0,1:T(2,128)(2,1)S(1)}, u32[]{:S(2)}, u32[]{:S(2)}) collective-permute-start(bf16[1,64,256]{2,0,1:T(2,128)(2,1)S(1)} %get-tuple-element.58), channel_id=1, source_target_pairs={{8,0},{16,8},{24,16},{9,1},{17,9},{25,17},{10,2},{18,10},{26,18},{... | collective-permute-start | bytes 98312 | tf_op jit(solution)/shard_map/ppermute | solution.py:21
  310.4 7.3 %collective-permute-start.4 = (bf16[18,1,256]{2,0,1:T(8,128)(2,1)S(1)}, bf16[18,1,256]{2,0,1:T(8,128)(2,1)S(1)}, u32[]{:S(2)}, u32[]{:S(2)}) collective-permute-start(bf16[18,1,256]{2,0,1:T(8,128)(2,1)S(1)} %get-tuple-element.54), channel_id=1, source_target_pairs={{1,0},{2,1},{3,2},{4,3},{5,4},{6,5},{7,6},{9,8},{10,9},{11,10},{12... | collective-permute-start | bytes 27656 | tf_op jit(solution)/shard_map/ppermute | solution.py:21
  311.7 6.1 %collective-permute-start.5 = (bf16[18,1,256]{2,0,1:T(8,128)(2,1)S(1)}, bf16[18,1,256]{2,0,1:T(8,128)(2,1)S(1)}, u32[]{:S(2)}, u32[]{:S(2)}) collective-permute-start(bf16[18,1,256]{2,0,1:T(8,128)(2,1)S(1)} %get-tuple-element.53), channel_id=1, source_target_pairs={{0,1},{1,2},{2,3},{3,4},{4,5},{5,6},{6,7},{8,9},{9,10},{10,11},{11... | collective-permute-start | bytes 27656 | tf_op jit(solution)/shard_map/ppermute | solution.py:18
  321.4 152.0 %copy-start.1 = (bf16[12,16,14]{2,1,0:T(8,128)(2,1)S(1)}, bf16[12,16,14]{2,1,0:T(8,128)(2,1)}, u32[]{:S(2)}) copy-start(bf16[12,16,14]{2,1,0:T(8,128)(2,1)} %param.24) | copy-start | bytes 16132
Sparse Core Ops, SparseCore 0:
  300.3 168.4 all-reduce.9
where the time goes:
time: 488 us; the launch traced here: 480 us
  local copies, waits for them, and re-layouts  165 us (34%)
  waiting for transfers between devices  158 us (32%)
  matrix products  88.2 us (18%)
  starting transfers between devices  44.7 us (9%)
  between operations  14.7 us (3%)
  other arithmetic  9.97 us (2%)
    unnamed x2, waiting for transfers between devices  145 us
    unnamed x89, local copies, waits for them, and re-layouts  68 us
    concatenate x15, local copies, waits for them, and re-layouts, window_patches(): return jnp.concatenate(pieces, axis=-1)  31.7 us
    dot_general x1, matrix products, place_windows(): jnp.einsum('sYy,syXc->YXc', row_hit, spread, preferred_element_type=jnp.f...  29.1 us
    dot_general x3, matrix products, weight_term(): lax.dot_general(gradient, inputs_patch, (((0,), (0,)), ((), ())), preferr...  22.1 us
    ppermute x4, starting transfers between devices, extended(): lax.ppermute(lax.slice_in_dim(block, block.shape[dim] - width, None, axis...  17.1 us
    reshape x1, local copies, waits for them, and re-layouts, local(): window_patches(jnp.pad(grad_two, region_pad), pool_size, pool_size, True)  16.8 us
    reshape x1, local copies, waits for them, and re-layouts, local(): window_patches(jnp.pad(roi_feat, region_pad), pool_size, pool_size, False)  16.7 us
  transfers between devices with their start and end apart: 13, of which 5 were waited for; matrix products, arithmetic and copies ran while one was open for 42% of the time, Pallas kernels for 0%

commit v1 on v0

v1 whole, which is shorter than its diff:
```python
import functools

import jax
import jax.numpy as jnp
from jax import lax
from jax.experimental import pallas as pl
from jax.experimental.pallas import tpu as pltpu
from jax.sharding import PartitionSpec as P

BF = jnp.bfloat16
F32 = jnp.float32
VMEM_BYTES = 56 << 20
NT = (((1,), (1,)), ((), ()))


def ceil_to(value, multiple):
    return -(-value // multiple) * multiple


def slot_rows(pool):
    return ceil_to(pool * pool + 3, 8)


def params():
    return pltpu.CompilerParams(vmem_limit_bytes=VMEM_BYTES)


def cost(flops=1):
    return pl.CostEstimate(flops=int(flops), bytes_accessed=1, transcendentals=0)


def whole(array):
    return pl.BlockSpec(array.shape, lambda *_: (0,) * array.ndim)


def head_body(geometry, target, off_row, off_col, row_ref, col_ref, grad_hbm, pre_hbm, w_two_hbm, w_one_hbm, *rest):
    pool, pitch, regions, capacity, columns, together = geometry
    one_hbm, out = rest[0], rest[1]
    (order, slot_at, held, facts, bare, grads, pres, ones, w_two, w_one, wide, mask, again, packed, taps, sems, out_sems, w_sems) = rest[2:]
    block = (pool + 1) * pitch
    length, rows = together * block + pitch, together * block - pitch

    for j, (src, dst) in enumerate(((w_two_hbm, w_two), (w_one_hbm, w_one))):
        pltpu.make_async_copy(src, dst, w_sems.at[j]).start()
    for q in range(columns):
        held[q] = 0

    def scan(r, count):
        group = target[r]
        rank = held[group]
        held[group] = rank + 1
        order[count] = r
        slot_at[count] = group * capacity + rank
        return count + 1

    count = lax.fori_loop(0, regions, scan, 0)
    steps = (count + together - 1) // together

    def loads(step, which):
        copies = []
        for r in range(together):
            region = order[jnp.minimum(step * together + r, count - 1)]
            for j, (src, dst) in enumerate(((grad_hbm, grads), (pre_hbm, pres))):
                copies.append(pltpu.make_async_copy(src.at[region], dst.at[which, r], sems.at[which, r, j]))
        return copies

    def store(step, which, r):
        region = order[jnp.minimum(step * together + r, count - 1)]
        return pltpu.make_async_copy(
            ones.at[which, pl.ds(r * block, block)],
            one_hbm.at[pl.ds(pl.multiple_of(region * block, block), block)],
            out_sems.at[which, r],
        )

    def settle(step, which):
        for r in range(together):

            @pl.when(step * together + r < count)
            def _(r=r):
                store(step, which, r).wait()

    @pl.when(count > 0)
    def _():
        for copy in loads(0, 0):
            copy.start()

    channels, bins = wide.shape[1], pool * pool
    extent = row_ref.shape[1]
    lane = lax.broadcasted_iota(jnp.int32, (128, channels), 1)
    own = lax.broadcasted_iota(jnp.int32, (128, channels), 0) == lane % pool
    spread = jnp.where(own & (lane < extent * pool), 1.0, 0.0).astype(BF)
    flat = (regions * extent, channels)
    own = lax.broadcasted_iota(jnp.int32, flat, 0) % extent == lax.broadcasted_iota(jnp.int32, flat, 1) // pool
    bare[...] = jnp.zeros_like(bare)
    for j, ref in enumerate((row_ref, col_ref)):
        bare[:, pl.ds(0, pool)] = ref[...].reshape(regions * extent, pool).astype(F32)
        entry = jnp.dot(bare[...].astype(BF), spread, preferred_element_type=F32)
        entry = jnp.where(own, entry, 0.0).reshape(regions, extent, channels)
        facts[j, pl.ds(0, regions), :] = jnp.sum(entry, axis=1)
    lane = lax.broadcasted_iota(jnp.int32, (1, channels), 1)
    out[...] = jnp.zeros_like(out)
    wide[...] = jnp.zeros_like(wide)
    again[...] = jnp.zeros_like(again)
    mask[...] = jnp.zeros_like(mask)
    packed[...] = jnp.zeros_like(packed)
    for which in range(2):
        for r in range(together):
            ones[which, pl.ds((r + 1) * block - pitch, pitch), :] = jnp.zeros((pitch, wide.shape[1]), BF)
    for j, (src, dst) in enumerate(((w_two_hbm, w_two), (w_one_hbm, w_one))):
        pltpu.make_async_copy(src, dst, w_sems.at[j]).wait()

    def conv(source, weight):
        for e in range(3):
            taps[e] = source[pl.ds(7 + e, length), :].astype(BF)
        total = None
        for ey in range(3):
            for ex in range(3):
                term = lax.dot_general(
                    taps[ex, pl.ds(ey * pitch, rows), :],
                    weight[2 - ey, 2 - ex],
                    NT,
                    preferred_element_type=F32,
                )
                total = term if total is None else total + term
        return total

    def turn(step, carry):
        which = step % 2

        @pl.when(step + 1 < steps)
        def _():
            for copy in loads(step + 1, 1 - which):
                copy.start()

        for copy in loads(step, which):
            copy.wait()

        @pl.when(step >= 2)
        def _():
            settle(step - 2, which)

        for r in range(together):
            for y in range(pool):
                at = r * block + y * pitch
                wide[pl.ds(8 + pitch + at, pool), :] = grads[which, r, y].astype(F32)
                mask[pl.ds(at, pool), :] = pres[which, r, y].astype(F32)
        grad_one = jnp.where(mask[pl.ds(0, rows), :] > 0, conv(wide, w_two), 0.0)
        again[pl.ds(8 + pitch, rows), :] = grad_one
        ones[which, pl.ds(0, rows), :] = grad_one.astype(BF)
        for r in range(together):

            @pl.when(step * together + r < count)
            def _(r=r):
                store(step, which, r).start()

        region_grad = conv(again, w_one)
        for r in range(together):
            for y in range(pool):
                at = r * block + y * pitch
                packed[pl.ds(y * pool, pitch), :] = region_grad[at : at + pitch]
            at = jnp.minimum(step * together + r, count - 1)
            region = order[at]
            for j in range(2):
                packed[pl.ds(bins + j, 1), :] = facts[j, pl.ds(region, 1), :]
            place = jnp.where(lane == 0, off_row[region], jnp.where(lane == 1, off_col[region], lane == 2))
            packed[pl.ds(bins + 2, 1), :] = place.astype(F32)
            out[slot_at[at]] = packed[pl.ds(0, out.shape[1]), :].astype(BF)

        return carry

    lax.fori_loop(0, steps, turn, 0)

    @pl.when(steps > 1)
    def _():
        settle(steps - 2, steps % 2)

    @pl.when(steps > 0)
    def _():
        settle(steps - 1, (steps - 1) % 2)


def region_heads(grad_two, pre_one, w_two, w_one, roi_rows, roi_cols, target, off_row, off_col, columns, capacity, together=2):
    regions, pool, _, channels = grad_two.shape
    pitch = ceil_to(pool + 1, 16)
    block = (pool + 1) * pitch
    length = together * block + pitch
    anywhere = pl.BlockSpec(memory_space=pl.ANY)
    smem = pl.BlockSpec(memory_space=pltpu.SMEM)
    vmem = pl.BlockSpec(memory_space=pltpu.VMEM)
    return pl.pallas_call(
        functools.partial(head_body, (pool, pitch, regions, capacity, columns, together)),
        in_specs=[smem] * 3 + [vmem] * 2 + [anywhere] * 4,
        out_specs=[anywhere, vmem],
        out_shape=[
            jax.ShapeDtypeStruct((regions * block, channels), BF),
            jax.ShapeDtypeStruct((columns * capacity, slot_rows(pool), channels), BF),
        ],
        scratch_shapes=[
            pltpu.SMEM((regions,), jnp.int32),
            pltpu.SMEM((regions,), jnp.int32),
            pltpu.SMEM((columns,), jnp.int32),
            pltpu.VMEM((2, ceil_to(regions, 8), channels), F32),
            pltpu.VMEM((regions * roi_rows.shape[1], 128), F32),
            pltpu.VMEM((2, together, pool, pool, channels), BF),
            pltpu.VMEM((2, together, pool, pool, channels), BF),
            pltpu.VMEM((2, together * block, channels), BF),
            pltpu.VMEM(w_two.shape, BF),
            pltpu.VMEM(w_one.shape, BF),
            pltpu.VMEM((length + 16, channels), F32),
            pltpu.VMEM((length, channels), F32),
            pltpu.VMEM((length + 16, channels), F32),
            pltpu.VMEM((pool * pool + pitch, channels), F32),
            pltpu.VMEM((3, length, channels), BF),
            pltpu.SemaphoreType.DMA((2, together, 2)),
            pltpu.SemaphoreType.DMA((2, together)),
            pltpu.SemaphoreType.DMA((2,)),
        ],
        compiler_params=params(),
        cost_estimate=cost(72 * regions * block * channels * channels),
        name="region_heads",
    )(target, off_row, off_col, roi_rows, roi_cols, grad_two, pre_one, w_two, w_one)


def spread_rows(where, source, keep, send, layout):
    chips, highs, share = layout
    core, chip, low, high = where[0] % 2, where[0] // 2, where[1] % 2, where[1] // 2
    for other, out in enumerate((keep, send)):
        for a in range(chips):
            for b in range(2):
                for k in range(highs):
                    block = (((chip ^ a) * 2 + (core ^ other)) * highs + (high ^ k)) * 2 + (low ^ b)
                    place = ((a * 2 + b) * highs + k) * share
                    if share % 8 == 0:
                        rows = source[pl.ds(pl.multiple_of(block * share, 8), share), :]
                    else:
                        rows = source[pl.ds(pl.multiple_of(block * share // 8 * 8, 8), 8), :]
                        rows = pltpu.roll(rows, (8 - block * share % 8) % 8, 0)[:share]
                    out[pl.ds(place, share), :] = rows


def head_weight_body(geometry, where, two_ref, pre_ref, one_hbm, feat_hbm, keep_ref, send_ref, one, feat, turned, wide, taps, product, passed, sems):
    regions, pool, pitch, layout = geometry
    block = (pool + 1) * pitch
    length = turned.shape[1]
    step = pl.program_id(0)
    copies = [pltpu.make_async_copy(one_hbm, one, sems.at[0]), pltpu.make_async_copy(feat_hbm, feat, sems.at[1])]

    def lay_out(ref, relu):
        for r in range(regions):
            for y in range(pool):
                entry = ref[r, y].astype(F32)
                wide[pl.ds(8 + pitch + r * block + y * pitch, pool), :] = jnp.maximum(entry, 0.0) if relu else entry
        for e in range(3):
            taps[e] = wide[pl.ds(7 + e, length + 2 * pitch), :].astype(BF)

    @pl.when(step == 0)
    def _():
        for copy in copies:
            copy.start()
        wide[...] = jnp.zeros_like(wide)
        turned[...] = jnp.zeros_like(turned)
        lay_out(two_ref, False)
        for r in range(regions):
            turned[:, pl.ds(r * block, block)] = taps[1, pl.ds(pitch + r * block, block), :].T
        lay_out(pre_ref, True)

    @pl.when(step == 3)
    def _():
        for copy in copies:
            copy.wait()
        for r in range(regions):
            turned[:, pl.ds(r * block, block)] = one[pl.ds(r * block, block), :].T
        lay_out(feat, False)

    channels = taps.shape[2]
    for ex in range(3):
        patch = taps[ex, pl.ds(pl.multiple_of(step % 3 * pitch, pitch), length), :]
        product[:, ex * channels : (ex + 1) * channels] = jnp.dot(turned[...], patch, preferred_element_type=F32)
    spread_rows(where, product, keep_ref.at[0], passed, layout)
    send_ref[0] = passed[...].astype(BF)


def head_weight_grads(where, layout, grad_two, pre_one, grad_one, roi_feat):
    regions, pool, _, channels = roi_feat.shape
    pitch = ceil_to(pool + 1, 16)
    length = ceil_to(regions * (pool + 1) * pitch, 128)
    anywhere = pl.BlockSpec(memory_space=pl.ANY)
    out = pl.BlockSpec((1, channels // 2, 3 * channels), lambda s: (s // 3, 0, s % 3))
    return pl.pallas_call(
        functools.partial(head_weight_body, (regions, pool, pitch, layout)),
        grid=(6,),
        in_specs=[pl.BlockSpec(memory_space=pltpu.SMEM), whole(grad_two), whole(pre_one), anywhere, anywhere],
        out_specs=[out, out],
        out_shape=[
            jax.ShapeDtypeStruct((2, channels // 2, 9 * channels), F32),
            jax.ShapeDtypeStruct((2, channels // 2, 9 * channels), BF),
        ],
        scratch_shapes=[
            pltpu.VMEM(grad_one.shape, BF),
            pltpu.VMEM(roi_feat.shape, BF),
            pltpu.VMEM((channels, length), BF),
            pltpu.VMEM((length + 2 * pitch + 16, channels), F32),
            pltpu.VMEM((3, length + 2 * pitch, channels), BF),
            pltpu.VMEM((channels, 3 * channels), F32),
            pltpu.VMEM((channels // 2, 3 * channels), F32),
            pltpu.SemaphoreType.DMA((2,)),
        ],
        compiler_params=params(),
        cost_estimate=cost(),
        name="head_weight_grads",
    )(where, grad_two, pre_one, grad_one, roi_feat)


def lay_body(geometry, own_ref, left_ref, right_ref, out_ref, wide):
    rows, pitch, tile_cols = geometry
    wide[...] = jnp.zeros_like(wide)
    for y in range(rows):
        at = 8 + y * pitch
        wide[pl.ds(at, tile_cols), :] = own_ref[y].astype(F32)
        wide[pl.ds(at + tile_cols, pitch - tile_cols), :] = right_ref[y].astype(F32)
    for e in (1, 2):
        out_ref[e] = wide[pl.ds(7 + e, out_ref.shape[1]), :].astype(BF)
    for y in range(rows):
        wide[pl.ds(7 + y * pitch, 1), :] = left_ref[y].astype(F32)
    out_ref[0] = wide[pl.ds(7, out_ref.shape[1]), :].astype(BF)


def lay_out_input(own, left, right):
    rows, tile_cols, channels = own.shape
    pitch = tile_cols + right.shape[1]
    vmem = pl.BlockSpec(memory_space=pltpu.VMEM)
    full = ceil_to(rows, 2)
    return pl.pallas_call(
        functools.partial(lay_body, (rows, pitch, tile_cols)),
        in_specs=[vmem] * 3,
        out_specs=vmem,
        out_shape=jax.ShapeDtypeStruct((3, full * pitch, channels), BF),
        scratch_shapes=[pltpu.VMEM((full * pitch + 16, channels), F32)],
        compiler_params=params(),
        cost_estimate=cost(),
        name="lay_out_input",
    )(own, left, right)


def place_all(geometry, received, start_ref, canvas, row_spread, col_spread, block, numbers, place, sem):
    slots, extent, pool, tile_rows, tile_cols = geometry
    depth, channels = received.shape[1], received.shape[2]
    wide, bins = extent + 8, pool * pool
    facts = received[:, pl.ds(bins // 8 * 8, depth - bins // 8 * 8), :].astype(F32)
    numbers[...] = facts[:, bins % 8 + 2, :128].astype(jnp.int32)
    copy = pltpu.make_async_copy(numbers, place, sem)
    copy.start()
    full = block.shape[0]
    lane = lax.broadcasted_iota(jnp.int32, (channels, full), 1)
    source = lax.broadcasted_iota(jnp.int32, (channels, full), 0) % pool
    own = lax.broadcasted_iota(jnp.int32, (slots, extent, channels), 1) == (
        lax.broadcasted_iota(jnp.int32, (slots, extent, channels), 2) // pool
    )
    for j, (out, part) in enumerate(((row_spread, lane // pool), (col_spread, lane % pool))):
        chosen = jnp.where((part == source) & (lane < bins), 1.0, 0.0).astype(BF)
        entry = jnp.broadcast_to(facts[:, bins % 8 + j : bins % 8 + j + 1, :], (slots, extent, channels))
        entry = jnp.where(own, entry, 0.0).astype(BF).reshape(slots * extent, channels)
        entry = jnp.dot(entry, chosen, preferred_element_type=F32).reshape(slots, extent, full)
        out[:, pl.ds(0, extent), :] = entry
    col_spread[:, pl.ds(extent, 8), :] = jnp.zeros((slots, 8, full), F32)
    block[...] = jnp.zeros_like(block)
    canvas[...] = jnp.zeros_like(canvas)
    canvas[pl.ds(0, tile_rows), pl.ds(0, tile_cols), :] = start_ref[...].astype(F32)
    copy.wait()

    def put(slot, carry):
        @pl.when(place[slot, 2] > 0)
        def _():
            row, col = place[slot, 0], place[slot, 1]
            cols = pltpu.roll(col_spread[slot], col % 8, 0)
            rows = row_spread[slot]
            weights = jnp.concatenate([rows[y : y + 1] * cols for y in range(extent)], axis=0).astype(BF)
            block[pl.ds(0, depth), :] = received[slot]
            window = jnp.dot(weights, block[...], preferred_element_type=F32)
            at = pl.multiple_of(col // 8 * 8, 8)
            for y in range(extent):
                here = (row + y, pl.ds(at, wide))
                canvas[here] = canvas[here] + window[y * wide : (y + 1) * wide]

        return carry

    lax.fori_loop(0, slots, put, 0)


def tile_body(geometry, where, start_ref, received, taps_hbm, canvas, keep_hbm, send_hbm, taps, turned, product, keep, send, row_spread, col_spread, block, numbers, place, sems):
    slots, extent, pool, tile_rows, tile_cols, downs, acrosses, layout = geometry
    rows, pitch, channels = canvas.shape
    load = pltpu.make_async_copy(taps_hbm, taps, sems.at[0])
    load.start()
    place_all(
        (slots, extent, pool, tile_rows, tile_cols), received, start_ref, canvas, row_spread, col_spread, block, numbers, place, sems.at[1]
    )

    @pl.when(where[0] == downs - 1)
    def _():
        canvas[pl.ds(tile_rows, extent)] = jnp.zeros((extent, pitch, channels), F32)

    @pl.when(where[1] == acrosses - 1)
    def _():
        canvas[:, pl.ds(tile_cols, extent), :] = jnp.zeros((rows, extent, channels), F32)

    for y in range(0, rows, 2):
        entry = canvas[pl.ds(y, 2)].reshape(2 * pitch, channels)
        turned[:, pl.ds(y * pitch, 2 * pitch)] = entry.astype(BF).T
    load.wait()
    length = rows * pitch
    for ey in range(3):
        for ex in range(3):
            patch = taps[ex, pl.ds(ey * pitch, length), :]
            product[:, ex * channels : (ex + 1) * channels] = jnp.dot(
                turned[...], patch, preferred_element_type=F32
            )
        at = pl.ds(ey * 3 * channels, 3 * channels)
        spread_rows(where, product, keep.at[:, at], send.at[:, at], layout)
    keep_hbm[0] = keep[...]
    send_hbm[0] = send[...].astype(BF)


def tile_gradient(where, layout, start, received, taps, extent, pool, downs, acrosses):
    tile_rows, tile_cols, channels = start.shape
    slots, depth, _ = received.shape
    rows, pitch = tile_rows + extent, tile_cols + extent
    smem = pl.BlockSpec(memory_space=pltpu.SMEM)
    vmem = pl.BlockSpec(memory_space=pltpu.VMEM)
    geometry = (slots, extent, pool, tile_rows, tile_cols, downs, acrosses, layout)
    return pl.pallas_call(
        functools.partial(tile_body, geometry),
        in_specs=[smem, vmem, vmem, pl.BlockSpec(memory_space=pl.ANY)],
        out_specs=[vmem, vmem, vmem],
        out_shape=[
            jax.ShapeDtypeStruct((rows, pitch, channels), F32),
            jax.ShapeDtypeStruct((1, channels // 2, 9 * channels), F32),
            jax.ShapeDtypeStruct((1, channels // 2, 9 * channels), BF),
        ],
        scratch_shapes=[
            pltpu.VMEM(taps.shape, BF),
            pltpu.VMEM((channels, rows * pitch), BF),
            pltpu.VMEM((channels, 3 * channels), F32),
            pltpu.VMEM((channels // 2, 9 * channels), F32),
            pltpu.VMEM((channels // 2, 9 * channels), F32),
            pltpu.VMEM((slots, extent, ceil_to(depth, 128)), F32),
            pltpu.VMEM((slots, extent + 8, ceil_to(depth, 128)), F32),
            pltpu.VMEM((ceil_to(depth, 128), channels), BF),
            pltpu.VMEM((slots, 128), jnp.int32),
            pltpu.SMEM((slots, 128), jnp.int32),
            pltpu.SemaphoreType.DMA((2,)),
        ],
        compiler_params=params(),
        cost_estimate=cost(36 * rows * pitch * channels * channels),
        name="tile_gradient",
    )(where, start, received, taps)


def tile_input_body(pitch, rows, left_ref, mid_ref, right_ref, weight, out_ref):
    refs = (left_ref, mid_ref, right_ref)
    half = rows // 2
    for part in range(2):
        total = None
        for ey in range(3):
            for ex in range(3):
                term = lax.dot_general(
                    refs[ex][pl.ds((part * half + ey) * pitch, half * pitch), :],
                    weight[2 - ey, 2 - ex],
                    NT,
                    preferred_element_type=F32,
                )
                total = term if total is None else total + term
        out_ref[pl.ds(part * half * pitch, half * pitch), :] = total.astype(BF)


def tile_input_grad(shifted_grads, weight):
    rows, pitch, channels = shifted_grads[0].shape
    rows = rows - 2
    flat = [a.reshape((rows + 2) * pitch, channels) for a in shifted_grads]
    out = pl.pallas_call(
        functools.partial(tile_input_body, pitch, rows),
        out_shape=jax.ShapeDtypeStruct((rows * pitch, channels), BF),
        compiler_params=params(),
        cost_estimate=cost(),
        name="tile_input_grad",
    )(*flat, weight)
    return out.reshape(rows, pitch, channels)


def neighbours(array, axis, by):
    count = lax.axis_size(axis)
    return lax.ppermute(array, axis, [(i, i + by) for i in range(count) if 0 <= i + by < count])


def partner(array, bits_ty, bits_tx):
    down, across = lax.axis_size("ty"), lax.axis_size("tx")
    if bits_ty == 0:
        return lax.ppermute(array, "tx", [(i, i ^ bits_tx) for i in range(across)])
    if bits_tx == 0:
        return lax.ppermute(array, "ty", [(i, i ^ bits_ty) for i in range(down)])
    pairs = [
        (t * across + s, (t ^ bits_ty) * across + (s ^ bits_tx)) for t in range(down) for s in range(across)
    ]
    return lax.ppermute(array, ("ty", "tx"), pairs)


def sum_pairs(keep, send, layout):
    chips, highs, share = layout
    got = partner(send, 1, 0)
    return (keep + got.astype(F32)).reshape(keep.shape[0], chips * 2, highs * share, keep.shape[2])


def sum_chips(total, layout):
    chips, highs, share = layout
    arrived = [
        partner(total[:, 2 * a + b].astype(BF), 2 * a, b) for a in range(chips) for b in range(2) if a or b
    ]
    total = total[:, 0] + sum(got.astype(F32) for got in arrived)
    return total.reshape(total.shape[0], highs, share, total.shape[2])


def sum_rest(total, layout):
    chips, highs, share = layout
    arrived = [partner(total[:, k].astype(BF), 0, 2 * k) for k in range(1, highs)]
    return (total[:, 0] + sum(got.astype(F32) for got in arrived)).reshape(total.shape[0], -1)


def after(value, *earlier):
    return lax.optimization_barrier((value, earlier))[0]


def local(
    roi_feat,
    pre_one,
    grad_two,
    w_one,
    w_two,
    roi_rows,
    roi_cols,
    target_col,
    off_row,
    off_col,
    fpn_input,
    fpn_grad,
    w_fpn,
):
    regions, pool, channels = roi_feat.shape[0], roi_feat.shape[1], roi_feat.shape[3]
    tile_rows, tile_cols = fpn_input.shape[0], fpn_input.shape[1]
    extent = roi_rows.shape[1]
    down, across = lax.axis_size("ty"), lax.axis_size("tx")
    ty, tx = lax.axis_index("ty"), lax.axis_index("tx")
    capacity = max(2, (2 * regions + across - 1) // across)
    layout = (down // 2, across // 2, channels // (down * across))
    where = jnp.stack([ty, tx]).astype(jnp.int32)

    grad_one, sent = region_heads(
        grad_two, pre_one, w_two, w_one, roi_rows, roi_cols, target_col.reshape(-1), off_row, off_col, across, capacity
    )
    received = lax.all_to_all(sent, "tx", 0, 0, tiled=True)

    terms = head_weight_grads(where, layout, grad_two, pre_one, grad_one, roi_feat)
    heads = sum_pairs(*terms, layout)

    above = neighbours(fpn_input[tile_rows - 1 :], "ty", 1)
    below = neighbours(fpn_input[:extent], "ty", -1)
    tall = jnp.concatenate([above, fpn_input, below], axis=0)
    left = neighbours(tall[:, tile_cols - 1 :], "tx", 1)
    right = neighbours(tall[:, :extent], "tx", -1)
    taps = lay_out_input(tall, left, right)

    canvas, *terms = tile_gradient(
        where, layout, after(fpn_grad, heads), received, taps, extent, pool, down, across
    )
    heads = sum_chips(after(heads, canvas), layout)
    total = sum_pairs(*terms, layout)
    canvas = after(canvas, total)
    total = sum_chips(total, layout)
    head_fpn = sum_rest(total, layout)
    heads = sum_rest(after(heads, total), layout)

    spilled = neighbours(canvas[:, tile_cols - 1 : tile_cols + extent - 1].astype(BF), "tx", 1)
    first = neighbours(canvas[:, :1].astype(BF), "tx", -1)
    wide = jnp.pad(canvas[:, : tile_cols + 1], ((0, 0), (1, 0), (0, 0)))
    wide = wide + jnp.pad(spilled.astype(F32), ((0, 0), (0, tile_cols + 2 - extent), (0, 0)))
    wide = wide + jnp.pad(first.astype(F32), ((0, 0), (tile_cols + 1, 0), (0, 0)))
    spilled = neighbours(wide[tile_rows - 1 : tile_rows + extent - 1].astype(BF), "ty", 1)
    first = neighbours(wide[:1].astype(BF), "ty", -1)
    tall = jnp.pad(wide[: tile_rows + 1], ((1, 0), (0, 0), (0, 0)))
    tall = tall + jnp.pad(spilled.astype(F32), ((0, tile_rows + 2 - extent), (0, 0), (0, 0)))
    tall = (tall + jnp.pad(first.astype(F32), ((tile_rows + 1, 0), (0, 0), (0, 0)))).astype(BF)
    input_grad = tile_input_grad([tall[:, e : e + tile_cols] for e in range(3)], w_fpn)
    return (input_grad, heads[1], heads[0], head_fpn[0])


def solution(mesh):
    placed = (
        P(("ty", "tx"), None, None, None),
        P(("ty", "tx"), None, None, None),
        P(("ty", "tx"), None, None, None),
        P(),
        P(),
        P(("ty", "tx"), None, None),
        P(("ty", "tx"), None, None),
        P(("ty", "tx"), None),
        P(("ty", "tx")),
        P(("ty", "tx")),
        P("ty", "tx", None),
        P("ty", "tx", None),
        P(),
    )
    return jax.shard_map(
        local,
        mesh=mesh,
        in_specs=placed,
        out_specs=(P("ty", "tx", None), P(("ty", "tx")), P(("ty", "tx")), P(("ty", "tx"))),
        check_vma=False,
    )
```

time: 488 us -> 171 us (0.35); the launches traced: 480 us -> 170 us
  local copies, waits for them, and re-layouts: 165 us -> 8 us
  waiting for transfers between devices: 158 us -> 39.6 us
  matrix products: 88.2 us -> 0 us
  Pallas kernels: 0 us -> 56.7 us
  between operations: 14.7 us -> 0.98 us
  starting transfers between devices: 44.7 us -> 58.4 us
    unnamed x2 -> x0, waiting for transfers between devices: 145 us -> none
    dot_general x12 -> x0, matrix products: 88.2 us -> none  [the longest x1 29.1 us: place_windows(): jnp.einsum('sYy,syXc->YXc', row_hit, spread, preferred_element_type=jnp.f...]
    unnamed x89 -> x18, local copies, waits for them, and re-layouts: 68 us -> 0.78 us
    pallas_call x0 -> x5, Pallas kernels: none -> 56.7 us  [the longest x1 19.8 us: region_heads(): pl.pallas_call(functools.partial(head_body, (pool, pitch, regions, capaci...]
    reshape x9 -> x0, local copies, waits for them, and re-layouts: 48.6 us -> none  [the longest x1 16.8 us: local(): window_patches(jnp.pad(grad_two, region_pad), pool_size, pool_size, True)]
    concatenate x15 -> x1, local copies, waits for them, and re-layouts: 31.7 us -> 0.03 us  [local(): tall = jnp.concatenate([above, fpn_input, below], axis=0)]
    ppermute x10 -> x22, starting transfers between devices: 32.4 us -> 52 us  [the longest x8 26.1 us: neighbours(): lax.ppermute(array, axis, [(i, i + by) for i in range(count) if 0 <= i +...]
    ppermute x10 -> x22, waiting for transfers between devices: 12.8 us -> 32.2 us  [the longest x8 17.3 us: neighbours(): lax.ppermute(array, axis, [(i, i + by) for i in range(count) if 0 <= i +...]
  transfers between devices with their start and end apart: 13 -> 23, of which waited for: 5 -> 10; matrix products, arithmetic and copies ran while one was open for 42% -> 5% of each run, Pallas kernels for 0% -> 12%
where the time goes in v1:
time: 171 us; the launch traced here: 170 us
  starting transfers between devices  58.4 us (34%)
  Pallas kernels  56.7 us (33%)
  waiting for transfers between devices  39.6 us (23%)
  local copies, waits for them, and re-layouts  8 us (5%)
  other arithmetic  5.97 us (3%)
    ppermute x8, starting transfers between devices, neighbours(): lax.ppermute(array, axis, [(i, i + by) for i in range(count) if 0 <= i +...  26.1 us
    pallas_call x1, Pallas kernels, region_heads(): pl.pallas_call(functools.partial(head_body, (pool, pitch, regions, capaci...  19.8 us
    ppermute x8, waiting for transfers between devices, neighbours(): lax.ppermute(array, axis, [(i, i + by) for i in range(count) if 0 <= i +...  17.3 us
    pallas_call x1, Pallas kernels, head_weight_grads(): pl.pallas_call(functools.partial(head_weight_body, (regions, pool, pitch,...  15.6 us
    ppermute x8, starting transfers between devices, partner(): return lax.ppermute(array, 'tx', [(i, i ^ bits_tx) for i in range(across)])  15.4 us
    ppermute x8, waiting for transfers between devices, partner(): return lax.ppermute(array, 'tx', [(i, i ^ bits_tx) for i in range(across)])  14.9 us
    pallas_call x1, Pallas kernels, tile_gradient(): pl.pallas_call(functools.partial(tile_body, geometry), in_specs=[smem, vm...  12.6 us
    all_to_all x1, waiting for transfers between devices, local(): received = lax.all_to_all(sent, 'tx', 0, 0, tiled=True)  7.37 us
  transfers between devices with their start and end apart: 23, of which 10 were waited for; matrix products, arithmetic and copies ran while one was open for 5% of the time, Pallas kernels for 12%

profile of v1, /device:TPU:1, one launch (start us, length us, event | category | flops | bytes accessed | tf_op | source)
XLA Modules:
  0.0 169.7 jit_solution(3580733780141682568)
XLA Ops:
  0.6 19.8 %region_heads.1 = (bf16[2880,256]{1,0:T(8,128)(2,1)}, bf16[24,200,256]{2,1,0:T(8,128)(2,1)}) custom-call(s32[12]{0:T(128)} %bitcast.75, s32[12]{0:T(128)} %off_row.1, s32[12]{0:T(128)} %off_col.1, bf16[12,16,14]{2,1,0:T(8,128)(2,1)} %row_ref.1, bf16[12,16,14]{2,1,0:T(8,128)(2,1)} %col_ref.1, bf16[12,14,14,256]{3,2,1,0:T(8,128)(2,1)} %two_ref.1, ...), custom_call_target="tpu_custom_call" | custom-call | flops 13589544960 | bytes 1 | tf_op jit(solution)/shard_map/region_heads/pallas_call | solution.py:190
  20.5 6.4 %all-to-all-start = ((bf16[24,200,256]{2,1,0:T(8,128)(2,1)}), bf16[24,200,256]{2,1,0:T(8,128)(2,1)}, u32[]{:S(2)}, u32[]{:S(2)}) async-start(bf16[24,200,256]{2,1,0:T(8,128)(2,1)} %get-tuple-element.19), calls=%async_computation | async-start | bytes 4915200 | tf_op jit(solution)/shard_map/all_to_all | solution.py:559
  26.9 0.6 pad_add_fusion.where
  27.5 15.6 %head_weight_grads.1 = (f32[2,128,2304]{2,1,0:T(8,128)}, bf16[2,128,2304]{2,1,0:T(8,128)(2,1)}) custom-call(s32[2]{0:T(128)} %pad_add_fusion.where, bf16[12,14,14,256]{3,2,1,0:T(8,128)(2,1)} %two_ref.1, bf16[12,14,14,256]{3,2,1,0:T(8,128)(2,1)} %pre_ref.1, bf16[2880,256]{1,0:T(8,128)(2,1)} %get-tuple-element.15.one_hbm, bf16[12,14,14,256]{3,2,1,0:T(8,128)(2,1)} %feat_hbm.1), custom_call_target="tpu_custom_call" | custom-call | flops 1 | bytes 1 | tf_op jit(solution)/shard_map/head_weight_grads/pallas_call | solution.py:289
  43.1 1.0 collective-permute-start
  44.1 1.9 %collective-permute-start.2 = (bf16[16,64,256]{2,1,0:T(8,128)(2,1)S(1)}, bf16[16,64,256]{2,1,0:T(8,128)(2,1)S(1)}, u32[]{:S(2)}, u32[]{:S(2)}) collective-permute-start(bf16[16,64,256]{2,1,0:T(8,128)(2,1)S(1)} %copy-done.5), channel_id=1, source_target_pairs={{8,0},{16,8},{24,16},{9,1},{17,9},{25,17},{10,2},{18,10},{26,18},{... | collective-permute-start | bytes 1572872 | tf_op jit(solution)/shard_map/ppermute | solution.py:492
  46.0 3.6 %collective-permute-start.1 = (bf16[1,64,256]{2,1,0:T(8,128)(2,1)S(1)}, bf16[1,64,256]{2,1,0:T(8,128)(2,1)S(1)}, u32[]{:S(2)}, u32[]{:S(2)}) collective-permute-start(bf16[1,64,256]{2,1,0:T(8,128)(2,1)S(1)} %slice.108), channel_id=1, source_target_pairs={{0,8},{8,16},{16,24},{1,9},{9,17},{17,25},{2,10},{10,18},{18,26},{... | collective-permute-start | bytes 98312 | tf_op jit(solution)/shard_map/ppermute | solution.py:492
  49.7 1.0 collective-permute-done.1
  50.7 4.3 %collective-permute-done.2 = bf16[16,64,256]{2,1,0:T(8,128)(2,1)S(1)} collective-permute-done((bf16[16,64,256]{2,1,0:T(8,128)(2,1)S(1)}, bf16[16,64,256]{2,1,0:T(8,128)(2,1)S(1)}, u32[]{:S(2)}, u32[]{:S(2)}) %collective-permute-start.2) | collective-permute-done | bytes 524320 | tf_op jit(solution)/shard_map/ppermute | solution.py:492
  55.1 1.3 collective-permute-start.4
  56.4 4.0 %collective-permute-start.3 = (bf16[33,1,256]{2,1,0:T(2,128)(2,1)S(1)}, bf16[33,1,256]{2,1,0:T(2,128)(2,1)S(1)}, u32[]{:S(2)}, u32[]{:S(2)}) collective-permute-start(bf16[33,1,256]{2,1,0:T(2,128)(2,1)S(1)} %slice.138), channel_id=1, source_target_pairs={{0,1},{1,2},{2,3},{3,4},{4,5},{5,6},{6,7},{8,9},{9,10},{10,11},{11... | collective-permute-start | bytes 50696 | tf_op jit(solution)/shard_map/ppermute | solution.py:492
  60.4 2.9 %collective-permute-done.3.left_ref = bf16[33,1,256]{2,1,0:T(2,128)(2,1)S(1)} collective-permute-done((bf16[33,1,256]{2,1,0:T(2,128)(2,1)S(1)}, bf16[33,1,256]{2,1,0:T(2,128)(2,1)S(1)}, u32[]{:S(2)}, u32[]{:S(2)}) %collective-permute-start.3) | collective-permute-done | bytes 16928 | tf_op jit(solution)/shard_map/ppermute | solution.py:492
  63.3 5.8 %collective-permute-done.4.right_ref = bf16[33,16,256]{2,1,0:T(8,128)(2,1)S(1)} collective-permute-done((bf16[33,16,256]{2,1,0:T(8,128)(2,1)S(1)}, bf16[33,16,256]{2,1,0:T(8,128)(2,1)S(1)}, u32[]{:S(2)}, u32[]{:S(2)}) %collective-permute-start.4) | collective-permute-done | bytes 270368 | tf_op jit(solution)/shard_map/ppermute | solution.py:492
  69.1 0.7 copy-done.6
  69.8 4.7 %lay_out_input.1.taps_hbm = bf16[3,2720,256]{2,1,0:T(8,128)(2,1)} custom-call(bf16[33,64,256]{2,1,0:T(8,128)(2,1)} %copy-done.3, bf16[33,1,256]{2,1,0:T(2,128)(2,1)} %copy-done.7, bf16[33,16,256]{2,1,0:T(8,128)(2,1)} %copy-done.6), custom_call_target="tpu_custom_call" | custom-call | flops 1 | bytes 1 | tf_op jit(solution)/shard_map/lay_out_input/pallas_call | solution.py:333
  74.5 0.0 collective-permute-done
  74.5 0.2 convert_add_fusion.1
  74.7 7.4 %all-to-all-done.received = bf16[24,200,256]{2,1,0:T(8,128)(2,1)} async-done(((bf16[24,200,256]{2,1,0:T(8,128)(2,1)}), bf16[24,200,256]{2,1,0:T(8,128)(2,1)}, u32[]{:S(2)}, u32[]{:S(2)}) %all-to-all-start) | async-done | bytes 2457632 | tf_op jit(solution)/shard_map/all_to_all | solution.py:559
  82.1 12.6 %tile_gradient.1 = (f32[32,80,256]{2,1,0:T(8,128)}, f32[1,128,2304]{2,1,0:T(8,128)}, bf16[1,128,2304]{2,1,0:T(8,128)(2,1)}) custom-call(s32[2]{0:T(128)} %pad_add_fusion.where, bf16[16,64,256]{2,1,0:T(8,128)(2,1)} %start_ref, bf16[24,200,256]{2,1,0:T(8,128)(2,1)} %all-to-all-done.received, bf16[3,2720,256]{2,1,0:T(8,128)(2,1)} %lay_out_input.1.taps_hbm), custom_call_target="tpu_custom_call" | custom-call | flops 6039797760 | bytes 1 | tf_op jit(solution)/shard_map/tile_gradient/pallas_call | solution.py:431
  94.7 3.3 %collective-permute-start.5 = (bf16[1,128,2304]{2,1,0:T(8,128)(2,1)}, bf16[1,128,2304]{2,1,0:T(8,128)(2,1)S(1)}, u32[]{:S(2)}, u32[]{:S(2)}) collective-permute-start(bf16[1,128,2304]{2,1,0:T(8,128)(2,1)} %get-tuple-element.22), channel_id=1, source_target_pairs={{0,8},{8,0},{16,24},{24,16},{1,9},{9,1},{17,25},{25,17},{2,10},{10... | collective-permute-start | bytes 1769480 | tf_op jit(solution)/shard_map/ppermute | solution.py:500
  98.0 0.1 convert.38
  98.1 0.1 slice_bitcast_fusion.4
  98.2 0.1 collective-permute-start.10
  98.3 2.4 %collective-permute-start.12 = (bf16[2,32,2304]{2,1,0:T(8,128)(2,1)S(1)}, bf16[2,32,2304]{2,1,0:T(8,128)(2,1)S(1)}, u32[]{:S(2)}, u32[]{:S(2)}) collective-permute-start(bf16[2,32,2304]{2,1,0:T(8,128)(2,1)S(1)} %get-tuple-element.31), channel_id=1, source_target_pairs={{0,17},{1,16},{2,19},{3,18},{4,21},{5,20},{6,23},{7,22},{8,25},{9,... | collective-permute-start | bytes 884744 | tf_op jit(solution)/shard_map/ppermute | solution.py:504
  100.6 0.3 collective-permute-start.11
  100.9 0.0 collective-permute-done.5
  100.9 0.1 convert_add_fusion.2
  101.0 0.1 convert.39
  101.1 0.1 collective-permute-start.13
  101.3 2.3 %collective-permute-start.15 = (bf16[1,32,2304]{2,1,0:T(8,128)(2,1)S(1)}, bf16[1,32,2304]{2,1,0:T(8,128)(2,1)S(1)}, u32[]{:S(2)}, u32[]{:S(2)}) collective-permute-start(bf16[1,32,2304]{2,1,0:T(8,128)(2,1)S(1)} %get-tuple-element.37), channel_id=1, source_target_pairs={{0,17},{1,16},{2,19},{3,18},{4,21},{5,20},{6,23},{7,22},{8,25},{9,... | collective-permute-start | bytes 442376 | tf_op jit(solution)/shard_map/ppermute | solution.py:504
  103.6 9.6 %collective-permute-done.10 = bf16[2,32,2304]{2,1,0:T(8,128)(2,1)S(1)} collective-permute-done((bf16[2,32,2304]{2,1,0:T(8,128)(2,1)S(1)}, bf16[2,32,2304]{2,1,0:T(8,128)(2,1)S(1)}, u32[]{:S(2)}, u32[]{:S(2)}) %collective-permute-start.10) | collective-permute-done | bytes 294944 | tf_op jit(solution)/shard_map/ppermute | solution.py:498
  113.2 1.2 collective-permute-start.14
  114.4 0.0 collective-permute-done.12
  114.4 0.1 fusion.1
  114.6 0.1 convert.36
  114.7 0.2 slice.111
  114.9 0.6 slice.141
  115.5 0.1 slice.140
  115.6 1.3 collective-permute-start.7
  116.9 4.0 %collective-permute-start.6 = (bf16[32,16,256]{2,1,0:T(8,128)(2,1)S(1)}, bf16[32,16,256]{2,1,0:T(8,128)(2,1)S(1)}, u32[]{:S(2)}, u32[]{:S(2)}) collective-permute-start(bf16[32,16,256]{2,1,0:T(8,128)(2,1)S(1)} %slice.140), channel_id=1, source_target_pairs={{0,1},{1,2},{2,3},{3,4},{4,5},{5,6},{6,7},{8,9},{9,10},{10,11},{11... | collective-permute-start | bytes 786440 | tf_op jit(solution)/shard_map/ppermute | solution.py:492
  121.0 0.1 fusion.6
  121.1 8.5 %collective-permute-start.19 = (bf16[1,8,2304]{2,1,0:T(8,128)(2,1)S(1)}, bf16[1,8,2304]{2,1,0:T(8,128)(2,1)S(1)}, u32[]{:S(2)}, u32[]{:S(2)}) collective-permute-start(bf16[1,8,2304]{2,1,0:T(8,128)(2,1)S(1)} %get-tuple-element.42), channel_id=1, source_target_pairs={{0,2},{1,3},{2,0},{3,1},{4,6},{5,7},{6,4},{7,5},{8,10},{9,11},{10,... | collective-permute-start | bytes 110600 | tf_op jit(solution)/shard_map/ppermute | solution.py:498
  129.6 3.6 %collective-permute-start.21 = (bf16[1,8,2304]{2,1,0:T(8,128)(2,1)S(1)}, bf16[1,8,2304]{2,1,0:T(8,128)(2,1)S(1)}, u32[]{:S(2)}, u32[]{:S(2)}) collective-permute-start(bf16[1,8,2304]{2,1,0:T(8,128)(2,1)S(1)} %get-tuple-element.43), channel_id=1, source_target_pairs={{0,6},{1,7},{2,4},{3,5},{4,2},{5,3},{6,0},{7,1},{8,14},{9,15},{10,... | collective-permute-start | bytes 110600 | tf_op jit(solution)/shard_map/ppermute | solution.py:498
  133.2 0.7 slice_bitcast_fusion.12
  133.9 0.3 collective-permute-start.16
  134.1 0.7 collective-permute-done.21
  134.9 2.9 %collective-permute-start.18 = (bf16[2,8,2304]{2,1,0:T(8,128)(2,1)}, bf16[2,8,2304]{2,1,0:T(8,128)(2,1)}, u32[]{:S(2)}, u32[]{:S(2)}) collective-permute-start(bf16[2,8,2304]{2,1,0:T(8,128)(2,1)} %get-tuple-element.40), channel_id=1, source_target_pairs={{0,6},{1,7},{2,4},{3,5},{4,2},{5,3},{6,0},{7,1},{8,14},{9,15},{10,... | collective-permute-start | bytes 221192 | tf_op jit(solution)/shard_map/ppermute | solution.py:498
  137.8 0.6 squeeze_reshape.3
  138.4 2.0 %collective-permute-done.18 = bf16[2,8,2304]{2,1,0:T(8,128)(2,1)} collective-permute-done((bf16[2,8,2304]{2,1,0:T(8,128)(2,1)}, bf16[2,8,2304]{2,1,0:T(8,128)(2,1)}, u32[]{:S(2)}, u32[]{:S(2)}) %collective-permute-start.18) | collective-permute-done | bytes 73760 | tf_op jit(solution)/shard_map/ppermute | solution.py:498
  140.4 2.6 %collective-permute-done.17 = bf16[2,8,2304]{2,1,0:T(8,128)(2,1)} collective-permute-done((bf16[2,8,2304]{2,1,0:T(8,128)(2,1)}, bf16[2,8,2304]{2,1,0:T(8,128)(2,1)}, u32[]{:S(2)}, u32[]{:S(2)}) %collective-permute-start.17) | collective-permute-done | bytes 73760 | tf_op jit(solution)/shard_map/ppermute | solution.py:498
  142.9 1.0 fusion.4
  144.0 2.5 %fusion.8 = (bf16[32,66,256]{2,1,0:T(8,128)(2,1)S(1)}, f32[32,66,256]{2,1,0:T(8,128)}) fusion(bf16[32,1,256]{2,1,0:T(2,128)(2,1)} %collective-permute-done.7, bf16[32,16,256]{2,1,0:T(8,128)(2,1)S(1)} %collective-permute-done.6, f32[32,65,256]{2,1,0:T(8,128)S(1)} %slice.111), kind=kLoop, calls=%fused_computation.31 | loop fusion | flops 2703360 | bytes 5652480 | tf_op jit(solution)/shard_map/convert.21
  146.5 0.1 copy.23
  146.6 6.7 %collective-permute-start.9 = (bf16[1,66,256]{2,1,0:T(8,128)(2,1)S(1)}, bf16[1,66,256]{2,1,0:T(8,128)(2,1)}, u32[]{:S(2)}, u32[]{:S(2)}) collective-permute-start(bf16[1,66,256]{2,1,0:T(8,128)(2,1)S(1)} %slice.144), channel_id=1, source_target_pairs={{8,0},{16,8},{24,16},{9,1},{17,9},{25,17},{10,2},{18,10},{26,18},{... | collective-permute-start | bytes 101384 | tf_op jit(solution)/shard_map/ppermute | solution.py:492
  153.4 3.2 %collective-permute-start.8 = (bf16[16,66,256]{2,0,1:T(8,128)(2,1)S(1)}, bf16[16,66,256]{2,0,1:T(8,128)(2,1)S(1)}, u32[]{:S(2)}, u32[]{:S(2)}) collective-permute-start(bf16[16,66,256]{2,0,1:T(8,128)(2,1)S(1)} %copy.23), channel_id=1, source_target_pairs={{0,8},{8,16},{16,24},{1,9},{9,17},{17,25},{2,10},{10,18},{18,26},{... | collective-permute-start | bytes 1622024 | tf_op jit(solution)/shard_map/ppermute | solution.py:492
  156.6 0.6 fusion.10
  157.3 1.5 squeeze.16
  158.8 0.6 squeeze.15
  159.5 0.1 slice.142
  159.5 3.4 %collective-permute-done.8 = bf16[16,66,256]{2,0,1:T(8,128)(2,1)S(1)} collective-permute-done((bf16[16,66,256]{2,0,1:T(8,128)(2,1)S(1)}, bf16[16,66,256]{2,0,1:T(8,128)(2,1)S(1)}, u32[]{:S(2)}, u32[]{:S(2)}) %collective-permute-start.8) | collective-permute-done | bytes 540704 | tf_op jit(solution)/shard_map/ppermute | solution.py:492
  162.9 0.2 copy.24
  163.1 1.0 add_convert_fusion
  164.1 1.6 fusion.9
  165.7 4.0 %tile_input_grad.1 = bf16[1024,256]{1,0:T(8,128)(2,1)} custom-call(bf16[1152,256]{1,0:T(8,128)(2,1)} %bitcast.73, bf16[1152,256]{1,0:T(8,128)(2,1)} %bitcast.72, bf16[1152,256]{1,0:T(8,128)(2,1)} %bitcast.71, bf16[3,3,256,256]{3,2,1,0:T(8,128)(2,1)} %weight.1), custom_call_target="tpu_custom_call" | custom-call | flops 1 | bytes 1 | tf_op jit(solution)/shard_map/tile_input_grad/pallas_call | solution.py:480
  (39 shorter events, 0.3 us)
Async XLA Ops:
  20.5 61.6 %all-to-all-start = ((bf16[24,200,256]{2,1,0:T(8,128)(2,1)}), bf16[24,200,256]{2,1,0:T(8,128)(2,1)}, u32[]{:S(2)}, u32[]{:S(2)}) async-start(bf16[24,200,256]{2,1,0:T(8,128)(2,1)} %get-tuple-element.19), calls=%async_computation | async-start | bytes 4915200 | tf_op jit(solution)/shard_map/all_to_all | solution.py:559
  27.5 16.6 %copy-start.5 = (bf16[16,64,256]{2,1,0:T(8,128)(2,1)S(1)}, bf16[16,64,256]{2,1,0:T(8,128)(2,1)}, u32[]{:S(2)}) copy-start(bf16[16,64,256]{2,1,0:T(8,128)(2,1)} %param.23) | copy-start | bytes 1572868
  43.1 31.4 %collective-permute-start = (bf16[2,128,2304]{2,1,0:T(8,128)(2,1)}, bf16[2,128,2304]{2,1,0:T(8,128)(2,1)S(1)}, u32[]{:S(2)}, u32[]{:S(2)}) collective-permute-start(bf16[2,128,2304]{2,1,0:T(8,128)(2,1)} %get-tuple-element.17), channel_id=1, source_target_pairs={{0,8},{8,0},{16,24},{24,16},{1,9},{9,1},{17,25},{25,17},{2,10},{10... | collective-permute-start | bytes 3538952 | tf_op jit(solution)/shard_map/ppermute | solution.py:500
  44.1 10.9 %collective-permute-start.2 = (bf16[16,64,256]{2,1,0:T(8,128)(2,1)S(1)}, bf16[16,64,256]{2,1,0:T(8,128)(2,1)S(1)}, u32[]{:S(2)}, u32[]{:S(2)}) collective-permute-start(bf16[16,64,256]{2,1,0:T(8,128)(2,1)S(1)} %copy-done.5), channel_id=1, source_target_pairs={{8,0},{16,8},{24,16},{9,1},{17,9},{25,17},{10,2},{18,10},{26,18},{... | collective-permute-start | bytes 1572872 | tf_op jit(solution)/shard_map/ppermute | solution.py:492
  46.0 4.6 %collective-permute-start.1 = (bf16[1,64,256]{2,1,0:T(8,128)(2,1)S(1)}, bf16[1,64,256]{2,1,0:T(8,128)(2,1)S(1)}, u32[]{:S(2)}, u32[]{:S(2)}) collective-permute-start(bf16[1,64,256]{2,1,0:T(8,128)(2,1)S(1)} %slice.108), channel_id=1, source_target_pairs={{0,8},{8,16},{16,24},{1,9},{9,17},{17,25},{2,10},{10,18},{18,26},{... | collective-permute-start | bytes 98312 | tf_op jit(solution)/shard_map/ppermute | solution.py:492
  55.0 14.1 %copy-start.3 = (bf16[33,64,256]{2,1,0:T(8,128)(2,1)}, bf16[33,64,256]{2,1,0:T(8,128)(2,1)S(1)}, u32[]{:S(2)}) copy-start(bf16[33,64,256]{2,1,0:T(8,128)(2,1)S(1)} %constant_dynamic-update-slice_fusion.own_ref) | copy-start | bytes 3244036
  55.1 14.0 %collective-permute-start.4 = (bf16[33,16,256]{2,1,0:T(8,128)(2,1)S(1)}, bf16[33,16,256]{2,1,0:T(8,128)(2,1)S(1)}, u32[]{:S(2)}, u32[]{:S(2)}) collective-permute-start(bf16[33,16,256]{2,1,0:T(8,128)(2,1)S(1)} %slice.139), channel_id=1, source_target_pairs={{1,0},{2,1},{3,2},{4,3},{5,4},{6,5},{7,6},{9,8},{10,9},{11,10},{12... | collective-permute-start | bytes 811016 | tf_op jit(solution)/shard_map/ppermute | solution.py:492
  56.4 6.8 %collective-permute-start.3 = (bf16[33,1,256]{2,1,0:T(2,128)(2,1)S(1)}, bf16[33,1,256]{2,1,0:T(2,128)(2,1)S(1)}, u32[]{:S(2)}, u32[]{:S(2)}) collective-permute-start(bf16[33,1,256]{2,1,0:T(2,128)(2,1)S(1)} %slice.138), channel_id=1, source_target_pairs={{0,1},{1,2},{2,3},{3,4},{4,5},{5,6},{6,7},{8,9},{9,10},{10,11},{11... | collective-permute-start | bytes 50696 | tf_op jit(solution)/shard_map/ppermute | solution.py:492
  63.3 5.8 %copy-start.7 = (bf16[33,1,256]{2,1,0:T(2,128)(2,1)}, bf16[33,1,256]{2,1,0:T(2,128)(2,1)S(1)}, u32[]{:S(2)}) copy-start(bf16[33,1,256]{2,1,0:T(2,128)(2,1)S(1)} %collective-permute-done.3.left_ref) | copy-start | bytes 50692
  69.1 0.7 copy-start.6
  69.8 4.7 %copy-start.2 = (f32[2,128,2304]{2,1,0:T(8,128)S(1)}, f32[2,128,2304]{2,1,0:T(8,128)}, u32[]{:S(2)}) copy-start(f32[2,128,2304]{2,1,0:T(8,128)} %get-tuple-element.16) | copy-start | bytes 7077892
  94.7 6.2 %collective-permute-start.5 = (bf16[1,128,2304]{2,1,0:T(8,128)(2,1)}, bf16[1,128,2304]{2,1,0:T(8,128)(2,1)S(1)}, u32[]{:S(2)}, u32[]{:S(2)}) collective-permute-start(bf16[1,128,2304]{2,1,0:T(8,128)(2,1)} %get-tuple-element.22), channel_id=1, source_target_pairs={{0,8},{8,0},{16,24},{24,16},{1,9},{9,1},{17,25},{25,17},{2,10},{10... | collective-permute-start | bytes 1769480 | tf_op jit(solution)/shard_map/ppermute | solution.py:500
  98.1 2.8 %copy-start.4 = (f32[1,128,2304]{2,1,0:T(8,128)S(1)}, f32[1,128,2304]{2,1,0:T(8,128)}, u32[]{:S(2)}) copy-start(f32[1,128,2304]{2,1,0:T(8,128)} %get-tuple-element.21) | copy-start | bytes 3538948
  98.2 15.0 %collective-permute-start.10 = (bf16[2,32,2304]{2,1,0:T(8,128)(2,1)S(1)}, bf16[2,32,2304]{2,1,0:T(8,128)(2,1)S(1)}, u32[]{:S(2)}, u32[]{:S(2)}) collective-permute-start(bf16[2,32,2304]{2,1,0:T(8,128)(2,1)S(1)} %get-tuple-element.30), channel_id=1, source_target_pairs={{0,1},{1,0},{2,3},{3,2},{4,5},{5,4},{6,7},{7,6},{8,9},{9,8},{10,11... | collective-permute-start | bytes 884744 | tf_op jit(solution)/shard_map/ppermute | solution.py:498
  98.3 16.1 %collective-permute-start.12 = (bf16[2,32,2304]{2,1,0:T(8,128)(2,1)S(1)}, bf16[2,32,2304]{2,1,0:T(8,128)(2,1)S(1)}, u32[]{:S(2)}, u32[]{:S(2)}) collective-permute-start(bf16[2,32,2304]{2,1,0:T(8,128)(2,1)S(1)} %get-tuple-element.31), channel_id=1, source_target_pairs={{0,17},{1,16},{2,19},{3,18},{4,21},{5,20},{6,23},{7,22},{8,25},{9,... | collective-permute-start | bytes 884744 | tf_op jit(solution)/shard_map/ppermute | solution.py:504
  100.6 13.8 %collective-permute-start.11 = (bf16[2,32,2304]{2,1,0:T(8,128)(2,1)S(1)}, bf16[2,32,2304]{2,1,0:T(8,128)(2,1)S(1)}, u32[]{:S(2)}, u32[]{:S(2)}) collective-permute-start(bf16[2,32,2304]{2,1,0:T(8,128)(2,1)S(1)} %get-tuple-element.32), channel_id=1, source_target_pairs={{0,16},{8,24},{16,0},{24,8},{1,17},{9,25},{17,1},{25,9},{2,18},{10... | collective-permute-start | bytes 884744 | tf_op jit(solution)/shard_map/ppermute | solution.py:500
  101.1 13.5 %copy-start = (f32[32,80,256]{2,1,0:T(8,128)S(1)}, f32[32,80,256]{2,1,0:T(8,128)}, u32[]{:S(2)}) copy-start(f32[32,80,256]{2,1,0:T(8,128)} %get-tuple-element.23) | copy-start | bytes 7864324
  101.1 19.8 %collective-permute-start.13 = (bf16[1,32,2304]{2,1,0:T(8,128)(2,1)S(1)}, bf16[1,32,2304]{2,1,0:T(8,128)(2,1)S(1)}, u32[]{:S(2)}, u32[]{:S(2)}) collective-permute-start(bf16[1,32,2304]{2,1,0:T(8,128)(2,1)S(1)} %get-tuple-element.36), channel_id=1, source_target_pairs={{0,1},{1,0},{2,3},{3,2},{4,5},{5,4},{6,7},{7,6},{8,9},{9,8},{10,11... | collective-permute-start | bytes 442376 | tf_op jit(solution)/shard_map/ppermute | solution.py:498
  101.3 19.7 %collective-permute-start.15 = (bf16[1,32,2304]{2,1,0:T(8,128)(2,1)S(1)}, bf16[1,32,2304]{2,1,0:T(8,128)(2,1)S(1)}, u32[]{:S(2)}, u32[]{:S(2)}) collective-permute-start(bf16[1,32,2304]{2,1,0:T(8,128)(2,1)S(1)} %get-tuple-element.37), channel_id=1, source_target_pairs={{0,17},{1,16},{2,19},{3,18},{4,21},{5,20},{6,23},{7,22},{8,25},{9,... | collective-permute-start | bytes 442376 | tf_op jit(solution)/shard_map/ppermute | solution.py:504
  113.2 7.8 %collective-permute-start.14 = (bf16[1,32,2304]{2,1,0:T(8,128)(2,1)S(1)}, bf16[1,32,2304]{2,1,0:T(8,128)(2,1)S(1)}, u32[]{:S(2)}, u32[]{:S(2)}) collective-permute-start(bf16[1,32,2304]{2,1,0:T(8,128)(2,1)S(1)} %get-tuple-element.38), channel_id=1, source_target_pairs={{0,16},{8,24},{16,0},{24,8},{1,17},{9,25},{17,1},{25,9},{2,18},{10... | collective-permute-start | bytes 442376 | tf_op jit(solution)/shard_map/ppermute | solution.py:500
  115.6 28.3 %collective-permute-start.7 = (bf16[32,1,256]{2,1,0:T(2,128)(2,1)}, bf16[32,1,256]{2,1,0:T(2,128)(2,1)}, u32[]{:S(2)}, u32[]{:S(2)}) collective-permute-start(bf16[32,1,256]{2,1,0:T(2,128)(2,1)} %slice.141), channel_id=1, source_target_pairs={{1,0},{2,1},{3,2},{4,3},{5,4},{6,5},{7,6},{9,8},{10,9},{11,10},{12... | collective-permute-start | bytes 49160 | tf_op jit(solution)/shard_map/ppermute | solution.py:492
  116.9 27.0 %collective-permute-start.6 = (bf16[32,16,256]{2,1,0:T(8,128)(2,1)S(1)}, bf16[32,16,256]{2,1,0:T(8,128)(2,1)S(1)}, u32[]{:S(2)}, u32[]{:S(2)}) collective-permute-start(bf16[32,16,256]{2,1,0:T(8,128)(2,1)S(1)} %slice.140), channel_id=1, source_target_pairs={{0,1},{1,2},{2,3},{3,4},{4,5},{5,6},{6,7},{8,9},{9,10},{10,11},{11... | collective-permute-start | bytes 786440 | tf_op jit(solution)/shard_map/ppermute | solution.py:492
  121.1 12.8 %collective-permute-start.19 = (bf16[1,8,2304]{2,1,0:T(8,128)(2,1)S(1)}, bf16[1,8,2304]{2,1,0:T(8,128)(2,1)S(1)}, u32[]{:S(2)}, u32[]{:S(2)}) collective-permute-start(bf16[1,8,2304]{2,1,0:T(8,128)(2,1)S(1)} %get-tuple-element.42), channel_id=1, source_target_pairs={{0,2},{1,3},{2,0},{3,1},{4,6},{5,7},{6,4},{7,5},{8,10},{9,11},{10,... | collective-permute-start | bytes 110600 | tf_op jit(solution)/shard_map/ppermute | solution.py:498
  129.6 5.3 %collective-permute-start.21 = (bf16[1,8,2304]{2,1,0:T(8,128)(2,1)S(1)}, bf16[1,8,2304]{2,1,0:T(8,128)(2,1)S(1)}, u32[]{:S(2)}, u32[]{:S(2)}) collective-permute-start(bf16[1,8,2304]{2,1,0:T(8,128)(2,1)S(1)} %get-tuple-element.43), channel_id=1, source_target_pairs={{0,6},{1,7},{2,4},{3,5},{4,2},{5,3},{6,0},{7,1},{8,14},{9,15},{10,... | collective-permute-start | bytes 110600 | tf_op jit(solution)/shard_map/ppermute | solution.py:498
  133.1 4.6 %collective-permute-start.20 = (bf16[1,8,2304]{2,1,0:T(8,128)(2,1)S(1)}, bf16[1,8,2304]{2,1,0:T(8,128)(2,1)S(1)}, u32[]{:S(2)}, u32[]{:S(2)}) collective-permute-start(bf16[1,8,2304]{2,1,0:T(8,128)(2,1)S(1)} %get-tuple-element.44), channel_id=1, source_target_pairs={{0,4},{1,5},{2,6},{3,7},{4,0},{5,1},{6,2},{7,3},{8,12},{9,13},{10,... | collective-permute-start | bytes 110600 | tf_op jit(solution)/shard_map/ppermute | solution.py:498
  133.9 4.6 %collective-permute-start.16 = (bf16[2,8,2304]{2,1,0:T(8,128)(2,1)}, bf16[2,8,2304]{2,1,0:T(8,128)(2,1)}, u32[]{:S(2)}, u32[]{:S(2)}) collective-permute-start(bf16[2,8,2304]{2,1,0:T(8,128)(2,1)} %get-tuple-element.39), channel_id=1, source_target_pairs={{0,2},{1,3},{2,0},{3,1},{4,6},{5,7},{6,4},{7,5},{8,10},{9,11},{10,... | collective-permute-start | bytes 221192 | tf_op jit(solution)/shard_map/ppermute | solution.py:498
  134.9 5.5 %collective-permute-start.18 = (bf16[2,8,2304]{2,1,0:T(8,128)(2,1)}, bf16[2,8,2304]{2,1,0:T(8,128)(2,1)}, u32[]{:S(2)}, u32[]{:S(2)}) collective-permute-start(bf16[2,8,2304]{2,1,0:T(8,128)(2,1)} %get-tuple-element.40), channel_id=1, source_target_pairs={{0,6},{1,7},{2,4},{3,5},{4,2},{5,3},{6,0},{7,1},{8,14},{9,15},{10,... | collective-permute-start | bytes 221192 | tf_op jit(solution)/shard_map/ppermute | solution.py:498
  137.7 5.2 %collective-permute-start.17 = (bf16[2,8,2304]{2,1,0:T(8,128)(2,1)}, bf16[2,8,2304]{2,1,0:T(8,128)(2,1)}, u32[]{:S(2)}, u32[]{:S(2)}) collective-permute-start(bf16[2,8,2304]{2,1,0:T(8,128)(2,1)} %get-tuple-element.41), channel_id=1, source_target_pairs={{0,4},{1,5},{2,6},{3,7},{4,0},{5,1},{6,2},{7,3},{8,12},{9,13},{10,... | collective-permute-start | bytes 221192 | tf_op jit(solution)/shard_map/ppermute | solution.py:498
  146.5 13.0 %copy-start.1 = (f32[32,66,256]{2,1,0:T(8,128)S(1)}, f32[32,66,256]{2,1,0:T(8,128)}, u32[]{:S(2)}) copy-start(f32[32,66,256]{2,1,0:T(8,128)} %get-tuple-element.29) | copy-start | bytes 6488068
  146.6 16.5 %collective-permute-start.9 = (bf16[1,66,256]{2,1,0:T(8,128)(2,1)S(1)}, bf16[1,66,256]{2,1,0:T(8,128)(2,1)}, u32[]{:S(2)}, u32[]{:S(2)}) collective-permute-start(bf16[1,66,256]{2,1,0:T(8,128)(2,1)S(1)} %slice.144), channel_id=1, source_target_pairs={{8,0},{16,8},{24,16},{9,1},{17,9},{25,17},{10,2},{18,10},{26,18},{... | collective-permute-start | bytes 101384 | tf_op jit(solution)/shard_map/ppermute | solution.py:492
  153.4 9.5 %collective-permute-start.8 = (bf16[16,66,256]{2,0,1:T(8,128)(2,1)S(1)}, bf16[16,66,256]{2,0,1:T(8,128)(2,1)S(1)}, u32[]{:S(2)}, u32[]{:S(2)}) collective-permute-start(bf16[16,66,256]{2,0,1:T(8,128)(2,1)S(1)} %copy.23), channel_id=1, source_target_pairs={{0,8},{8,16},{16,24},{1,9},{9,17},{17,25},{2,10},{10,18},{18,26},{... | collective-permute-start | bytes 1622024 | tf_op jit(solution)/shard_map/ppermute | solution.py:492

commit v2 on v1

--- a/solution.py
+++ b/solution.py
@@ -568,21 +568,21 @@
     right = neighbours(tall[:, :extent], "tx", -1)
     taps = lay_out_input(tall, left, right)
 
+    heads = sum_chips(heads, layout)
     canvas, *terms = tile_gradient(
         where, layout, after(fpn_grad, heads), received, taps, extent, pool, down, across
     )
-    heads = sum_chips(after(heads, canvas), layout)
     total = sum_pairs(*terms, layout)
     canvas = after(canvas, total)
     total = sum_chips(total, layout)
-    head_fpn = sum_rest(total, layout)
-    heads = sum_rest(after(heads, total), layout)
 
     spilled = neighbours(canvas[:, tile_cols - 1 : tile_cols + extent - 1].astype(BF), "tx", 1)
     first = neighbours(canvas[:, :1].astype(BF), "tx", -1)
     wide = jnp.pad(canvas[:, : tile_cols + 1], ((0, 0), (1, 0), (0, 0)))
     wide = wide + jnp.pad(spilled.astype(F32), ((0, 0), (0, tile_cols + 2 - extent), (0, 0)))
     wide = wide + jnp.pad(first.astype(F32), ((0, 0), (tile_cols + 1, 0), (0, 0)))
+    head_fpn = sum_rest(after(total, wide), layout)
+    heads = sum_rest(after(heads, wide), layout)
     spilled = neighbours(wide[tile_rows - 1 : tile_rows + extent - 1].astype(BF), "ty", 1)
     first = neighbours(wide[:1].astype(BF), "ty", -1)
     tall = jnp.pad(wide[: tile_rows + 1], ((1, 0), (0, 0), (0, 0)))

time: 171 us -> 152 us (0.89)
  waiting for transfers between devices: 39.6 us -> 32 us
  starting transfers between devices: 58.4 us -> 53.1 us
  local copies, waits for them, and re-layouts: 8 us -> 5.14 us
  Pallas kernels: 56.7 us -> 54.9 us
    ppermute x8, waiting for transfers between devices: 14.9 us -> 0.02 us  [partner(): return lax.ppermute(array, 'tx', [(i, i ^ bits_tx) for i in range(across)])]
    ppermute x8, waiting for transfers between devices: 17.3 us -> 27.8 us  [neighbours(): lax.ppermute(array, axis, [(i, i + by) for i in range(count) if 0 <= i +...]
    all_to_all x1, waiting for transfers between devices: 7.37 us -> 0.01 us  [local(): received = lax.all_to_all(sent, 'tx', 0, 0, tiled=True)]
    ppermute x8, starting transfers between devices: 15.4 us -> 20.5 us  [partner(): return lax.ppermute(array, 'tx', [(i, i ^ bits_tx) for i in range(across)])]
    ppermute x4, starting transfers between devices: 5.79 us -> 1.7 us  [partner(): return lax.ppermute(array, 'ty', [(i, i ^ bits_ty) for i in range(down)])]
    ppermute x8, starting transfers between devices: 26.1 us -> 22.6 us  [neighbours(): lax.ppermute(array, axis, [(i, i + by) for i in range(count) if 0 <= i +...]
    add x2, other arithmetic: 0.32 us -> 3.3 us  [sum_pairs(): keep + got.astype(F32)]
    ppermute x2, starting transfers between devices: 4.69 us -> 1.92 us  [partner(): return lax.ppermute(array, ('ty', 'tx'), pairs)]
  transfers between devices with their start and end apart: 23 -> 23, of which waited for: 10 -> 8; matrix products, arithmetic and copies ran while one was open for 5% -> 4% of each run, Pallas kernels for 12% -> 13%
where the time goes in v2:
time: 152 us; the launch traced here: 151 us
  Pallas kernels  54.9 us (36%)
  starting transfers between devices  53.1 us (35%)
  waiting for transfers between devices  32 us (21%)
  local copies, waits for them, and re-layouts  5.14 us (3%)
  other arithmetic  5.03 us (3%)
    ppermute x8, waiting for transfers between devices, neighbours(): lax.ppermute(array, axis, [(i, i + by) for i in range(count) if 0 <= i +...  27.8 us
    ppermute x8, starting transfers between devices, neighbours(): lax.ppermute(array, axis, [(i, i + by) for i in range(count) if 0 <= i +...  22.6 us
    ppermute x8, starting transfers between devices, partner(): return lax.ppermute(array, 'tx', [(i, i ^ bits_tx) for i in range(across)])  20.5 us
    pallas_call x1, Pallas kernels, region_heads(): pl.pallas_call(functools.partial(head_body, (pool, pitch, regions, capaci...  19.8 us
    pallas_call x1, Pallas kernels, head_weight_grads(): pl.pallas_call(functools.partial(head_weight_body, (regions, pool, pitch,...  15.6 us
    pallas_call x1, Pallas kernels, tile_gradient(): pl.pallas_call(functools.partial(tile_body, geometry), in_specs=[smem, vm...  11 us
    all_to_all x1, starting transfers between devices, local(): received = lax.all_to_all(sent, 'tx', 0, 0, tiled=True)  6.4 us
    pallas_call x1, Pallas kernels, lay_out_input(): pl.pallas_call(functools.partial(lay_body, (rows, pitch, tile_cols)), in_...  4.48 us
  transfers between devices with their start and end apart: 23, of which 8 were waited for; matrix products, arithmetic and copies ran while one was open for 4% of the time, Pallas kernels for 13%

profile of v2, /device:TPU:1, one launch (start us, length us, event | category | flops | bytes accessed | tf_op | source)
XLA Modules:
  0.0 151.2 jit_solution(7728118854338358035)
XLA Ops:
  0.6 19.8 %region_heads.1 = (bf16[2880,256]{1,0:T(8,128)(2,1)}, bf16[24,200,256]{2,1,0:T(8,128)(2,1)}) custom-call(s32[12]{0:T(128)} %bitcast.73, s32[12]{0:T(128)} %off_row.1, s32[12]{0:T(128)} %off_col.1, bf16[12,16,14]{2,1,0:T(8,128)(2,1)} %row_ref.1, bf16[12,16,14]{2,1,0:T(8,128)(2,1)} %col_ref.1, bf16[12,14,14,256]{3,2,1,0:T(8,128)(2,1)} %two_ref.1, ...), custom_call_target="tpu_custom_call" | custom-call | flops 13589544960 | bytes 1 | tf_op jit(solution)/shard_map/region_heads/pallas_call | solution.py:190
  20.4 6.4 %all-to-all-start = ((bf16[24,200,256]{2,1,0:T(8,128)(2,1)}), bf16[24,200,256]{2,1,0:T(8,128)(2,1)}, u32[]{:S(2)}, u32[]{:S(2)}) async-start(bf16[24,200,256]{2,1,0:T(8,128)(2,1)} %get-tuple-element.19), calls=%async_computation | async-start | bytes 4915200 | tf_op jit(solution)/shard_map/all_to_all | solution.py:559
  26.8 0.6 pad_add_fusion.where
  27.4 15.6 %head_weight_grads.1 = (f32[2,128,2304]{2,1,0:T(8,128)}, bf16[2,128,2304]{2,1,0:T(8,128)(2,1)}) custom-call(s32[2]{0:T(128)} %pad_add_fusion.where, bf16[12,14,14,256]{3,2,1,0:T(8,128)(2,1)} %two_ref.1, bf16[12,14,14,256]{3,2,1,0:T(8,128)(2,1)} %pre_ref.1, bf16[2880,256]{1,0:T(8,128)(2,1)} %get-tuple-element.15.one_hbm, bf16[12,14,14,256]{3,2,1,0:T(8,128)(2,1)} %feat_hbm.1), custom_call_target="tpu_custom_call" | custom-call | flops 1 | bytes 1 | tf_op jit(solution)/shard_map/head_weight_grads/pallas_call | solution.py:289
  43.0 1.0 collective-permute-start
  44.1 3.0 %collective-permute-start.4 = (bf16[1,64,256]{2,1,0:T(8,128)(2,1)S(1)}, bf16[1,64,256]{2,1,0:T(8,128)(2,1)S(1)}, u32[]{:S(2)}, u32[]{:S(2)}) collective-permute-start(bf16[1,64,256]{2,1,0:T(8,128)(2,1)S(1)} %slice.112), channel_id=1, source_target_pairs={{0,8},{8,16},{16,24},{1,9},{9,17},{17,25},{2,10},{10,18},{18,26},{... | collective-permute-start | bytes 98312 | tf_op jit(solution)/shard_map/ppermute | solution.py:492
  47.1 1.9 %collective-permute-start.5 = (bf16[16,64,256]{2,1,0:T(8,128)(2,1)S(1)}, bf16[16,64,256]{2,1,0:T(8,128)(2,1)S(1)}, u32[]{:S(2)}, u32[]{:S(2)}) collective-permute-start(bf16[16,64,256]{2,1,0:T(8,128)(2,1)S(1)} %copy-done.2), channel_id=1, source_target_pairs={{8,0},{16,8},{24,16},{9,1},{17,9},{25,17},{10,2},{18,10},{26,18},{... | collective-permute-start | bytes 1572872 | tf_op jit(solution)/shard_map/ppermute | solution.py:492
  49.0 0.0 collective-permute-done.4
  49.1 0.0 collective-permute-done
  49.1 1.9 %convert_add_fusion.1 = f32[2,128,2304]{2,1,0:T(8,128)S(1)} fusion(f32[2,128,2304]{2,1,0:T(8,128)} %get-tuple-element.16, bf16[2,128,2304]{2,1,0:T(8,128)(2,1)S(1)} %collective-permute-done), kind=kLoop, calls=%fused_computation.1 | loop fusion | flops 1179648 | bytes 5898240 | tf_op jit(solution)/shard_map/add | solution.py:510
  51.1 0.1 convert.36
  51.2 0.1 slice_bitcast_fusion.4
  51.2 1.8 %collective-permute-start.1 = (bf16[2,32,2304]{2,1,0:T(8,128)(2,1)S(1)}, bf16[2,32,2304]{2,1,0:T(8,128)(2,1)S(1)}, u32[]{:S(2)}, u32[]{:S(2)}) collective-permute-start(bf16[2,32,2304]{2,1,0:T(8,128)(2,1)S(1)} %get-tuple-element.28), channel_id=1, source_target_pairs={{0,1},{1,0},{2,3},{3,2},{4,5},{5,4},{6,7},{7,6},{8,9},{9,8},{10,11... | collective-permute-start | bytes 884744 | tf_op jit(solution)/shard_map/ppermute | solution.py:498
  53.1 0.6 collective-permute-start.2
  53.7 0.7 collective-permute-start.3
  54.3 5.6 %collective-permute-done.5 = bf16[16,64,256]{2,1,0:T(8,128)(2,1)S(1)} collective-permute-done((bf16[16,64,256]{2,1,0:T(8,128)(2,1)S(1)}, bf16[16,64,256]{2,1,0:T(8,128)(2,1)S(1)}, u32[]{:S(2)}, u32[]{:S(2)}) %collective-permute-start.5) | collective-permute-done | bytes 524320 | tf_op jit(solution)/shard_map/ppermute | solution.py:492
  60.0 1.3 collective-permute-start.7
  61.4 6.0 %collective-permute-start.6 = (bf16[33,1,256]{2,1,0:T(2,128)(2,1)S(1)}, bf16[33,1,256]{2,1,0:T(2,128)(2,1)S(1)}, u32[]{:S(2)}, u32[]{:S(2)}) collective-permute-start(bf16[33,1,256]{2,1,0:T(2,128)(2,1)S(1)} %slice.142), channel_id=1, source_target_pairs={{0,1},{1,2},{2,3},{3,4},{4,5},{5,6},{6,7},{8,9},{9,10},{10,11},{11... | collective-permute-start | bytes 50696 | tf_op jit(solution)/shard_map/ppermute | solution.py:492
  67.4 9.3 %collective-permute-done.6.left_ref = bf16[33,1,256]{2,1,0:T(2,128)(2,1)S(1)} collective-permute-done((bf16[33,1,256]{2,1,0:T(2,128)(2,1)S(1)}, bf16[33,1,256]{2,1,0:T(2,128)(2,1)S(1)}, u32[]{:S(2)}, u32[]{:S(2)}) %collective-permute-start.6) | collective-permute-done | bytes 16928 | tf_op jit(solution)/shard_map/ppermute | solution.py:492
  76.6 5.3 %collective-permute-done.7.right_ref = bf16[33,16,256]{2,1,0:T(8,128)(2,1)S(1)} collective-permute-done((bf16[33,16,256]{2,1,0:T(8,128)(2,1)S(1)}, bf16[33,16,256]{2,1,0:T(8,128)(2,1)S(1)}, u32[]{:S(2)}, u32[]{:S(2)}) %collective-permute-start.7) | collective-permute-done | bytes 270368 | tf_op jit(solution)/shard_map/ppermute | solution.py:492
  81.9 0.7 copy-done.3
  82.6 4.5 %lay_out_input.1.taps_hbm = bf16[3,2720,256]{2,1,0:T(8,128)(2,1)} custom-call(bf16[33,64,256]{2,1,0:T(8,128)(2,1)} %copy-done.1, bf16[33,1,256]{2,1,0:T(2,128)(2,1)} %copy-done.4, bf16[33,16,256]{2,1,0:T(8,128)(2,1)} %copy-done.3), custom_call_target="tpu_custom_call" | custom-call | flops 1 | bytes 1 | tf_op jit(solution)/shard_map/lay_out_input/pallas_call | solution.py:333
  87.1 0.0 collective-permute-done.1
  87.1 0.0 collective-permute-done.2
  87.1 0.0 collective-permute-done.3
  87.1 0.1 fusion.1
  87.2 0.0 all-to-all-done.received
  87.2 11.0 %tile_gradient.1 = (f32[32,80,256]{2,1,0:T(8,128)}, f32[1,128,2304]{2,1,0:T(8,128)}, bf16[1,128,2304]{2,1,0:T(8,128)(2,1)}) custom-call(s32[2]{0:T(128)} %pad_add_fusion.where, bf16[16,64,256]{2,1,0:T(8,128)(2,1)} %start_ref, bf16[24,200,256]{2,1,0:T(8,128)(2,1)} %all-to-all-done.received, bf16[3,2720,256]{2,1,0:T(8,128)(2,1)} %lay_out_input.1.taps_hbm), custom_call_target="tpu_custom_call" | custom-call | flops 6039797760 | bytes 1 | tf_op jit(solution)/shard_map/tile_gradient/pallas_call | solution.py:431
  98.2 0.1 collective-permute-start.8
  98.3 2.2 %collective-permute-done.8 = bf16[1,128,2304]{2,1,0:T(8,128)(2,1)S(1)} collective-permute-done((bf16[1,128,2304]{2,1,0:T(8,128)(2,1)}, bf16[1,128,2304]{2,1,0:T(8,128)(2,1)S(1)}, u32[]{:S(2)}, u32[]{:S(2)}) %collective-permute-start.8) | collective-permute-done | bytes 589856 | tf_op jit(solution)/shard_map/ppermute | solution.py:500
  100.5 1.4 convert_add_fusion.2
  101.9 0.1 convert.40
  102.0 6.1 %collective-permute-start.16 = (bf16[1,32,2304]{2,1,0:T(8,128)(2,1)S(1)}, bf16[1,32,2304]{2,1,0:T(8,128)(2,1)S(1)}, u32[]{:S(2)}, u32[]{:S(2)}) collective-permute-start(bf16[1,32,2304]{2,1,0:T(8,128)(2,1)S(1)} %get-tuple-element.34), channel_id=1, source_target_pairs={{0,1},{1,0},{2,3},{3,2},{4,5},{5,4},{6,7},{7,6},{8,9},{9,8},{10,11... | collective-permute-start | bytes 442376 | tf_op jit(solution)/shard_map/ppermute | solution.py:498
  108.1 0.0 collective-permute-start.17
  108.1 1.3 collective-permute-start.18
  109.4 0.2 slice.115
  109.5 0.1 convert.37
  109.7 0.1 slice.144
  109.8 3.3 %collective-permute-start.9 = (bf16[32,16,256]{2,1,0:T(8,128)(2,1)S(1)}, bf16[32,16,256]{2,1,0:T(8,128)(2,1)S(1)}, u32[]{:S(2)}, u32[]{:S(2)}) collective-permute-start(bf16[32,16,256]{2,1,0:T(8,128)(2,1)S(1)} %slice.144), channel_id=1, source_target_pairs={{0,1},{1,2},{2,3},{3,4},{4,5},{5,6},{6,7},{8,9},{9,10},{10,11},{11... | collective-permute-start | bytes 786440 | tf_op jit(solution)/shard_map/ppermute | solution.py:492
  113.1 1.3 collective-permute-start.10
  114.4 0.0 collective-permute-done.17
  114.4 1.9 %collective-permute-done.18 = bf16[1,32,2304]{2,1,0:T(8,128)(2,1)S(1)} collective-permute-done((bf16[1,32,2304]{2,1,0:T(8,128)(2,1)S(1)}, bf16[1,32,2304]{2,1,0:T(8,128)(2,1)S(1)}, u32[]{:S(2)}, u32[]{:S(2)}) %collective-permute-start.18) | collective-permute-done | bytes 147488 | tf_op jit(solution)/shard_map/ppermute | solution.py:504
  116.4 0.1 fusion.3
  116.4 3.4 %collective-permute-done.10 = bf16[32,1,256]{2,1,0:T(2,128)(2,1)S(1)} collective-permute-done((bf16[32,1,256]{2,1,0:T(2,128)(2,1)S(1)}, bf16[32,1,256]{2,1,0:T(2,128)(2,1)S(1)}, u32[]{:S(2)}, u32[]{:S(2)}) %collective-permute-start.10) | collective-permute-done | bytes 16416 | tf_op jit(solution)/shard_map/ppermute | solution.py:492
  119.8 1.9 %collective-permute-done.9 = bf16[32,16,256]{2,1,0:T(8,128)(2,1)S(1)} collective-permute-done((bf16[32,16,256]{2,1,0:T(8,128)(2,1)S(1)}, bf16[32,16,256]{2,1,0:T(8,128)(2,1)S(1)}, u32[]{:S(2)}, u32[]{:S(2)}) %collective-permute-start.9) | collective-permute-done | bytes 262176 | tf_op jit(solution)/shard_map/ppermute | solution.py:492
  121.7 0.3 fusion.5
  122.1 5.2 %collective-permute-start.19 = (bf16[1,8,2304]{2,1,0:T(8,128)(2,1)S(1)}, bf16[1,8,2304]{2,1,0:T(8,128)(2,1)S(1)}, u32[]{:S(2)}, u32[]{:S(2)}) collective-permute-start(bf16[1,8,2304]{2,1,0:T(8,128)(2,1)S(1)} %get-tuple-element.40), channel_id=1, source_target_pairs={{0,2},{1,3},{2,0},{3,1},{4,6},{5,7},{6,4},{7,5},{8,10},{9,11},{10,... | collective-permute-start | bytes 110600 | tf_op jit(solution)/shard_map/ppermute | solution.py:498
  127.3 2.6 %collective-permute-start.20 = (bf16[1,8,2304]{2,1,0:T(8,128)(2,1)S(1)}, bf16[1,8,2304]{2,1,0:T(8,128)(2,1)S(1)}, u32[]{:S(2)}, u32[]{:S(2)}) collective-permute-start(bf16[1,8,2304]{2,1,0:T(8,128)(2,1)S(1)} %get-tuple-element.42), channel_id=1, source_target_pairs={{0,4},{1,5},{2,6},{3,7},{4,0},{5,1},{6,2},{7,3},{8,12},{9,13},{10,... | collective-permute-start | bytes 110600 | tf_op jit(solution)/shard_map/ppermute | solution.py:498
  129.9 1.1 collective-permute-start.21
  131.1 0.1 slice.146
  131.3 0.3 collective-permute-start.13
  131.6 2.2 %collective-permute-start.14 = (bf16[2,8,2304]{2,1,0:T(8,128)(2,1)S(1)}, bf16[2,8,2304]{2,1,0:T(8,128)(2,1)S(1)}, u32[]{:S(2)}, u32[]{:S(2)}) collective-permute-start(bf16[2,8,2304]{2,1,0:T(8,128)(2,1)S(1)} %get-tuple-element.39), channel_id=1, source_target_pairs={{0,4},{1,5},{2,6},{3,7},{4,0},{5,1},{6,2},{7,3},{8,12},{9,13},{10,... | collective-permute-start | bytes 221192 | tf_op jit(solution)/shard_map/ppermute | solution.py:498
  133.8 0.1 copy.26
  133.9 1.2 collective-permute-start.15
  135.1 3.9 %collective-permute-start.11 = (bf16[16,66,256]{2,0,1:T(8,128)(2,1)S(1)}, bf16[16,66,256]{2,0,1:T(8,128)(2,1)S(1)}, u32[]{:S(2)}, u32[]{:S(2)}) collective-permute-start(bf16[16,66,256]{2,0,1:T(8,128)(2,1)S(1)} %copy.26), channel_id=1, source_target_pairs={{0,8},{8,16},{16,24},{1,9},{9,17},{17,25},{2,10},{10,18},{18,26},{... | collective-permute-start | bytes 1622024 | tf_op jit(solution)/shard_map/ppermute | solution.py:492
  139.0 1.9 %collective-permute-start.12 = (bf16[1,66,256]{2,1,0:T(8,128)(2,1)S(1)}, bf16[1,66,256]{2,1,0:T(8,128)(2,1)S(1)}, u32[]{:S(2)}, u32[]{:S(2)}) collective-permute-start(bf16[1,66,256]{2,1,0:T(8,128)(2,1)S(1)} %slice.148), channel_id=1, source_target_pairs={{8,0},{16,8},{24,16},{9,1},{17,9},{25,17},{10,2},{18,10},{26,18},{... | collective-permute-start | bytes 101384 | tf_op jit(solution)/shard_map/ppermute | solution.py:492
  140.9 0.6 squeeze_reshape.3
  141.6 0.6 squeeze.14
  142.3 0.6 squeeze.15
  142.9 2.3 %collective-permute-done.11 = bf16[16,66,256]{2,0,1:T(8,128)(2,1)S(1)} collective-permute-done((bf16[16,66,256]{2,0,1:T(8,128)(2,1)S(1)}, bf16[16,66,256]{2,0,1:T(8,128)(2,1)S(1)}, u32[]{:S(2)}, u32[]{:S(2)}) %collective-permute-start.11) | collective-permute-done | bytes 540704 | tf_op jit(solution)/shard_map/ppermute | solution.py:492
  145.2 0.2 copy.27
  145.4 0.2 add_convert_fusion
  145.6 1.6 %fusion.6 = (bf16[18,64,256]{2,1,0:T(8,128)(2,1)}, bf16[18,64,256]{2,1,0:T(8,128)(2,1)}, bf16[18,64,256]{2,1,0:T(8,128)(2,1)}) fusion(bf16[18,66,256]{2,1,0:T(8,128)(2,1)S(1)} %add_convert_fusion), kind=kLoop, calls=%fused_computation.30 | loop fusion | bytes 3538944 | tf_op jit(solution)/shard_map/slice | solution.py:591
  147.2 4.0 %tile_input_grad.1 = bf16[1024,256]{1,0:T(8,128)(2,1)} custom-call(bf16[1152,256]{1,0:T(8,128)(2,1)} %bitcast.71, bf16[1152,256]{1,0:T(8,128)(2,1)} %bitcast.70, bf16[1152,256]{1,0:T(8,128)(2,1)} %bitcast.69, bf16[3,3,256,256]{3,2,1,0:T(8,128)(2,1)} %weight.1), custom_call_target="tpu_custom_call" | custom-call | flops 1 | bytes 1 | tf_op jit(solution)/shard_map/tile_input_grad/pallas_call | solution.py:480
  (34 shorter events, 0.4 us)
Async XLA Ops:
  20.4 66.8 %all-to-all-start = ((bf16[24,200,256]{2,1,0:T(8,128)(2,1)}), bf16[24,200,256]{2,1,0:T(8,128)(2,1)}, u32[]{:S(2)}, u32[]{:S(2)}) async-start(bf16[24,200,256]{2,1,0:T(8,128)(2,1)} %get-tuple-element.19), calls=%async_computation | async-start | bytes 4915200 | tf_op jit(solution)/shard_map/all_to_all | solution.py:559
  27.4 16.6 %copy-start.2 = (bf16[16,64,256]{2,1,0:T(8,128)(2,1)S(1)}, bf16[16,64,256]{2,1,0:T(8,128)(2,1)}, u32[]{:S(2)}) copy-start(bf16[16,64,256]{2,1,0:T(8,128)(2,1)} %param.23) | copy-start | bytes 1572868
  43.0 6.1 %collective-permute-start = (bf16[2,128,2304]{2,1,0:T(8,128)(2,1)}, bf16[2,128,2304]{2,1,0:T(8,128)(2,1)S(1)}, u32[]{:S(2)}, u32[]{:S(2)}) collective-permute-start(bf16[2,128,2304]{2,1,0:T(8,128)(2,1)} %get-tuple-element.17), channel_id=1, source_target_pairs={{0,8},{8,0},{16,24},{24,16},{1,9},{9,1},{17,25},{25,17},{2,10},{10... | collective-permute-start | bytes 3538952 | tf_op jit(solution)/shard_map/ppermute | solution.py:500
  44.1 5.0 %collective-permute-start.4 = (bf16[1,64,256]{2,1,0:T(8,128)(2,1)S(1)}, bf16[1,64,256]{2,1,0:T(8,128)(2,1)S(1)}, u32[]{:S(2)}, u32[]{:S(2)}) collective-permute-start(bf16[1,64,256]{2,1,0:T(8,128)(2,1)S(1)} %slice.112), channel_id=1, source_target_pairs={{0,8},{8,16},{16,24},{1,9},{9,17},{17,25},{2,10},{10,18},{18,26},{... | collective-permute-start | bytes 98312 | tf_op jit(solution)/shard_map/ppermute | solution.py:492
  47.1 12.9 %collective-permute-start.5 = (bf16[16,64,256]{2,1,0:T(8,128)(2,1)S(1)}, bf16[16,64,256]{2,1,0:T(8,128)(2,1)S(1)}, u32[]{:S(2)}, u32[]{:S(2)}) collective-permute-start(bf16[16,64,256]{2,1,0:T(8,128)(2,1)S(1)} %copy-done.2), channel_id=1, source_target_pairs={{8,0},{16,8},{24,16},{9,1},{17,9},{25,17},{10,2},{18,10},{26,18},{... | collective-permute-start | bytes 1572872 | tf_op jit(solution)/shard_map/ppermute | solution.py:492
  51.2 35.8 %collective-permute-start.1 = (bf16[2,32,2304]{2,1,0:T(8,128)(2,1)S(1)}, bf16[2,32,2304]{2,1,0:T(8,128)(2,1)S(1)}, u32[]{:S(2)}, u32[]{:S(2)}) collective-permute-start(bf16[2,32,2304]{2,1,0:T(8,128)(2,1)S(1)} %get-tuple-element.28), channel_id=1, source_target_pairs={{0,1},{1,0},{2,3},{3,2},{4,5},{5,4},{6,7},{7,6},{8,9},{9,8},{10,11... | collective-permute-start | bytes 884744 | tf_op jit(solution)/shard_map/ppermute | solution.py:498
  53.1 34.0 %collective-permute-start.2 = (bf16[2,32,2304]{2,1,0:T(8,128)(2,1)S(1)}, bf16[2,32,2304]{2,1,0:T(8,128)(2,1)S(1)}, u32[]{:S(2)}, u32[]{:S(2)}) collective-permute-start(bf16[2,32,2304]{2,1,0:T(8,128)(2,1)S(1)} %get-tuple-element.30), channel_id=1, source_target_pairs={{0,16},{8,24},{16,0},{24,8},{1,17},{9,25},{17,1},{25,9},{2,18},{10... | collective-permute-start | bytes 884744 | tf_op jit(solution)/shard_map/ppermute | solution.py:500
  53.7 33.4 %collective-permute-start.3 = (bf16[2,32,2304]{2,1,0:T(8,128)(2,1)S(1)}, bf16[2,32,2304]{2,1,0:T(8,128)(2,1)S(1)}, u32[]{:S(2)}, u32[]{:S(2)}) collective-permute-start(bf16[2,32,2304]{2,1,0:T(8,128)(2,1)S(1)} %get-tuple-element.29), channel_id=1, source_target_pairs={{0,17},{1,16},{2,19},{3,18},{4,21},{5,20},{6,23},{7,22},{8,25},{9,... | collective-permute-start | bytes 884744 | tf_op jit(solution)/shard_map/ppermute | solution.py:504
  60.0 21.9 %copy-start.1 = (bf16[33,64,256]{2,1,0:T(8,128)(2,1)}, bf16[33,64,256]{2,1,0:T(8,128)(2,1)S(1)}, u32[]{:S(2)}) copy-start(bf16[33,64,256]{2,1,0:T(8,128)(2,1)S(1)} %constant_dynamic-update-slice_fusion.own_ref) | copy-start | bytes 3244036
  60.0 21.8 %collective-permute-start.7 = (bf16[33,16,256]{2,1,0:T(8,128)(2,1)S(1)}, bf16[33,16,256]{2,1,0:T(8,128)(2,1)S(1)}, u32[]{:S(2)}, u32[]{:S(2)}) collective-permute-start(bf16[33,16,256]{2,1,0:T(8,128)(2,1)S(1)} %slice.143), channel_id=1, source_target_pairs={{1,0},{2,1},{3,2},{4,3},{5,4},{6,5},{7,6},{9,8},{10,9},{11,10},{12... | collective-permute-start | bytes 811016 | tf_op jit(solution)/shard_map/ppermute | solution.py:492
  61.4 15.2 %collective-permute-start.6 = (bf16[33,1,256]{2,1,0:T(2,128)(2,1)S(1)}, bf16[33,1,256]{2,1,0:T(2,128)(2,1)S(1)}, u32[]{:S(2)}, u32[]{:S(2)}) collective-permute-start(bf16[33,1,256]{2,1,0:T(2,128)(2,1)S(1)} %slice.142), channel_id=1, source_target_pairs={{0,1},{1,2},{2,3},{3,4},{4,5},{5,6},{6,7},{8,9},{9,10},{10,11},{11... | collective-permute-start | bytes 50696 | tf_op jit(solution)/shard_map/ppermute | solution.py:492
  76.6 5.3 %copy-start.4 = (bf16[33,1,256]{2,1,0:T(2,128)(2,1)}, bf16[33,1,256]{2,1,0:T(2,128)(2,1)S(1)}, u32[]{:S(2)}) copy-start(bf16[33,1,256]{2,1,0:T(2,128)(2,1)S(1)} %collective-permute-done.6.left_ref) | copy-start | bytes 50692
  81.9 0.7 copy-start.3
  98.2 2.3 %collective-permute-start.8 = (bf16[1,128,2304]{2,1,0:T(8,128)(2,1)}, bf16[1,128,2304]{2,1,0:T(8,128)(2,1)S(1)}, u32[]{:S(2)}, u32[]{:S(2)}) collective-permute-start(bf16[1,128,2304]{2,1,0:T(8,128)(2,1)} %get-tuple-element.22), channel_id=1, source_target_pairs={{0,8},{8,0},{16,24},{24,16},{1,9},{9,1},{17,25},{25,17},{2,10},{10... | collective-permute-start | bytes 1769480 | tf_op jit(solution)/shard_map/ppermute | solution.py:500
  101.9 7.5 %copy-start = (f32[32,80,256]{2,1,0:T(8,128)S(1)}, f32[32,80,256]{2,1,0:T(8,128)}, u32[]{:S(2)}) copy-start(f32[32,80,256]{2,1,0:T(8,128)} %get-tuple-element.23) | copy-start | bytes 7864324
  102.0 12.4 %collective-permute-start.16 = (bf16[1,32,2304]{2,1,0:T(8,128)(2,1)S(1)}, bf16[1,32,2304]{2,1,0:T(8,128)(2,1)S(1)}, u32[]{:S(2)}, u32[]{:S(2)}) collective-permute-start(bf16[1,32,2304]{2,1,0:T(8,128)(2,1)S(1)} %get-tuple-element.34), channel_id=1, source_target_pairs={{0,1},{1,0},{2,3},{3,2},{4,5},{5,4},{6,7},{7,6},{8,9},{9,8},{10,11... | collective-permute-start | bytes 442376 | tf_op jit(solution)/shard_map/ppermute | solution.py:498
  108.1 6.3 %collective-permute-start.17 = (bf16[1,32,2304]{2,1,0:T(8,128)(2,1)S(1)}, bf16[1,32,2304]{2,1,0:T(8,128)(2,1)S(1)}, u32[]{:S(2)}, u32[]{:S(2)}) collective-permute-start(bf16[1,32,2304]{2,1,0:T(8,128)(2,1)S(1)} %get-tuple-element.36), channel_id=1, source_target_pairs={{0,16},{8,24},{16,0},{24,8},{1,17},{9,25},{17,1},{25,9},{2,18},{10... | collective-permute-start | bytes 442376 | tf_op jit(solution)/shard_map/ppermute | solution.py:500
  108.1 8.3 %collective-permute-start.18 = (bf16[1,32,2304]{2,1,0:T(8,128)(2,1)S(1)}, bf16[1,32,2304]{2,1,0:T(8,128)(2,1)S(1)}, u32[]{:S(2)}, u32[]{:S(2)}) collective-permute-start(bf16[1,32,2304]{2,1,0:T(8,128)(2,1)S(1)} %get-tuple-element.35), channel_id=1, source_target_pairs={{0,17},{1,16},{2,19},{3,18},{4,21},{5,20},{6,23},{7,22},{8,25},{9,... | collective-permute-start | bytes 442376 | tf_op jit(solution)/shard_map/ppermute | solution.py:504
  109.8 11.9 %collective-permute-start.9 = (bf16[32,16,256]{2,1,0:T(8,128)(2,1)S(1)}, bf16[32,16,256]{2,1,0:T(8,128)(2,1)S(1)}, u32[]{:S(2)}, u32[]{:S(2)}) collective-permute-start(bf16[32,16,256]{2,1,0:T(8,128)(2,1)S(1)} %slice.144), channel_id=1, source_target_pairs={{0,1},{1,2},{2,3},{3,4},{4,5},{5,6},{6,7},{8,9},{9,10},{10,11},{11... | collective-permute-start | bytes 786440 | tf_op jit(solution)/shard_map/ppermute | solution.py:492
  113.1 6.7 %collective-permute-start.10 = (bf16[32,1,256]{2,1,0:T(2,128)(2,1)S(1)}, bf16[32,1,256]{2,1,0:T(2,128)(2,1)S(1)}, u32[]{:S(2)}, u32[]{:S(2)}) collective-permute-start(bf16[32,1,256]{2,1,0:T(2,128)(2,1)S(1)} %slice.145), channel_id=1, source_target_pairs={{1,0},{2,1},{3,2},{4,3},{5,4},{6,5},{7,6},{9,8},{10,9},{11,10},{12... | collective-permute-start | bytes 49160 | tf_op jit(solution)/shard_map/ppermute | solution.py:492
  122.1 11.7 %collective-permute-start.19 = (bf16[1,8,2304]{2,1,0:T(8,128)(2,1)S(1)}, bf16[1,8,2304]{2,1,0:T(8,128)(2,1)S(1)}, u32[]{:S(2)}, u32[]{:S(2)}) collective-permute-start(bf16[1,8,2304]{2,1,0:T(8,128)(2,1)S(1)} %get-tuple-element.40), channel_id=1, source_target_pairs={{0,2},{1,3},{2,0},{3,1},{4,6},{5,7},{6,4},{7,5},{8,10},{9,11},{10,... | collective-permute-start | bytes 110600 | tf_op jit(solution)/shard_map/ppermute | solution.py:498
  127.3 7.7 %collective-permute-start.20 = (bf16[1,8,2304]{2,1,0:T(8,128)(2,1)S(1)}, bf16[1,8,2304]{2,1,0:T(8,128)(2,1)S(1)}, u32[]{:S(2)}, u32[]{:S(2)}) collective-permute-start(bf16[1,8,2304]{2,1,0:T(8,128)(2,1)S(1)} %get-tuple-element.42), channel_id=1, source_target_pairs={{0,4},{1,5},{2,6},{3,7},{4,0},{5,1},{6,2},{7,3},{8,12},{9,13},{10,... | collective-permute-start | bytes 110600 | tf_op jit(solution)/shard_map/ppermute | solution.py:498
  129.9 9.0 %collective-permute-start.21 = (bf16[1,8,2304]{2,1,0:T(8,128)(2,1)S(1)}, bf16[1,8,2304]{2,1,0:T(8,128)(2,1)S(1)}, u32[]{:S(2)}, u32[]{:S(2)}) collective-permute-start(bf16[1,8,2304]{2,1,0:T(8,128)(2,1)S(1)} %get-tuple-element.41), channel_id=1, source_target_pairs={{0,6},{1,7},{2,4},{3,5},{4,2},{5,3},{6,0},{7,1},{8,14},{9,15},{10,... | collective-permute-start | bytes 110600 | tf_op jit(solution)/shard_map/ppermute | solution.py:498
  131.3 10.3 %collective-permute-start.13 = (bf16[2,8,2304]{2,1,0:T(8,128)(2,1)S(1)}, bf16[2,8,2304]{2,1,0:T(8,128)(2,1)S(1)}, u32[]{:S(2)}, u32[]{:S(2)}) collective-permute-start(bf16[2,8,2304]{2,1,0:T(8,128)(2,1)S(1)} %get-tuple-element.37), channel_id=1, source_target_pairs={{0,2},{1,3},{2,0},{3,1},{4,6},{5,7},{6,4},{7,5},{8,10},{9,11},{10,... | collective-permute-start | bytes 221192 | tf_op jit(solution)/shard_map/ppermute | solution.py:498
  131.6 10.0 %collective-permute-start.14 = (bf16[2,8,2304]{2,1,0:T(8,128)(2,1)S(1)}, bf16[2,8,2304]{2,1,0:T(8,128)(2,1)S(1)}, u32[]{:S(2)}, u32[]{:S(2)}) collective-permute-start(bf16[2,8,2304]{2,1,0:T(8,128)(2,1)S(1)} %get-tuple-element.39), channel_id=1, source_target_pairs={{0,4},{1,5},{2,6},{3,7},{4,0},{5,1},{6,2},{7,3},{8,12},{9,13},{10,... | collective-permute-start | bytes 221192 | tf_op jit(solution)/shard_map/ppermute | solution.py:498
  133.9 7.7 %collective-permute-start.15 = (bf16[2,8,2304]{2,1,0:T(8,128)(2,1)S(1)}, bf16[2,8,2304]{2,1,0:T(8,128)(2,1)S(1)}, u32[]{:S(2)}, u32[]{:S(2)}) collective-permute-start(bf16[2,8,2304]{2,1,0:T(8,128)(2,1)S(1)} %get-tuple-element.38), channel_id=1, source_target_pairs={{0,6},{1,7},{2,4},{3,5},{4,2},{5,3},{6,0},{7,1},{8,14},{9,15},{10,... | collective-permute-start | bytes 221192 | tf_op jit(solution)/shard_map/ppermute | solution.py:498
  135.1 10.2 %collective-permute-start.11 = (bf16[16,66,256]{2,0,1:T(8,128)(2,1)S(1)}, bf16[16,66,256]{2,0,1:T(8,128)(2,1)S(1)}, u32[]{:S(2)}, u32[]{:S(2)}) collective-permute-start(bf16[16,66,256]{2,0,1:T(8,128)(2,1)S(1)} %copy.26), channel_id=1, source_target_pairs={{0,8},{8,16},{16,24},{1,9},{9,17},{17,25},{2,10},{10,18},{18,26},{... | collective-permute-start | bytes 1622024 | tf_op jit(solution)/shard_map/ppermute | solution.py:492
  139.0 6.4 %collective-permute-start.12 = (bf16[1,66,256]{2,1,0:T(8,128)(2,1)S(1)}, bf16[1,66,256]{2,1,0:T(8,128)(2,1)S(1)}, u32[]{:S(2)}, u32[]{:S(2)}) collective-permute-start(bf16[1,66,256]{2,1,0:T(8,128)(2,1)S(1)} %slice.148), channel_id=1, source_target_pairs={{8,0},{16,8},{24,16},{9,1},{17,9},{25,17},{10,2},{18,10},{26,18},{... | collective-permute-start | bytes 101384 | tf_op jit(solution)/shard_map/ppermute | solution.py:492

commit v3 on v2

--- a/solution.py
+++ b/solution.py
@@ -311,7 +311,7 @@
     )(where, grad_two, pre_one, grad_one, roi_feat)
 
 
-def lay_body(geometry, own_ref, left_ref, right_ref, out_ref, wide):
+def lay_out(geometry, own_ref, left_ref, right_ref, out_ref, wide):
     rows, pitch, tile_cols = geometry
     wide[...] = jnp.zeros_like(wide)
     for y in range(rows):
@@ -323,23 +323,6 @@
     for y in range(rows):
         wide[pl.ds(7 + y * pitch, 1), :] = left_ref[y].astype(F32)
     out_ref[0] = wide[pl.ds(7, out_ref.shape[1]), :].astype(BF)
-
-
-def lay_out_input(own, left, right):
-    rows, tile_cols, channels = own.shape
-    pitch = tile_cols + right.shape[1]
-    vmem = pl.BlockSpec(memory_space=pltpu.VMEM)
-    full = ceil_to(rows, 2)
-    return pl.pallas_call(
-        functools.partial(lay_body, (rows, pitch, tile_cols)),
-        in_specs=[vmem] * 3,
-        out_specs=vmem,
-        out_shape=jax.ShapeDtypeStruct((3, full * pitch, channels), BF),
-        scratch_shapes=[pltpu.VMEM((full * pitch + 16, channels), F32)],
-        compiler_params=params(),
-        cost_estimate=cost(),
-        name="lay_out_input",
-    )(own, left, right)
 
 
 def place_all(geometry, received, start_ref, canvas, row_spread, col_spread, block, numbers, place, sem):
@@ -387,13 +370,11 @@
     lax.fori_loop(0, slots, put, 0)
 
 
-def tile_body(geometry, where, start_ref, received, taps_hbm, canvas, keep_hbm, send_hbm, taps, turned, product, keep, send, row_spread, col_spread, block, numbers, place, sems):
+def tile_body(geometry, where, start_ref, received, own_ref, left_ref, right_ref, canvas, keep_hbm, send_hbm, taps, wide, turned, product, keep, send, row_spread, col_spread, block, numbers, place, sems):
     slots, extent, pool, tile_rows, tile_cols, downs, acrosses, layout = geometry
     rows, pitch, channels = canvas.shape
-    load = pltpu.make_async_copy(taps_hbm, taps, sems.at[0])
-    load.start()
     place_all(
-        (slots, extent, pool, tile_rows, tile_cols), received, start_ref, canvas, row_spread, col_spread, block, numbers, place, sems.at[1]
+        (slots, extent, pool, tile_rows, tile_cols), received, start_ref, canvas, row_spread, col_spread, block, numbers, place, sems.at[0]
     )
 
     @pl.when(where[0] == downs - 1)
@@ -407,7 +388,7 @@
     for y in range(0, rows, 2):
         entry = canvas[pl.ds(y, 2)].reshape(2 * pitch, channels)
         turned[:, pl.ds(y * pitch, 2 * pitch)] = entry.astype(BF).T
-    load.wait()
+    lay_out((own_ref.shape[0], pitch, tile_cols), own_ref, left_ref, right_ref, taps, wide)
     length = rows * pitch
     for ey in range(3):
         for ex in range(3):
@@ -421,7 +402,7 @@
     send_hbm[0] = send[...].astype(BF)
 
 
-def tile_gradient(where, layout, start, received, taps, extent, pool, downs, acrosses):
+def tile_gradient(where, layout, start, received, tall, left, right, extent, pool, downs, acrosses):
     tile_rows, tile_cols, channels = start.shape
     slots, depth, _ = received.shape
     rows, pitch = tile_rows + extent, tile_cols + extent
@@ -430,7 +411,7 @@
     geometry = (slots, extent, pool, tile_rows, tile_cols, downs, acrosses, layout)
     return pl.pallas_call(
         functools.partial(tile_body, geometry),
-        in_specs=[smem, vmem, vmem, pl.BlockSpec(memory_space=pl.ANY)],
+        in_specs=[smem] + [vmem] * 5,
         out_specs=[vmem, vmem, vmem],
         out_shape=[
             jax.ShapeDtypeStruct((rows, pitch, channels), F32),
@@ -438,7 +419,8 @@
             jax.ShapeDtypeStruct((1, channels // 2, 9 * channels), BF),
         ],
         scratch_shapes=[
-            pltpu.VMEM(taps.shape, BF),
+            pltpu.VMEM((3, (rows + 2) * pitch, channels), BF),
+            pltpu.VMEM(((rows + 2) * pitch + 16, channels), F32),
             pltpu.VMEM((channels, rows * pitch), BF),
             pltpu.VMEM((channels, 3 * channels), F32),
             pltpu.VMEM((channels // 2, 9 * channels), F32),
@@ -448,12 +430,12 @@
             pltpu.VMEM((ceil_to(depth, 128), channels), BF),
             pltpu.VMEM((slots, 128), jnp.int32),
             pltpu.SMEM((slots, 128), jnp.int32),
-            pltpu.SemaphoreType.DMA((2,)),
+            pltpu.SemaphoreType.DMA((1,)),
         ],
         compiler_params=params(),
         cost_estimate=cost(36 * rows * pitch * channels * channels),
         name="tile_gradient",
-    )(where, start, received, taps)
+    )(where, start, received, tall, left, right)
 
 
 def tile_input_body(pitch, rows, left_ref, mid_ref, right_ref, weight, out_ref):
@@ -566,11 +548,10 @@
     tall = jnp.concatenate([above, fpn_input, below], axis=0)
     left = neighbours(tall[:, tile_cols - 1 :], "tx", 1)
     right = neighbours(tall[:, :extent], "tx", -1)
-    taps = lay_out_input(tall, left, right)
 
     heads = sum_chips(heads, layout)
     canvas, *terms = tile_gradient(
-        where, layout, after(fpn_grad, heads), received, taps, extent, pool, down, across
+        where, layout, after(fpn_grad, heads), received, tall, left, right, extent, pool, down, across
     )
     total = sum_pairs(*terms, layout)
     canvas = after(canvas, total)

time: 152 us -> 150 us (0.987)
  waiting for transfers between devices: 32 us -> 38.2 us
  Pallas kernels: 54.9 us -> 51.2 us
  starting transfers between devices: 53.1 us -> 49.5 us
    ppermute x8, waiting for transfers between devices: 0.02 us -> 15.6 us  [partner(): return lax.ppermute(array, 'tx', [(i, i ^ bits_tx) for i in range(across)])]
    ppermute x8, waiting for transfers between devices: 27.8 us -> 16.6 us  [neighbours(): lax.ppermute(array, axis, [(i, i + by) for i in range(count) if 0 <= i +...]
    ppermute x8, starting transfers between devices: 20.5 us -> 14.8 us  [partner(): return lax.ppermute(array, 'tx', [(i, i ^ bits_tx) for i in range(across)])]
    pallas_call x2 -> x1, Pallas kernels: 15.5 us -> 11.7 us  [tile_gradient(): pl.pallas_call(functools.partial(tile_body, geometry), in_specs=[smem] +...]
    ppermute x4, starting transfers between devices: 1.7 us -> 4.41 us  [partner(): return lax.ppermute(array, 'ty', [(i, i ^ bits_ty) for i in range(down)])]
    ppermute x8, starting transfers between devices: 22.6 us -> 20.1 us  [neighbours(): lax.ppermute(array, axis, [(i, i + by) for i in range(count) if 0 <= i +...]
    ppermute x2, starting transfers between devices: 1.92 us -> 3.81 us  [partner(): return lax.ppermute(array, ('ty', 'tx'), pairs)]
  transfers between devices with their start and end apart: 23 -> 23, of which waited for: 8 -> 8; matrix products, arithmetic and copies ran while one was open for 4% -> 4% of each run, Pallas kernels for 13% -> 10%
where the time goes in v3:
time: 150 us; the launch traced here: 149 us
  Pallas kernels  51.2 us (34%)
  starting transfers between devices  49.5 us (33%)
  waiting for transfers between devices  38.2 us (25%)
  other arithmetic  5.03 us (3%)
  local copies, waits for them, and re-layouts  4.43 us (3%)
    ppermute x8, starting transfers between devices, neighbours(): lax.ppermute(array, axis, [(i, i + by) for i in range(count) if 0 <= i +...  20.1 us
    pallas_call x1, Pallas kernels, region_heads(): pl.pallas_call(functools.partial(head_body, (pool, pitch, regions, capaci...  19.8 us
    ppermute x8, waiting for transfers between devices, neighbours(): lax.ppermute(array, axis, [(i, i + by) for i in range(count) if 0 <= i +...  16.6 us
    ppermute x8, waiting for transfers between devices, partner(): return lax.ppermute(array, 'tx', [(i, i ^ bits_tx) for i in range(across)])  15.6 us
    pallas_call x1, Pallas kernels, head_weight_grads(): pl.pallas_call(functools.partial(head_weight_body, (regions, pool, pitch,...  15.6 us
    ppermute x8, starting transfers between devices, partner(): return lax.ppermute(array, 'tx', [(i, i ^ bits_tx) for i in range(across)])  14.8 us
    pallas_call x1, Pallas kernels, tile_gradient(): pl.pallas_call(functools.partial(tile_body, geometry), in_specs=[smem] +...  11.7 us
    all_to_all x1, starting transfers between devices, local(): received = lax.all_to_all(sent, 'tx', 0, 0, tiled=True)  6.4 us
  transfers between devices with their start and end apart: 23, of which 8 were waited for; matrix products, arithmetic and copies ran while one was open for 4% of the time, Pallas kernels for 10%

profile of v3, /device:TPU:1, one launch (start us, length us, event | category | flops | bytes accessed | tf_op | source)
XLA Modules:
  0.0 149.3 jit_solution(11289928328986103589)
XLA Ops:
  0.6 19.8 %region_heads.1 = (bf16[2880,256]{1,0:T(8,128)(2,1)}, bf16[24,200,256]{2,1,0:T(8,128)(2,1)}) custom-call(s32[12]{0:T(128)} %bitcast.73, s32[12]{0:T(128)} %off_row.1, s32[12]{0:T(128)} %off_col.1, bf16[12,16,14]{2,1,0:T(8,128)(2,1)} %row_ref.1, bf16[12,16,14]{2,1,0:T(8,128)(2,1)} %col_ref.1, bf16[12,14,14,256]{3,2,1,0:T(8,128)(2,1)} %two_ref.1, ...), custom_call_target="tpu_custom_call" | custom-call | flops 13589544960 | bytes 1 | tf_op jit(solution)/shard_map/region_heads/pallas_call | solution.py:190
  20.5 6.4 %all-to-all-start = ((bf16[24,200,256]{2,1,0:T(8,128)(2,1)}), bf16[24,200,256]{2,1,0:T(8,128)(2,1)}, u32[]{:S(2)}, u32[]{:S(2)}) async-start(bf16[24,200,256]{2,1,0:T(8,128)(2,1)} %get-tuple-element.19), calls=%async_computation | async-start | bytes 4915200 | tf_op jit(solution)/shard_map/all_to_all | solution.py:541
  26.9 0.6 pad_add_fusion.where
  27.5 15.6 %head_weight_grads.1 = (f32[2,128,2304]{2,1,0:T(8,128)}, bf16[2,128,2304]{2,1,0:T(8,128)(2,1)}) custom-call(s32[2]{0:T(128)} %pad_add_fusion.where, bf16[12,14,14,256]{3,2,1,0:T(8,128)(2,1)} %two_ref.1, bf16[12,14,14,256]{3,2,1,0:T(8,128)(2,1)} %pre_ref.1, bf16[2880,256]{1,0:T(8,128)(2,1)} %get-tuple-element.15.one_hbm, bf16[12,14,14,256]{3,2,1,0:T(8,128)(2,1)} %feat_hbm.1), custom_call_target="tpu_custom_call" | custom-call | flops 1 | bytes 1 | tf_op jit(solution)/shard_map/head_weight_grads/pallas_call | solution.py:289
  43.1 1.0 collective-permute-start
  44.1 1.9 %collective-permute-start.5 = (bf16[16,64,256]{2,1,0:T(8,128)(2,1)S(1)}, bf16[16,64,256]{2,1,0:T(8,128)(2,1)S(1)}, u32[]{:S(2)}, u32[]{:S(2)}) collective-permute-start(bf16[16,64,256]{2,1,0:T(8,128)(2,1)S(1)} %copy-done.1), channel_id=1, source_target_pairs={{8,0},{16,8},{24,16},{9,1},{17,9},{25,17},{10,2},{18,10},{26,18},{... | collective-permute-start | bytes 1572872 | tf_op jit(solution)/shard_map/ppermute | solution.py:474
  46.0 3.6 %collective-permute-start.4 = (bf16[1,64,256]{2,1,0:T(8,128)(2,1)S(1)}, bf16[1,64,256]{2,1,0:T(8,128)(2,1)S(1)}, u32[]{:S(2)}, u32[]{:S(2)}) collective-permute-start(bf16[1,64,256]{2,1,0:T(8,128)(2,1)S(1)} %slice.112), channel_id=1, source_target_pairs={{0,8},{8,16},{16,24},{1,9},{9,17},{17,25},{2,10},{10,18},{18,26},{... | collective-permute-start | bytes 98312 | tf_op jit(solution)/shard_map/ppermute | solution.py:474
  49.7 0.0 collective-permute-done
  49.7 1.9 %convert_add_fusion.1 = f32[2,128,2304]{2,1,0:T(8,128)S(1)} fusion(f32[2,128,2304]{2,1,0:T(8,128)} %get-tuple-element.16, bf16[2,128,2304]{2,1,0:T(8,128)(2,1)S(1)} %collective-permute-done), kind=kLoop, calls=%fused_computation.1 | loop fusion | flops 1179648 | bytes 5898240 | tf_op jit(solution)/shard_map/add | solution.py:492
  51.6 0.1 convert.36
  51.7 0.1 slice_bitcast_fusion.4
  51.8 1.8 %collective-permute-start.1 = (bf16[2,32,2304]{2,1,0:T(8,128)(2,1)S(1)}, bf16[2,32,2304]{2,1,0:T(8,128)(2,1)S(1)}, u32[]{:S(2)}, u32[]{:S(2)}) collective-permute-start(bf16[2,32,2304]{2,1,0:T(8,128)(2,1)S(1)} %get-tuple-element.28), channel_id=1, source_target_pairs={{0,1},{1,0},{2,3},{3,2},{4,5},{5,4},{6,7},{7,6},{8,9},{9,8},{10,11... | collective-permute-start | bytes 884744 | tf_op jit(solution)/shard_map/ppermute | solution.py:480
  53.6 0.0 collective-permute-start.2
  53.6 1.3 collective-permute-start.3
  54.9 0.0 collective-permute-done.4
  54.9 0.1 collective-permute-done.5
  55.1 1.3 collective-permute-start.7
  56.4 4.3 %collective-permute-start.6 = (bf16[33,1,256]{2,1,0:T(2,128)(2,1)S(1)}, bf16[33,1,256]{2,1,0:T(2,128)(2,1)S(1)}, u32[]{:S(2)}, u32[]{:S(2)}) collective-permute-start(bf16[33,1,256]{2,1,0:T(2,128)(2,1)S(1)} %slice.142), channel_id=1, source_target_pairs={{0,1},{1,2},{2,3},{3,4},{4,5},{5,6},{6,7},{8,9},{9,10},{10,11},{11... | collective-permute-start | bytes 50696 | tf_op jit(solution)/shard_map/ppermute | solution.py:474
  60.7 15.6 %collective-permute-done.1 = bf16[2,32,2304]{2,1,0:T(8,128)(2,1)S(1)} collective-permute-done((bf16[2,32,2304]{2,1,0:T(8,128)(2,1)S(1)}, bf16[2,32,2304]{2,1,0:T(8,128)(2,1)S(1)}, u32[]{:S(2)}, u32[]{:S(2)}) %collective-permute-start.1) | collective-permute-done | bytes 294944 | tf_op jit(solution)/shard_map/ppermute | solution.py:480
  76.3 0.0 collective-permute-done.2
  76.3 0.0 collective-permute-done.3
  76.3 0.1 fusion.1
  76.5 0.6 collective-permute-done.6.left_ref
  77.1 5.0 %collective-permute-done.7.right_ref = bf16[33,16,256]{2,1,0:T(8,128)(2,1)S(1)} collective-permute-done((bf16[33,16,256]{2,1,0:T(8,128)(2,1)S(1)}, bf16[33,16,256]{2,1,0:T(8,128)(2,1)S(1)}, u32[]{:S(2)}, u32[]{:S(2)}) %collective-permute-start.7) | collective-permute-done | bytes 270368 | tf_op jit(solution)/shard_map/ppermute | solution.py:474
  82.1 1.4 all-to-all-done.received
  83.6 11.7 %tile_gradient.1 = (f32[32,80,256]{2,1,0:T(8,128)}, f32[1,128,2304]{2,1,0:T(8,128)}, bf16[1,128,2304]{2,1,0:T(8,128)(2,1)}) custom-call(s32[2]{0:T(128)} %pad_add_fusion.where, bf16[16,64,256]{2,1,0:T(8,128)(2,1)} %start_ref, bf16[24,200,256]{2,1,0:T(8,128)(2,1)} %all-to-all-done.received, bf16[33,64,256]{2,1,0:T(8,128)(2,1)} %copy-done.2, ...), custom_call_target="tpu_custom_call" | custom-call | flops 6039797760 | bytes 1 | tf_op jit(solution)/shard_map/tile_gradient/pallas_call | solution.py:412
  95.3 3.3 %collective-permute-start.8 = (bf16[1,128,2304]{2,1,0:T(8,128)(2,1)}, bf16[1,128,2304]{2,1,0:T(8,128)(2,1)S(1)}, u32[]{:S(2)}, u32[]{:S(2)}) collective-permute-start(bf16[1,128,2304]{2,1,0:T(8,128)(2,1)} %get-tuple-element.22), channel_id=1, source_target_pairs={{0,8},{8,0},{16,24},{24,16},{1,9},{9,1},{17,25},{25,17},{2,10},{10... | collective-permute-start | bytes 1769480 | tf_op jit(solution)/shard_map/ppermute | solution.py:482
  98.6 1.8 %collective-permute-done.8 = bf16[1,128,2304]{2,1,0:T(8,128)(2,1)S(1)} collective-permute-done((bf16[1,128,2304]{2,1,0:T(8,128)(2,1)}, bf16[1,128,2304]{2,1,0:T(8,128)(2,1)S(1)}, u32[]{:S(2)}, u32[]{:S(2)}) %collective-permute-start.8) | collective-permute-done | bytes 589856 | tf_op jit(solution)/shard_map/ppermute | solution.py:482
  100.4 1.4 convert_add_fusion.2
  101.8 0.1 convert.40
  101.9 0.1 collective-permute-start.16
  102.0 0.1 collective-permute-start.17
  102.1 2.6 %collective-permute-start.18 = (bf16[1,32,2304]{2,1,0:T(8,128)(2,1)S(1)}, bf16[1,32,2304]{2,1,0:T(8,128)(2,1)S(1)}, u32[]{:S(2)}, u32[]{:S(2)}) collective-permute-start(bf16[1,32,2304]{2,1,0:T(8,128)(2,1)S(1)} %get-tuple-element.35), channel_id=1, source_target_pairs={{0,17},{1,16},{2,19},{3,18},{4,21},{5,20},{6,23},{7,22},{8,25},{9,... | collective-permute-start | bytes 442376 | tf_op jit(solution)/shard_map/ppermute | solution.py:486
  104.6 0.2 slice.115
  104.8 0.1 convert.37
  104.9 0.1 slice.144
  105.1 2.0 %collective-permute-start.9 = (bf16[32,16,256]{2,1,0:T(8,128)(2,1)S(1)}, bf16[32,16,256]{2,1,0:T(8,128)(2,1)S(1)}, u32[]{:S(2)}, u32[]{:S(2)}) collective-permute-start(bf16[32,16,256]{2,1,0:T(8,128)(2,1)S(1)} %slice.144), channel_id=1, source_target_pairs={{0,1},{1,2},{2,3},{3,4},{4,5},{5,6},{6,7},{8,9},{9,10},{10,11},{11... | collective-permute-start | bytes 786440 | tf_op jit(solution)/shard_map/ppermute | solution.py:474
  107.1 1.3 collective-permute-start.10
  108.4 2.7 %collective-permute-done.18 = bf16[1,32,2304]{2,1,0:T(8,128)(2,1)S(1)} collective-permute-done((bf16[1,32,2304]{2,1,0:T(8,128)(2,1)S(1)}, bf16[1,32,2304]{2,1,0:T(8,128)(2,1)S(1)}, u32[]{:S(2)}, u32[]{:S(2)}) %collective-permute-start.18) | collective-permute-done | bytes 147488 | tf_op jit(solution)/shard_map/ppermute | solution.py:486
  111.1 0.1 fusion.3
  111.1 8.6 %collective-permute-done.10 = bf16[32,1,256]{2,1,0:T(2,128)(2,1)S(1)} collective-permute-done((bf16[32,1,256]{2,1,0:T(2,128)(2,1)S(1)}, bf16[32,1,256]{2,1,0:T(2,128)(2,1)S(1)}, u32[]{:S(2)}, u32[]{:S(2)}) %collective-permute-start.10) | collective-permute-done | bytes 16416 | tf_op jit(solution)/shard_map/ppermute | solution.py:474
  119.7 0.0 collective-permute-done.9
  119.7 0.3 fusion.5
  120.1 7.1 %collective-permute-start.19 = (bf16[1,8,2304]{2,1,0:T(8,128)(2,1)S(1)}, bf16[1,8,2304]{2,1,0:T(8,128)(2,1)S(1)}, u32[]{:S(2)}, u32[]{:S(2)}) collective-permute-start(bf16[1,8,2304]{2,1,0:T(8,128)(2,1)S(1)} %get-tuple-element.40), channel_id=1, source_target_pairs={{0,2},{1,3},{2,0},{3,1},{4,6},{5,7},{6,4},{7,5},{8,10},{9,11},{10,... | collective-permute-start | bytes 110600 | tf_op jit(solution)/shard_map/ppermute | solution.py:480
  127.2 0.0 collective-permute-start.20
  127.2 2.2 %collective-permute-start.21 = (bf16[1,8,2304]{2,1,0:T(8,128)(2,1)S(1)}, bf16[1,8,2304]{2,1,0:T(8,128)(2,1)S(1)}, u32[]{:S(2)}, u32[]{:S(2)}) collective-permute-start(bf16[1,8,2304]{2,1,0:T(8,128)(2,1)S(1)} %get-tuple-element.41), channel_id=1, source_target_pairs={{0,6},{1,7},{2,4},{3,5},{4,2},{5,3},{6,0},{7,1},{8,14},{9,15},{10,... | collective-permute-start | bytes 110600 | tf_op jit(solution)/shard_map/ppermute | solution.py:480
  129.4 0.1 slice.146
  129.6 0.6 collective-permute-start.13
  130.2 0.9 collective-permute-start.14
  131.1 0.1 copy.26
  131.2 2.2 %collective-permute-start.15 = (bf16[2,8,2304]{2,1,0:T(8,128)(2,1)S(1)}, bf16[2,8,2304]{2,1,0:T(8,128)(2,1)S(1)}, u32[]{:S(2)}, u32[]{:S(2)}) collective-permute-start(bf16[2,8,2304]{2,1,0:T(8,128)(2,1)S(1)} %get-tuple-element.38), channel_id=1, source_target_pairs={{0,6},{1,7},{2,4},{3,5},{4,2},{5,3},{6,0},{7,1},{8,14},{9,15},{10,... | collective-permute-start | bytes 221192 | tf_op jit(solution)/shard_map/ppermute | solution.py:480
  133.4 0.0 collective-permute-done.20
  133.4 3.7 %collective-permute-start.11 = (bf16[16,66,256]{2,0,1:T(8,128)(2,1)S(1)}, bf16[16,66,256]{2,0,1:T(8,128)(2,1)S(1)}, u32[]{:S(2)}, u32[]{:S(2)}) collective-permute-start(bf16[16,66,256]{2,0,1:T(8,128)(2,1)S(1)} %copy.26), channel_id=1, source_target_pairs={{0,8},{8,16},{16,24},{1,9},{9,17},{17,25},{2,10},{10,18},{18,26},{... | collective-permute-start | bytes 1622024 | tf_op jit(solution)/shard_map/ppermute | solution.py:474
  137.1 0.0 collective-permute-done.21
  137.1 1.9 %collective-permute-start.12 = (bf16[1,66,256]{2,1,0:T(8,128)(2,1)S(1)}, bf16[1,66,256]{2,1,0:T(8,128)(2,1)S(1)}, u32[]{:S(2)}, u32[]{:S(2)}) collective-permute-start(bf16[1,66,256]{2,1,0:T(8,128)(2,1)S(1)} %slice.148), channel_id=1, source_target_pairs={{8,0},{16,8},{24,16},{9,1},{17,9},{25,17},{10,2},{18,10},{26,18},{... | collective-permute-start | bytes 101384 | tf_op jit(solution)/shard_map/ppermute | solution.py:474
  139.1 0.6 squeeze_reshape.3
  139.8 0.6 squeeze.14
  140.4 0.6 squeeze.15
  141.0 2.3 %collective-permute-done.11 = bf16[16,66,256]{2,0,1:T(8,128)(2,1)S(1)} collective-permute-done((bf16[16,66,256]{2,0,1:T(8,128)(2,1)S(1)}, bf16[16,66,256]{2,0,1:T(8,128)(2,1)S(1)}, u32[]{:S(2)}, u32[]{:S(2)}) %collective-permute-start.11) | collective-permute-done | bytes 540704 | tf_op jit(solution)/shard_map/ppermute | solution.py:474
  143.4 0.2 copy.27
  143.5 0.0 collective-permute-done.12
  143.5 0.2 add_convert_fusion
  143.7 1.6 %fusion.6 = (bf16[18,64,256]{2,1,0:T(8,128)(2,1)}, bf16[18,64,256]{2,1,0:T(8,128)(2,1)}, bf16[18,64,256]{2,1,0:T(8,128)(2,1)}) fusion(bf16[18,66,256]{2,1,0:T(8,128)(2,1)S(1)} %add_convert_fusion), kind=kLoop, calls=%fused_computation.30 | loop fusion | bytes 3538944 | tf_op jit(solution)/shard_map/slice | solution.py:572
  145.3 4.0 %tile_input_grad.1 = bf16[1024,256]{1,0:T(8,128)(2,1)} custom-call(bf16[1152,256]{1,0:T(8,128)(2,1)} %bitcast.71, bf16[1152,256]{1,0:T(8,128)(2,1)} %bitcast.70, bf16[1152,256]{1,0:T(8,128)(2,1)} %bitcast.69, bf16[3,3,256,256]{3,2,1,0:T(8,128)(2,1)} %weight.1), custom_call_target="tpu_custom_call" | custom-call | flops 1 | bytes 1 | tf_op jit(solution)/shard_map/tile_input_grad/pallas_call | solution.py:462
  (33 shorter events, 0.4 us)
Async XLA Ops:
  20.5 63.1 %all-to-all-start = ((bf16[24,200,256]{2,1,0:T(8,128)(2,1)}), bf16[24,200,256]{2,1,0:T(8,128)(2,1)}, u32[]{:S(2)}, u32[]{:S(2)}) async-start(bf16[24,200,256]{2,1,0:T(8,128)(2,1)} %get-tuple-element.19), calls=%async_computation | async-start | bytes 4915200 | tf_op jit(solution)/shard_map/all_to_all | solution.py:541
  27.5 16.6 %copy-start.1 = (bf16[16,64,256]{2,1,0:T(8,128)(2,1)S(1)}, bf16[16,64,256]{2,1,0:T(8,128)(2,1)}, u32[]{:S(2)}) copy-start(bf16[16,64,256]{2,1,0:T(8,128)(2,1)} %param.23) | copy-start | bytes 1572868
  43.1 6.6 %collective-permute-start = (bf16[2,128,2304]{2,1,0:T(8,128)(2,1)}, bf16[2,128,2304]{2,1,0:T(8,128)(2,1)S(1)}, u32[]{:S(2)}, u32[]{:S(2)}) collective-permute-start(bf16[2,128,2304]{2,1,0:T(8,128)(2,1)} %get-tuple-element.17), channel_id=1, source_target_pairs={{0,8},{8,0},{16,24},{24,16},{1,9},{9,1},{17,25},{25,17},{2,10},{10... | collective-permute-start | bytes 3538952 | tf_op jit(solution)/shard_map/ppermute | solution.py:482
  44.1 10.9 %collective-permute-start.5 = (bf16[16,64,256]{2,1,0:T(8,128)(2,1)S(1)}, bf16[16,64,256]{2,1,0:T(8,128)(2,1)S(1)}, u32[]{:S(2)}, u32[]{:S(2)}) collective-permute-start(bf16[16,64,256]{2,1,0:T(8,128)(2,1)S(1)} %copy-done.1), channel_id=1, source_target_pairs={{8,0},{16,8},{24,16},{9,1},{17,9},{25,17},{10,2},{18,10},{26,18},{... | collective-permute-start | bytes 1572872 | tf_op jit(solution)/shard_map/ppermute | solution.py:474
  46.0 8.8 %collective-permute-start.4 = (bf16[1,64,256]{2,1,0:T(8,128)(2,1)S(1)}, bf16[1,64,256]{2,1,0:T(8,128)(2,1)S(1)}, u32[]{:S(2)}, u32[]{:S(2)}) collective-permute-start(bf16[1,64,256]{2,1,0:T(8,128)(2,1)S(1)} %slice.112), channel_id=1, source_target_pairs={{0,8},{8,16},{16,24},{1,9},{9,17},{17,25},{2,10},{10,18},{18,26},{... | collective-permute-start | bytes 98312 | tf_op jit(solution)/shard_map/ppermute | solution.py:474
  51.8 24.5 %collective-permute-start.1 = (bf16[2,32,2304]{2,1,0:T(8,128)(2,1)S(1)}, bf16[2,32,2304]{2,1,0:T(8,128)(2,1)S(1)}, u32[]{:S(2)}, u32[]{:S(2)}) collective-permute-start(bf16[2,32,2304]{2,1,0:T(8,128)(2,1)S(1)} %get-tuple-element.28), channel_id=1, source_target_pairs={{0,1},{1,0},{2,3},{3,2},{4,5},{5,4},{6,7},{7,6},{8,9},{9,8},{10,11... | collective-permute-start | bytes 884744 | tf_op jit(solution)/shard_map/ppermute | solution.py:480
  53.6 22.7 %collective-permute-start.2 = (bf16[2,32,2304]{2,1,0:T(8,128)(2,1)S(1)}, bf16[2,32,2304]{2,1,0:T(8,128)(2,1)S(1)}, u32[]{:S(2)}, u32[]{:S(2)}) collective-permute-start(bf16[2,32,2304]{2,1,0:T(8,128)(2,1)S(1)} %get-tuple-element.30), channel_id=1, source_target_pairs={{0,16},{8,24},{16,0},{24,8},{1,17},{9,25},{17,1},{25,9},{2,18},{10... | collective-permute-start | bytes 884744 | tf_op jit(solution)/shard_map/ppermute | solution.py:482
  53.6 22.7 %collective-permute-start.3 = (bf16[2,32,2304]{2,1,0:T(8,128)(2,1)S(1)}, bf16[2,32,2304]{2,1,0:T(8,128)(2,1)S(1)}, u32[]{:S(2)}, u32[]{:S(2)}) collective-permute-start(bf16[2,32,2304]{2,1,0:T(8,128)(2,1)S(1)} %get-tuple-element.29), channel_id=1, source_target_pairs={{0,17},{1,16},{2,19},{3,18},{4,21},{5,20},{6,23},{7,22},{8,25},{9,... | collective-permute-start | bytes 884744 | tf_op jit(solution)/shard_map/ppermute | solution.py:486
  55.0 21.4 %copy-start.2 = (bf16[33,64,256]{2,1,0:T(8,128)(2,1)}, bf16[33,64,256]{2,1,0:T(8,128)(2,1)S(1)}, u32[]{:S(2)}) copy-start(bf16[33,64,256]{2,1,0:T(8,128)(2,1)S(1)} %constant_dynamic-update-slice_fusion.own_ref) | copy-start | bytes 3244036
  55.1 27.0 %collective-permute-start.7 = (bf16[33,16,256]{2,1,0:T(8,128)(2,1)S(1)}, bf16[33,16,256]{2,1,0:T(8,128)(2,1)S(1)}, u32[]{:S(2)}, u32[]{:S(2)}) collective-permute-start(bf16[33,16,256]{2,1,0:T(8,128)(2,1)S(1)} %slice.143), channel_id=1, source_target_pairs={{1,0},{2,1},{3,2},{4,3},{5,4},{6,5},{7,6},{9,8},{10,9},{11,10},{12... | collective-permute-start | bytes 811016 | tf_op jit(solution)/shard_map/ppermute | solution.py:474
  56.4 20.7 %collective-permute-start.6 = (bf16[33,1,256]{2,1,0:T(2,128)(2,1)S(1)}, bf16[33,1,256]{2,1,0:T(2,128)(2,1)S(1)}, u32[]{:S(2)}, u32[]{:S(2)}) collective-permute-start(bf16[33,1,256]{2,1,0:T(2,128)(2,1)S(1)} %slice.142), channel_id=1, source_target_pairs={{0,1},{1,2},{2,3},{3,4},{4,5},{5,6},{6,7},{8,9},{9,10},{10,11},{11... | collective-permute-start | bytes 50696 | tf_op jit(solution)/shard_map/ppermute | solution.py:474
  77.1 6.4 %copy-start.4 = (bf16[33,1,256]{2,1,0:T(2,128)(2,1)}, bf16[33,1,256]{2,1,0:T(2,128)(2,1)S(1)}, u32[]{:S(2)}) copy-start(bf16[33,1,256]{2,1,0:T(2,128)(2,1)S(1)} %collective-permute-done.6.left_ref) | copy-start | bytes 50692
  82.1 1.4 copy-start.3
  95.3 5.2 %collective-permute-start.8 = (bf16[1,128,2304]{2,1,0:T(8,128)(2,1)}, bf16[1,128,2304]{2,1,0:T(8,128)(2,1)S(1)}, u32[]{:S(2)}, u32[]{:S(2)}) collective-permute-start(bf16[1,128,2304]{2,1,0:T(8,128)(2,1)} %get-tuple-element.22), channel_id=1, source_target_pairs={{0,8},{8,0},{16,24},{24,16},{1,9},{9,1},{17,25},{25,17},{2,10},{10... | collective-permute-start | bytes 1769480 | tf_op jit(solution)/shard_map/ppermute | solution.py:482
  101.8 2.8 %copy-start = (f32[32,80,256]{2,1,0:T(8,128)S(1)}, f32[32,80,256]{2,1,0:T(8,128)}, u32[]{:S(2)}) copy-start(f32[32,80,256]{2,1,0:T(8,128)} %get-tuple-element.23) | copy-start | bytes 7864324
  101.9 6.5 %collective-permute-start.16 = (bf16[1,32,2304]{2,1,0:T(8,128)(2,1)S(1)}, bf16[1,32,2304]{2,1,0:T(8,128)(2,1)S(1)}, u32[]{:S(2)}, u32[]{:S(2)}) collective-permute-start(bf16[1,32,2304]{2,1,0:T(8,128)(2,1)S(1)} %get-tuple-element.34), channel_id=1, source_target_pairs={{0,1},{1,0},{2,3},{3,2},{4,5},{5,4},{6,7},{7,6},{8,9},{9,8},{10,11... | collective-permute-start | bytes 442376 | tf_op jit(solution)/shard_map/ppermute | solution.py:480
  102.0 6.4 %collective-permute-start.17 = (bf16[1,32,2304]{2,1,0:T(8,128)(2,1)S(1)}, bf16[1,32,2304]{2,1,0:T(8,128)(2,1)S(1)}, u32[]{:S(2)}, u32[]{:S(2)}) collective-permute-start(bf16[1,32,2304]{2,1,0:T(8,128)(2,1)S(1)} %get-tuple-element.36), channel_id=1, source_target_pairs={{0,16},{8,24},{16,0},{24,8},{1,17},{9,25},{17,1},{25,9},{2,18},{10... | collective-permute-start | bytes 442376 | tf_op jit(solution)/shard_map/ppermute | solution.py:482
  102.1 9.0 %collective-permute-start.18 = (bf16[1,32,2304]{2,1,0:T(8,128)(2,1)S(1)}, bf16[1,32,2304]{2,1,0:T(8,128)(2,1)S(1)}, u32[]{:S(2)}, u32[]{:S(2)}) collective-permute-start(bf16[1,32,2304]{2,1,0:T(8,128)(2,1)S(1)} %get-tuple-element.35), channel_id=1, source_target_pairs={{0,17},{1,16},{2,19},{3,18},{4,21},{5,20},{6,23},{7,22},{8,25},{9,... | collective-permute-start | bytes 442376 | tf_op jit(solution)/shard_map/ppermute | solution.py:486
  105.1 14.7 %collective-permute-start.9 = (bf16[32,16,256]{2,1,0:T(8,128)(2,1)S(1)}, bf16[32,16,256]{2,1,0:T(8,128)(2,1)S(1)}, u32[]{:S(2)}, u32[]{:S(2)}) collective-permute-start(bf16[32,16,256]{2,1,0:T(8,128)(2,1)S(1)} %slice.144), channel_id=1, source_target_pairs={{0,1},{1,2},{2,3},{3,4},{4,5},{5,6},{6,7},{8,9},{9,10},{10,11},{11... | collective-permute-start | bytes 786440 | tf_op jit(solution)/shard_map/ppermute | solution.py:474
  107.1 12.7 %collective-permute-start.10 = (bf16[32,1,256]{2,1,0:T(2,128)(2,1)S(1)}, bf16[32,1,256]{2,1,0:T(2,128)(2,1)S(1)}, u32[]{:S(2)}, u32[]{:S(2)}) collective-permute-start(bf16[32,1,256]{2,1,0:T(2,128)(2,1)S(1)} %slice.145), channel_id=1, source_target_pairs={{1,0},{2,1},{3,2},{4,3},{5,4},{6,5},{7,6},{9,8},{10,9},{11,10},{12... | collective-permute-start | bytes 49160 | tf_op jit(solution)/shard_map/ppermute | solution.py:474
  120.1 11.0 %collective-permute-start.19 = (bf16[1,8,2304]{2,1,0:T(8,128)(2,1)S(1)}, bf16[1,8,2304]{2,1,0:T(8,128)(2,1)S(1)}, u32[]{:S(2)}, u32[]{:S(2)}) collective-permute-start(bf16[1,8,2304]{2,1,0:T(8,128)(2,1)S(1)} %get-tuple-element.40), channel_id=1, source_target_pairs={{0,2},{1,3},{2,0},{3,1},{4,6},{5,7},{6,4},{7,5},{8,10},{9,11},{10,... | collective-permute-start | bytes 110600 | tf_op jit(solution)/shard_map/ppermute | solution.py:480
  127.2 6.2 %collective-permute-start.20 = (bf16[1,8,2304]{2,1,0:T(8,128)(2,1)S(1)}, bf16[1,8,2304]{2,1,0:T(8,128)(2,1)S(1)}, u32[]{:S(2)}, u32[]{:S(2)}) collective-permute-start(bf16[1,8,2304]{2,1,0:T(8,128)(2,1)S(1)} %get-tuple-element.42), channel_id=1, source_target_pairs={{0,4},{1,5},{2,6},{3,7},{4,0},{5,1},{6,2},{7,3},{8,12},{9,13},{10,... | collective-permute-start | bytes 110600 | tf_op jit(solution)/shard_map/ppermute | solution.py:480
  127.2 9.9 %collective-permute-start.21 = (bf16[1,8,2304]{2,1,0:T(8,128)(2,1)S(1)}, bf16[1,8,2304]{2,1,0:T(8,128)(2,1)S(1)}, u32[]{:S(2)}, u32[]{:S(2)}) collective-permute-start(bf16[1,8,2304]{2,1,0:T(8,128)(2,1)S(1)} %get-tuple-element.41), channel_id=1, source_target_pairs={{0,6},{1,7},{2,4},{3,5},{4,2},{5,3},{6,0},{7,1},{8,14},{9,15},{10,... | collective-permute-start | bytes 110600 | tf_op jit(solution)/shard_map/ppermute | solution.py:480
  129.6 10.1 %collective-permute-start.13 = (bf16[2,8,2304]{2,1,0:T(8,128)(2,1)S(1)}, bf16[2,8,2304]{2,1,0:T(8,128)(2,1)S(1)}, u32[]{:S(2)}, u32[]{:S(2)}) collective-permute-start(bf16[2,8,2304]{2,1,0:T(8,128)(2,1)S(1)} %get-tuple-element.37), channel_id=1, source_target_pairs={{0,2},{1,3},{2,0},{3,1},{4,6},{5,7},{6,4},{7,5},{8,10},{9,11},{10,... | collective-permute-start | bytes 221192 | tf_op jit(solution)/shard_map/ppermute | solution.py:480
  130.2 9.5 %collective-permute-start.14 = (bf16[2,8,2304]{2,1,0:T(8,128)(2,1)S(1)}, bf16[2,8,2304]{2,1,0:T(8,128)(2,1)S(1)}, u32[]{:S(2)}, u32[]{:S(2)}) collective-permute-start(bf16[2,8,2304]{2,1,0:T(8,128)(2,1)S(1)} %get-tuple-element.39), channel_id=1, source_target_pairs={{0,4},{1,5},{2,6},{3,7},{4,0},{5,1},{6,2},{7,3},{8,12},{9,13},{10,... | collective-permute-start | bytes 221192 | tf_op jit(solution)/shard_map/ppermute | solution.py:480
  131.2 8.5 %collective-permute-start.15 = (bf16[2,8,2304]{2,1,0:T(8,128)(2,1)S(1)}, bf16[2,8,2304]{2,1,0:T(8,128)(2,1)S(1)}, u32[]{:S(2)}, u32[]{:S(2)}) collective-permute-start(bf16[2,8,2304]{2,1,0:T(8,128)(2,1)S(1)} %get-tuple-element.38), channel_id=1, source_target_pairs={{0,6},{1,7},{2,4},{3,5},{4,2},{5,3},{6,0},{7,1},{8,14},{9,15},{10,... | collective-permute-start | bytes 221192 | tf_op jit(solution)/shard_map/ppermute | solution.py:480
  133.4 10.0 %collective-permute-start.11 = (bf16[16,66,256]{2,0,1:T(8,128)(2,1)S(1)}, bf16[16,66,256]{2,0,1:T(8,128)(2,1)S(1)}, u32[]{:S(2)}, u32[]{:S(2)}) collective-permute-start(bf16[16,66,256]{2,0,1:T(8,128)(2,1)S(1)} %copy.26), channel_id=1, source_target_pairs={{0,8},{8,16},{16,24},{1,9},{9,17},{17,25},{2,10},{10,18},{18,26},{... | collective-permute-start | bytes 1622024 | tf_op jit(solution)/shard_map/ppermute | solution.py:474
  137.1 6.4 %collective-permute-start.12 = (bf16[1,66,256]{2,1,0:T(8,128)(2,1)S(1)}, bf16[1,66,256]{2,1,0:T(8,128)(2,1)S(1)}, u32[]{:S(2)}, u32[]{:S(2)}) collective-permute-start(bf16[1,66,256]{2,1,0:T(8,128)(2,1)S(1)} %slice.148), channel_id=1, source_target_pairs={{8,0},{16,8},{24,16},{9,1},{17,9},{25,17},{10,2},{18,10},{26,18},{... | collective-permute-start | bytes 101384 | tf_op jit(solution)/shard_map/ppermute | solution.py:474

commit v4 on v3

--- a/solution.py
+++ b/solution.py
@@ -106,8 +106,7 @@
     for which in range(2):
         for r in range(together):
             ones[which, pl.ds((r + 1) * block - pitch, pitch), :] = jnp.zeros((pitch, wide.shape[1]), BF)
-    for j, (src, dst) in enumerate(((w_two_hbm, w_two), (w_one_hbm, w_one))):
-        pltpu.make_async_copy(src, dst, w_sems.at[j]).wait()
+    pltpu.make_async_copy(w_two_hbm, w_two, w_sems.at[0]).wait()
 
     def conv(source, weight):
         for e in range(3):
@@ -152,6 +151,10 @@
             @pl.when(step * together + r < count)
             def _(r=r):
                 store(step, which, r).start()
+
+        @pl.when(step == 0)
+        def _():
+            pltpu.make_async_copy(w_one_hbm, w_one, w_sems.at[1]).wait()
 
         region_grad = conv(again, w_one)
         for r in range(together):
@@ -313,7 +316,9 @@
 
 def lay_out(geometry, own_ref, left_ref, right_ref, out_ref, wide):
     rows, pitch, tile_cols = geometry
-    wide[...] = jnp.zeros_like(wide)
+    end = 8 + rows * pitch
+    wide[pl.ds(0, 8), :] = jnp.zeros((8, wide.shape[1]), F32)
+    wide[pl.ds(end, wide.shape[0] - end), :] = jnp.zeros((wide.shape[0] - end, wide.shape[1]), F32)
     for y in range(rows):
         at = 8 + y * pitch
         wide[pl.ds(at, tile_cols), :] = own_ref[y].astype(F32)

time: 150 us -> 148 us (0.987)
  waiting for transfers between devices: 38.2 us -> 35 us
    ppermute x8, waiting for transfers between devices: 16.6 us -> 13.5 us  [neighbours(): lax.ppermute(array, axis, [(i, i + by) for i in range(count) if 0 <= i +...]
  transfers between devices with their start and end apart: 23 -> 23, of which waited for: 8 -> 9; matrix products, arithmetic and copies ran while one was open for 4% -> 4% of each run, Pallas kernels for 10% -> 11%
where the time goes in v4:
time: 148 us; the launch traced here: 146 us
  Pallas kernels  51.4 us (35%)
  starting transfers between devices  49.5 us (33%)
  waiting for transfers between devices  35 us (24%)
  other arithmetic  5.03 us (3%)
  local copies, waits for them, and re-layouts  4.43 us (3%)
    pallas_call x1, Pallas kernels, region_heads(): pl.pallas_call(functools.partial(head_body, (pool, pitch, regions, capaci...  20.1 us
    ppermute x8, starting transfers between devices, neighbours(): lax.ppermute(array, axis, [(i, i + by) for i in range(count) if 0 <= i +...  20.1 us
    ppermute x8, waiting for transfers between devices, partner(): return lax.ppermute(array, 'tx', [(i, i ^ bits_tx) for i in range(across)])  15.6 us
    pallas_call x1, Pallas kernels, head_weight_grads(): pl.pallas_call(functools.partial(head_weight_body, (regions, pool, pitch,...  15.6 us
    ppermute x8, starting transfers between devices, partner(): return lax.ppermute(array, 'tx', [(i, i ^ bits_tx) for i in range(across)])  14.8 us
    ppermute x8, waiting for transfers between devices, neighbours(): lax.ppermute(array, axis, [(i, i + by) for i in range(count) if 0 <= i +...  13.5 us
    pallas_call x1, Pallas kernels, tile_gradient(): pl.pallas_call(functools.partial(tile_body, geometry), in_specs=[smem] +...  11.7 us
    all_to_all x1, starting transfers between devices, local(): received = lax.all_to_all(sent, 'tx', 0, 0, tiled=True)  6.4 us
  transfers between devices with their start and end apart: 23, of which 9 were waited for; matrix products, arithmetic and copies ran while one was open for 4% of the time, Pallas kernels for 11%

profile of v4, /device:TPU:1, one launch (start us, length us, event | category | flops | bytes accessed | tf_op | source)
XLA Modules:
  0.0 146.4 jit_solution(1663689538937130531)
XLA Ops:
  0.6 20.1 %region_heads.1 = (bf16[2880,256]{1,0:T(8,128)(2,1)}, bf16[24,200,256]{2,1,0:T(8,128)(2,1)}) custom-call(s32[12]{0:T(128)} %bitcast.73, s32[12]{0:T(128)} %off_row.1, s32[12]{0:T(128)} %off_col.1, bf16[12,16,14]{2,1,0:T(8,128)(2,1)} %row_ref.1, bf16[12,16,14]{2,1,0:T(8,128)(2,1)} %col_ref.1, bf16[12,14,14,256]{3,2,1,0:T(8,128)(2,1)} %two_ref.1, ...), custom_call_target="tpu_custom_call" | custom-call | flops 13589544960 | bytes 1 | tf_op jit(solution)/shard_map/region_heads/pallas_call | solution.py:193
  20.7 6.4 %all-to-all-start = ((bf16[24,200,256]{2,1,0:T(8,128)(2,1)}), bf16[24,200,256]{2,1,0:T(8,128)(2,1)}, u32[]{:S(2)}, u32[]{:S(2)}) async-start(bf16[24,200,256]{2,1,0:T(8,128)(2,1)} %get-tuple-element.19), calls=%async_computation | async-start | bytes 4915200 | tf_op jit(solution)/shard_map/all_to_all | solution.py:546
  27.1 0.6 pad_add_fusion.where
  27.7 15.6 %head_weight_grads.1 = (f32[2,128,2304]{2,1,0:T(8,128)}, bf16[2,128,2304]{2,1,0:T(8,128)(2,1)}) custom-call(s32[2]{0:T(128)} %pad_add_fusion.where, bf16[12,14,14,256]{3,2,1,0:T(8,128)(2,1)} %two_ref.1, bf16[12,14,14,256]{3,2,1,0:T(8,128)(2,1)} %pre_ref.1, bf16[2880,256]{1,0:T(8,128)(2,1)} %get-tuple-element.15.one_hbm, bf16[12,14,14,256]{3,2,1,0:T(8,128)(2,1)} %feat_hbm.1), custom_call_target="tpu_custom_call" | custom-call | flops 1 | bytes 1 | tf_op jit(solution)/shard_map/head_weight_grads/pallas_call | solution.py:292
  43.3 1.0 collective-permute-start
  44.3 1.9 %collective-permute-start.5 = (bf16[16,64,256]{2,1,0:T(8,128)(2,1)S(1)}, bf16[16,64,256]{2,1,0:T(8,128)(2,1)S(1)}, u32[]{:S(2)}, u32[]{:S(2)}) collective-permute-start(bf16[16,64,256]{2,1,0:T(8,128)(2,1)S(1)} %copy-done.1), channel_id=1, source_target_pairs={{8,0},{16,8},{24,16},{9,1},{17,9},{25,17},{10,2},{18,10},{26,18},{... | collective-permute-start | bytes 1572872 | tf_op jit(solution)/shard_map/ppermute | solution.py:479
  46.3 3.6 %collective-permute-start.4 = (bf16[1,64,256]{2,1,0:T(8,128)(2,1)S(1)}, bf16[1,64,256]{2,1,0:T(8,128)(2,1)S(1)}, u32[]{:S(2)}, u32[]{:S(2)}) collective-permute-start(bf16[1,64,256]{2,1,0:T(8,128)(2,1)S(1)} %slice.112), channel_id=1, source_target_pairs={{0,8},{8,16},{16,24},{1,9},{9,17},{17,25},{2,10},{10,18},{18,26},{... | collective-permute-start | bytes 98312 | tf_op jit(solution)/shard_map/ppermute | solution.py:479
  49.9 1.9 %convert_add_fusion.1 = f32[2,128,2304]{2,1,0:T(8,128)S(1)} fusion(f32[2,128,2304]{2,1,0:T(8,128)} %get-tuple-element.16, bf16[2,128,2304]{2,1,0:T(8,128)(2,1)S(1)} %collective-permute-done), kind=kLoop, calls=%fused_computation.1 | loop fusion | flops 1179648 | bytes 5898240 | tf_op jit(solution)/shard_map/add | solution.py:497
  51.9 0.1 convert.36
  52.0 0.1 slice_bitcast_fusion.4
  52.0 1.8 %collective-permute-start.1 = (bf16[2,32,2304]{2,1,0:T(8,128)(2,1)S(1)}, bf16[2,32,2304]{2,1,0:T(8,128)(2,1)S(1)}, u32[]{:S(2)}, u32[]{:S(2)}) collective-permute-start(bf16[2,32,2304]{2,1,0:T(8,128)(2,1)S(1)} %get-tuple-element.28), channel_id=1, source_target_pairs={{0,1},{1,0},{2,3},{3,2},{4,5},{5,4},{6,7},{7,6},{8,9},{9,8},{10,11... | collective-permute-start | bytes 884744 | tf_op jit(solution)/shard_map/ppermute | solution.py:485
  53.9 0.0 collective-permute-start.2
  53.9 1.3 collective-permute-start.3
  55.1 0.0 collective-permute-done.4
  55.2 0.1 collective-permute-done.5
  55.3 1.3 collective-permute-start.7
  56.6 4.3 %collective-permute-start.6 = (bf16[33,1,256]{2,1,0:T(2,128)(2,1)S(1)}, bf16[33,1,256]{2,1,0:T(2,128)(2,1)S(1)}, u32[]{:S(2)}, u32[]{:S(2)}) collective-permute-start(bf16[33,1,256]{2,1,0:T(2,128)(2,1)S(1)} %slice.142), channel_id=1, source_target_pairs={{0,1},{1,2},{2,3},{3,4},{4,5},{5,6},{6,7},{8,9},{9,10},{10,11},{11... | collective-permute-start | bytes 50696 | tf_op jit(solution)/shard_map/ppermute | solution.py:479
  61.0 15.6 %collective-permute-done.1 = bf16[2,32,2304]{2,1,0:T(8,128)(2,1)S(1)} collective-permute-done((bf16[2,32,2304]{2,1,0:T(8,128)(2,1)S(1)}, bf16[2,32,2304]{2,1,0:T(8,128)(2,1)S(1)}, u32[]{:S(2)}, u32[]{:S(2)}) %collective-permute-start.1) | collective-permute-done | bytes 294944 | tf_op jit(solution)/shard_map/ppermute | solution.py:485
  76.6 0.1 fusion.1
  76.7 0.6 collective-permute-done.6.left_ref
  77.3 5.0 %collective-permute-done.7.right_ref = bf16[33,16,256]{2,1,0:T(8,128)(2,1)S(1)} collective-permute-done((bf16[33,16,256]{2,1,0:T(8,128)(2,1)S(1)}, bf16[33,16,256]{2,1,0:T(8,128)(2,1)S(1)}, u32[]{:S(2)}, u32[]{:S(2)}) %collective-permute-start.7) | collective-permute-done | bytes 270368 | tf_op jit(solution)/shard_map/ppermute | solution.py:479
  82.4 1.4 all-to-all-done.received
  83.8 11.7 %tile_gradient.1 = (f32[32,80,256]{2,1,0:T(8,128)}, f32[1,128,2304]{2,1,0:T(8,128)}, bf16[1,128,2304]{2,1,0:T(8,128)(2,1)}) custom-call(s32[2]{0:T(128)} %pad_add_fusion.where, bf16[16,64,256]{2,1,0:T(8,128)(2,1)} %start_ref, bf16[24,200,256]{2,1,0:T(8,128)(2,1)} %all-to-all-done.received, bf16[33,64,256]{2,1,0:T(8,128)(2,1)} %copy-done.2, ...), custom_call_target="tpu_custom_call" | custom-call | flops 6039797760 | bytes 1 | tf_op jit(solution)/shard_map/tile_gradient/pallas_call | solution.py:417
  95.5 3.3 %collective-permute-start.8 = (bf16[1,128,2304]{2,1,0:T(8,128)(2,1)}, bf16[1,128,2304]{2,1,0:T(8,128)(2,1)S(1)}, u32[]{:S(2)}, u32[]{:S(2)}) collective-permute-start(bf16[1,128,2304]{2,1,0:T(8,128)(2,1)} %get-tuple-element.22), channel_id=1, source_target_pairs={{0,8},{8,0},{16,24},{24,16},{1,9},{9,1},{17,25},{25,17},{2,10},{10... | collective-permute-start | bytes 1769480 | tf_op jit(solution)/shard_map/ppermute | solution.py:487
  98.8 1.8 %collective-permute-done.8 = bf16[1,128,2304]{2,1,0:T(8,128)(2,1)S(1)} collective-permute-done((bf16[1,128,2304]{2,1,0:T(8,128)(2,1)}, bf16[1,128,2304]{2,1,0:T(8,128)(2,1)S(1)}, u32[]{:S(2)}, u32[]{:S(2)}) %collective-permute-start.8) | collective-permute-done | bytes 589856 | tf_op jit(solution)/shard_map/ppermute | solution.py:487
  100.7 1.4 convert_add_fusion.2
  102.0 0.1 convert.40
  102.1 0.1 collective-permute-start.16
  102.2 0.1 collective-permute-start.17
  102.3 2.6 %collective-permute-start.18 = (bf16[1,32,2304]{2,1,0:T(8,128)(2,1)S(1)}, bf16[1,32,2304]{2,1,0:T(8,128)(2,1)S(1)}, u32[]{:S(2)}, u32[]{:S(2)}) collective-permute-start(bf16[1,32,2304]{2,1,0:T(8,128)(2,1)S(1)} %get-tuple-element.35), channel_id=1, source_target_pairs={{0,17},{1,16},{2,19},{3,18},{4,21},{5,20},{6,23},{7,22},{8,25},{9,... | collective-permute-start | bytes 442376 | tf_op jit(solution)/shard_map/ppermute | solution.py:491
  104.9 0.2 slice.115
  105.0 0.1 convert.37
  105.2 0.1 slice.144
  105.3 2.0 %collective-permute-start.9 = (bf16[32,16,256]{2,1,0:T(8,128)(2,1)S(1)}, bf16[32,16,256]{2,1,0:T(8,128)(2,1)S(1)}, u32[]{:S(2)}, u32[]{:S(2)}) collective-permute-start(bf16[32,16,256]{2,1,0:T(8,128)(2,1)S(1)} %slice.144), channel_id=1, source_target_pairs={{0,1},{1,2},{2,3},{3,4},{4,5},{5,6},{6,7},{8,9},{9,10},{10,11},{11... | collective-permute-start | bytes 786440 | tf_op jit(solution)/shard_map/ppermute | solution.py:479
  107.3 1.3 collective-permute-start.10
  108.6 0.0 collective-permute-done.16
  108.6 2.7 %collective-permute-done.18 = bf16[1,32,2304]{2,1,0:T(8,128)(2,1)S(1)} collective-permute-done((bf16[1,32,2304]{2,1,0:T(8,128)(2,1)S(1)}, bf16[1,32,2304]{2,1,0:T(8,128)(2,1)S(1)}, u32[]{:S(2)}, u32[]{:S(2)}) %collective-permute-start.18) | collective-permute-done | bytes 147488 | tf_op jit(solution)/shard_map/ppermute | solution.py:491
  111.3 0.1 fusion.3
  111.4 5.4 %collective-permute-done.10 = bf16[32,1,256]{2,1,0:T(2,128)(2,1)S(1)} collective-permute-done((bf16[32,1,256]{2,1,0:T(2,128)(2,1)S(1)}, bf16[32,1,256]{2,1,0:T(2,128)(2,1)S(1)}, u32[]{:S(2)}, u32[]{:S(2)}) %collective-permute-start.10) | collective-permute-done | bytes 16416 | tf_op jit(solution)/shard_map/ppermute | solution.py:479
  116.8 0.3 fusion.5
  117.2 7.1 %collective-permute-start.19 = (bf16[1,8,2304]{2,1,0:T(8,128)(2,1)S(1)}, bf16[1,8,2304]{2,1,0:T(8,128)(2,1)S(1)}, u32[]{:S(2)}, u32[]{:S(2)}) collective-permute-start(bf16[1,8,2304]{2,1,0:T(8,128)(2,1)S(1)} %get-tuple-element.40), channel_id=1, source_target_pairs={{0,2},{1,3},{2,0},{3,1},{4,6},{5,7},{6,4},{7,5},{8,10},{9,11},{10,... | collective-permute-start | bytes 110600 | tf_op jit(solution)/shard_map/ppermute | solution.py:485
  124.3 0.0 collective-permute-start.20
  124.3 2.2 %collective-permute-start.21 = (bf16[1,8,2304]{2,1,0:T(8,128)(2,1)S(1)}, bf16[1,8,2304]{2,1,0:T(8,128)(2,1)S(1)}, u32[]{:S(2)}, u32[]{:S(2)}) collective-permute-start(bf16[1,8,2304]{2,1,0:T(8,128)(2,1)S(1)} %get-tuple-element.41), channel_id=1, source_target_pairs={{0,6},{1,7},{2,4},{3,5},{4,2},{5,3},{6,0},{7,1},{8,14},{9,15},{10,... | collective-permute-start | bytes 110600 | tf_op jit(solution)/shard_map/ppermute | solution.py:485
  126.5 0.1 slice.146
  126.7 0.6 collective-permute-start.13
  127.2 0.9 collective-permute-start.14
  128.1 0.1 copy.26
  128.2 0.0 collective-permute-done.19
  128.3 2.2 %collective-permute-start.15 = (bf16[2,8,2304]{2,1,0:T(8,128)(2,1)S(1)}, bf16[2,8,2304]{2,1,0:T(8,128)(2,1)S(1)}, u32[]{:S(2)}, u32[]{:S(2)}) collective-permute-start(bf16[2,8,2304]{2,1,0:T(8,128)(2,1)S(1)} %get-tuple-element.38), channel_id=1, source_target_pairs={{0,6},{1,7},{2,4},{3,5},{4,2},{5,3},{6,0},{7,1},{8,14},{9,15},{10,... | collective-permute-start | bytes 221192 | tf_op jit(solution)/shard_map/ppermute | solution.py:485
  130.5 0.0 collective-permute-done.20
  130.5 3.7 %collective-permute-start.11 = (bf16[16,66,256]{2,0,1:T(8,128)(2,1)S(1)}, bf16[16,66,256]{2,0,1:T(8,128)(2,1)S(1)}, u32[]{:S(2)}, u32[]{:S(2)}) collective-permute-start(bf16[16,66,256]{2,0,1:T(8,128)(2,1)S(1)} %copy.26), channel_id=1, source_target_pairs={{0,8},{8,16},{16,24},{1,9},{9,17},{17,25},{2,10},{10,18},{18,26},{... | collective-permute-start | bytes 1622024 | tf_op jit(solution)/shard_map/ppermute | solution.py:479
  134.2 0.0 collective-permute-done.21
  134.2 1.9 %collective-permute-start.12 = (bf16[1,66,256]{2,1,0:T(8,128)(2,1)S(1)}, bf16[1,66,256]{2,1,0:T(8,128)(2,1)S(1)}, u32[]{:S(2)}, u32[]{:S(2)}) collective-permute-start(bf16[1,66,256]{2,1,0:T(8,128)(2,1)S(1)} %slice.148), channel_id=1, source_target_pairs={{8,0},{16,8},{24,16},{9,1},{17,9},{25,17},{10,2},{18,10},{26,18},{... | collective-permute-start | bytes 101384 | tf_op jit(solution)/shard_map/ppermute | solution.py:479
  136.1 0.6 squeeze_reshape.3
  136.8 0.0 collective-permute-done.13
  136.8 0.0 collective-permute-done.14
  136.8 0.0 collective-permute-done.15
  136.8 0.6 squeeze.14
  137.5 0.6 squeeze.15
  138.1 2.3 %collective-permute-done.11 = bf16[16,66,256]{2,0,1:T(8,128)(2,1)S(1)} collective-permute-done((bf16[16,66,256]{2,0,1:T(8,128)(2,1)S(1)}, bf16[16,66,256]{2,0,1:T(8,128)(2,1)S(1)}, u32[]{:S(2)}, u32[]{:S(2)}) %collective-permute-start.11) | collective-permute-done | bytes 540704 | tf_op jit(solution)/shard_map/ppermute | solution.py:479
  140.4 0.2 copy.27
  140.6 0.2 add_convert_fusion
  140.8 1.6 %fusion.6 = (bf16[18,64,256]{2,1,0:T(8,128)(2,1)}, bf16[18,64,256]{2,1,0:T(8,128)(2,1)}, bf16[18,64,256]{2,1,0:T(8,128)(2,1)}) fusion(bf16[18,66,256]{2,1,0:T(8,128)(2,1)S(1)} %add_convert_fusion), kind=kLoop, calls=%fused_computation.30 | loop fusion | bytes 3538944 | tf_op jit(solution)/shard_map/slice | solution.py:577
  142.4 4.0 %tile_input_grad.1 = bf16[1024,256]{1,0:T(8,128)(2,1)} custom-call(bf16[1152,256]{1,0:T(8,128)(2,1)} %bitcast.71, bf16[1152,256]{1,0:T(8,128)(2,1)} %bitcast.70, bf16[1152,256]{1,0:T(8,128)(2,1)} %bitcast.69, bf16[3,3,256,256]{3,2,1,0:T(8,128)(2,1)} %weight.1), custom_call_target="tpu_custom_call" | custom-call | flops 1 | bytes 1 | tf_op jit(solution)/shard_map/tile_input_grad/pallas_call | solution.py:467
  (33 shorter events, 0.4 us)
Async XLA Ops:
  20.7 63.1 %all-to-all-start = ((bf16[24,200,256]{2,1,0:T(8,128)(2,1)}), bf16[24,200,256]{2,1,0:T(8,128)(2,1)}, u32[]{:S(2)}, u32[]{:S(2)}) async-start(bf16[24,200,256]{2,1,0:T(8,128)(2,1)} %get-tuple-element.19), calls=%async_computation | async-start | bytes 4915200 | tf_op jit(solution)/shard_map/all_to_all | solution.py:546
  27.7 16.6 %copy-start.1 = (bf16[16,64,256]{2,1,0:T(8,128)(2,1)S(1)}, bf16[16,64,256]{2,1,0:T(8,128)(2,1)}, u32[]{:S(2)}) copy-start(bf16[16,64,256]{2,1,0:T(8,128)(2,1)} %param.23) | copy-start | bytes 1572868
  43.3 6.6 %collective-permute-start = (bf16[2,128,2304]{2,1,0:T(8,128)(2,1)}, bf16[2,128,2304]{2,1,0:T(8,128)(2,1)S(1)}, u32[]{:S(2)}, u32[]{:S(2)}) collective-permute-start(bf16[2,128,2304]{2,1,0:T(8,128)(2,1)} %get-tuple-element.17), channel_id=1, source_target_pairs={{0,8},{8,0},{16,24},{24,16},{1,9},{9,1},{17,25},{25,17},{2,10},{10... | collective-permute-start | bytes 3538952 | tf_op jit(solution)/shard_map/ppermute | solution.py:487
  44.3 10.9 %collective-permute-start.5 = (bf16[16,64,256]{2,1,0:T(8,128)(2,1)S(1)}, bf16[16,64,256]{2,1,0:T(8,128)(2,1)S(1)}, u32[]{:S(2)}, u32[]{:S(2)}) collective-permute-start(bf16[16,64,256]{2,1,0:T(8,128)(2,1)S(1)} %copy-done.1), channel_id=1, source_target_pairs={{8,0},{16,8},{24,16},{9,1},{17,9},{25,17},{10,2},{18,10},{26,18},{... | collective-permute-start | bytes 1572872 | tf_op jit(solution)/shard_map/ppermute | solution.py:479
  46.3 8.8 %collective-permute-start.4 = (bf16[1,64,256]{2,1,0:T(8,128)(2,1)S(1)}, bf16[1,64,256]{2,1,0:T(8,128)(2,1)S(1)}, u32[]{:S(2)}, u32[]{:S(2)}) collective-permute-start(bf16[1,64,256]{2,1,0:T(8,128)(2,1)S(1)} %slice.112), channel_id=1, source_target_pairs={{0,8},{8,16},{16,24},{1,9},{9,17},{17,25},{2,10},{10,18},{18,26},{... | collective-permute-start | bytes 98312 | tf_op jit(solution)/shard_map/ppermute | solution.py:479
  52.0 24.5 %collective-permute-start.1 = (bf16[2,32,2304]{2,1,0:T(8,128)(2,1)S(1)}, bf16[2,32,2304]{2,1,0:T(8,128)(2,1)S(1)}, u32[]{:S(2)}, u32[]{:S(2)}) collective-permute-start(bf16[2,32,2304]{2,1,0:T(8,128)(2,1)S(1)} %get-tuple-element.28), channel_id=1, source_target_pairs={{0,1},{1,0},{2,3},{3,2},{4,5},{5,4},{6,7},{7,6},{8,9},{9,8},{10,11... | collective-permute-start | bytes 884744 | tf_op jit(solution)/shard_map/ppermute | solution.py:485
  53.9 22.7 %collective-permute-start.2 = (bf16[2,32,2304]{2,1,0:T(8,128)(2,1)S(1)}, bf16[2,32,2304]{2,1,0:T(8,128)(2,1)S(1)}, u32[]{:S(2)}, u32[]{:S(2)}) collective-permute-start(bf16[2,32,2304]{2,1,0:T(8,128)(2,1)S(1)} %get-tuple-element.30), channel_id=1, source_target_pairs={{0,16},{8,24},{16,0},{24,8},{1,17},{9,25},{17,1},{25,9},{2,18},{10... | collective-permute-start | bytes 884744 | tf_op jit(solution)/shard_map/ppermute | solution.py:487
  53.9 22.7 %collective-permute-start.3 = (bf16[2,32,2304]{2,1,0:T(8,128)(2,1)S(1)}, bf16[2,32,2304]{2,1,0:T(8,128)(2,1)S(1)}, u32[]{:S(2)}, u32[]{:S(2)}) collective-permute-start(bf16[2,32,2304]{2,1,0:T(8,128)(2,1)S(1)} %get-tuple-element.29), channel_id=1, source_target_pairs={{0,17},{1,16},{2,19},{3,18},{4,21},{5,20},{6,23},{7,22},{8,25},{9,... | collective-permute-start | bytes 884744 | tf_op jit(solution)/shard_map/ppermute | solution.py:491
  55.3 21.4 %copy-start.2 = (bf16[33,64,256]{2,1,0:T(8,128)(2,1)}, bf16[33,64,256]{2,1,0:T(8,128)(2,1)S(1)}, u32[]{:S(2)}) copy-start(bf16[33,64,256]{2,1,0:T(8,128)(2,1)S(1)} %constant_dynamic-update-slice_fusion.own_ref) | copy-start | bytes 3244036
  55.3 27.0 %collective-permute-start.7 = (bf16[33,16,256]{2,1,0:T(8,128)(2,1)S(1)}, bf16[33,16,256]{2,1,0:T(8,128)(2,1)S(1)}, u32[]{:S(2)}, u32[]{:S(2)}) collective-permute-start(bf16[33,16,256]{2,1,0:T(8,128)(2,1)S(1)} %slice.143), channel_id=1, source_target_pairs={{1,0},{2,1},{3,2},{4,3},{5,4},{6,5},{7,6},{9,8},{10,9},{11,10},{12... | collective-permute-start | bytes 811016 | tf_op jit(solution)/shard_map/ppermute | solution.py:479
  56.6 20.7 %collective-permute-start.6 = (bf16[33,1,256]{2,1,0:T(2,128)(2,1)S(1)}, bf16[33,1,256]{2,1,0:T(2,128)(2,1)S(1)}, u32[]{:S(2)}, u32[]{:S(2)}) collective-permute-start(bf16[33,1,256]{2,1,0:T(2,128)(2,1)S(1)} %slice.142), channel_id=1, source_target_pairs={{0,1},{1,2},{2,3},{3,4},{4,5},{5,6},{6,7},{8,9},{9,10},{10,11},{11... | collective-permute-start | bytes 50696 | tf_op jit(solution)/shard_map/ppermute | solution.py:479
  77.3 6.4 %copy-start.4 = (bf16[33,1,256]{2,1,0:T(2,128)(2,1)}, bf16[33,1,256]{2,1,0:T(2,128)(2,1)S(1)}, u32[]{:S(2)}) copy-start(bf16[33,1,256]{2,1,0:T(2,128)(2,1)S(1)} %collective-permute-done.6.left_ref) | copy-start | bytes 50692
  82.4 1.4 copy-start.3
  95.5 5.1 %collective-permute-start.8 = (bf16[1,128,2304]{2,1,0:T(8,128)(2,1)}, bf16[1,128,2304]{2,1,0:T(8,128)(2,1)S(1)}, u32[]{:S(2)}, u32[]{:S(2)}) collective-permute-start(bf16[1,128,2304]{2,1,0:T(8,128)(2,1)} %get-tuple-element.22), channel_id=1, source_target_pairs={{0,8},{8,0},{16,24},{24,16},{1,9},{9,1},{17,25},{25,17},{2,10},{10... | collective-permute-start | bytes 1769480 | tf_op jit(solution)/shard_map/ppermute | solution.py:487
  102.0 2.8 %copy-start = (f32[32,80,256]{2,1,0:T(8,128)S(1)}, f32[32,80,256]{2,1,0:T(8,128)}, u32[]{:S(2)}) copy-start(f32[32,80,256]{2,1,0:T(8,128)} %get-tuple-element.23) | copy-start | bytes 7864324
  102.1 6.5 %collective-permute-start.16 = (bf16[1,32,2304]{2,1,0:T(8,128)(2,1)S(1)}, bf16[1,32,2304]{2,1,0:T(8,128)(2,1)S(1)}, u32[]{:S(2)}, u32[]{:S(2)}) collective-permute-start(bf16[1,32,2304]{2,1,0:T(8,128)(2,1)S(1)} %get-tuple-element.34), channel_id=1, source_target_pairs={{0,1},{1,0},{2,3},{3,2},{4,5},{5,4},{6,7},{7,6},{8,9},{9,8},{10,11... | collective-permute-start | bytes 442376 | tf_op jit(solution)/shard_map/ppermute | solution.py:485
  102.2 6.4 %collective-permute-start.17 = (bf16[1,32,2304]{2,1,0:T(8,128)(2,1)S(1)}, bf16[1,32,2304]{2,1,0:T(8,128)(2,1)S(1)}, u32[]{:S(2)}, u32[]{:S(2)}) collective-permute-start(bf16[1,32,2304]{2,1,0:T(8,128)(2,1)S(1)} %get-tuple-element.36), channel_id=1, source_target_pairs={{0,16},{8,24},{16,0},{24,8},{1,17},{9,25},{17,1},{25,9},{2,18},{10... | collective-permute-start | bytes 442376 | tf_op jit(solution)/shard_map/ppermute | solution.py:487
  102.3 9.0 %collective-permute-start.18 = (bf16[1,32,2304]{2,1,0:T(8,128)(2,1)S(1)}, bf16[1,32,2304]{2,1,0:T(8,128)(2,1)S(1)}, u32[]{:S(2)}, u32[]{:S(2)}) collective-permute-start(bf16[1,32,2304]{2,1,0:T(8,128)(2,1)S(1)} %get-tuple-element.35), channel_id=1, source_target_pairs={{0,17},{1,16},{2,19},{3,18},{4,21},{5,20},{6,23},{7,22},{8,25},{9,... | collective-permute-start | bytes 442376 | tf_op jit(solution)/shard_map/ppermute | solution.py:491
  105.3 11.5 %collective-permute-start.9 = (bf16[32,16,256]{2,1,0:T(8,128)(2,1)S(1)}, bf16[32,16,256]{2,1,0:T(8,128)(2,1)S(1)}, u32[]{:S(2)}, u32[]{:S(2)}) collective-permute-start(bf16[32,16,256]{2,1,0:T(8,128)(2,1)S(1)} %slice.144), channel_id=1, source_target_pairs={{0,1},{1,2},{2,3},{3,4},{4,5},{5,6},{6,7},{8,9},{9,10},{10,11},{11... | collective-permute-start | bytes 786440 | tf_op jit(solution)/shard_map/ppermute | solution.py:479
  107.3 9.5 %collective-permute-start.10 = (bf16[32,1,256]{2,1,0:T(2,128)(2,1)S(1)}, bf16[32,1,256]{2,1,0:T(2,128)(2,1)S(1)}, u32[]{:S(2)}, u32[]{:S(2)}) collective-permute-start(bf16[32,1,256]{2,1,0:T(2,128)(2,1)S(1)} %slice.145), channel_id=1, source_target_pairs={{1,0},{2,1},{3,2},{4,3},{5,4},{6,5},{7,6},{9,8},{10,9},{11,10},{12... | collective-permute-start | bytes 49160 | tf_op jit(solution)/shard_map/ppermute | solution.py:479
  117.2 11.1 %collective-permute-start.19 = (bf16[1,8,2304]{2,1,0:T(8,128)(2,1)S(1)}, bf16[1,8,2304]{2,1,0:T(8,128)(2,1)S(1)}, u32[]{:S(2)}, u32[]{:S(2)}) collective-permute-start(bf16[1,8,2304]{2,1,0:T(8,128)(2,1)S(1)} %get-tuple-element.40), channel_id=1, source_target_pairs={{0,2},{1,3},{2,0},{3,1},{4,6},{5,7},{6,4},{7,5},{8,10},{9,11},{10,... | collective-permute-start | bytes 110600 | tf_op jit(solution)/shard_map/ppermute | solution.py:485
  124.3 6.2 %collective-permute-start.20 = (bf16[1,8,2304]{2,1,0:T(8,128)(2,1)S(1)}, bf16[1,8,2304]{2,1,0:T(8,128)(2,1)S(1)}, u32[]{:S(2)}, u32[]{:S(2)}) collective-permute-start(bf16[1,8,2304]{2,1,0:T(8,128)(2,1)S(1)} %get-tuple-element.42), channel_id=1, source_target_pairs={{0,4},{1,5},{2,6},{3,7},{4,0},{5,1},{6,2},{7,3},{8,12},{9,13},{10,... | collective-permute-start | bytes 110600 | tf_op jit(solution)/shard_map/ppermute | solution.py:485
  124.3 9.9 %collective-permute-start.21 = (bf16[1,8,2304]{2,1,0:T(8,128)(2,1)S(1)}, bf16[1,8,2304]{2,1,0:T(8,128)(2,1)S(1)}, u32[]{:S(2)}, u32[]{:S(2)}) collective-permute-start(bf16[1,8,2304]{2,1,0:T(8,128)(2,1)S(1)} %get-tuple-element.41), channel_id=1, source_target_pairs={{0,6},{1,7},{2,4},{3,5},{4,2},{5,3},{6,0},{7,1},{8,14},{9,15},{10,... | collective-permute-start | bytes 110600 | tf_op jit(solution)/shard_map/ppermute | solution.py:485
  126.7 10.1 %collective-permute-start.13 = (bf16[2,8,2304]{2,1,0:T(8,128)(2,1)S(1)}, bf16[2,8,2304]{2,1,0:T(8,128)(2,1)S(1)}, u32[]{:S(2)}, u32[]{:S(2)}) collective-permute-start(bf16[2,8,2304]{2,1,0:T(8,128)(2,1)S(1)} %get-tuple-element.37), channel_id=1, source_target_pairs={{0,2},{1,3},{2,0},{3,1},{4,6},{5,7},{6,4},{7,5},{8,10},{9,11},{10,... | collective-permute-start | bytes 221192 | tf_op jit(solution)/shard_map/ppermute | solution.py:485
  127.2 9.5 %collective-permute-start.14 = (bf16[2,8,2304]{2,1,0:T(8,128)(2,1)S(1)}, bf16[2,8,2304]{2,1,0:T(8,128)(2,1)S(1)}, u32[]{:S(2)}, u32[]{:S(2)}) collective-permute-start(bf16[2,8,2304]{2,1,0:T(8,128)(2,1)S(1)} %get-tuple-element.39), channel_id=1, source_target_pairs={{0,4},{1,5},{2,6},{3,7},{4,0},{5,1},{6,2},{7,3},{8,12},{9,13},{10,... | collective-permute-start | bytes 221192 | tf_op jit(solution)/shard_map/ppermute | solution.py:485
  128.3 8.5 %collective-permute-start.15 = (bf16[2,8,2304]{2,1,0:T(8,128)(2,1)S(1)}, bf16[2,8,2304]{2,1,0:T(8,128)(2,1)S(1)}, u32[]{:S(2)}, u32[]{:S(2)}) collective-permute-start(bf16[2,8,2304]{2,1,0:T(8,128)(2,1)S(1)} %get-tuple-element.38), channel_id=1, source_target_pairs={{0,6},{1,7},{2,4},{3,5},{4,2},{5,3},{6,0},{7,1},{8,14},{9,15},{10,... | collective-permute-start | bytes 221192 | tf_op jit(solution)/shard_map/ppermute | solution.py:485
  130.5 10.0 %collective-permute-start.11 = (bf16[16,66,256]{2,0,1:T(8,128)(2,1)S(1)}, bf16[16,66,256]{2,0,1:T(8,128)(2,1)S(1)}, u32[]{:S(2)}, u32[]{:S(2)}) collective-permute-start(bf16[16,66,256]{2,0,1:T(8,128)(2,1)S(1)} %copy.26), channel_id=1, source_target_pairs={{0,8},{8,16},{16,24},{1,9},{9,17},{17,25},{2,10},{10,18},{18,26},{... | collective-permute-start | bytes 1622024 | tf_op jit(solution)/shard_map/ppermute | solution.py:479
  134.2 6.4 %collective-permute-start.12 = (bf16[1,66,256]{2,1,0:T(8,128)(2,1)S(1)}, bf16[1,66,256]{2,1,0:T(8,128)(2,1)S(1)}, u32[]{:S(2)}, u32[]{:S(2)}) collective-permute-start(bf16[1,66,256]{2,1,0:T(8,128)(2,1)S(1)} %slice.148), channel_id=1, source_target_pairs={{8,0},{16,8},{24,16},{9,1},{17,9},{25,17},{10,2},{18,10},{26,18},{... | collective-permute-start | bytes 101384 | tf_op jit(solution)/shard_map/ppermute | solution.py:479
